TPU v7x, 32 devices: a whole 2x2x4 slice. The times are simulated.
32 devices in a mesh: dp: 16 (over z, x, core), tensor: 2 (over y).
Axes of the slice: x: 2, y: 2, z: 4, core: 2. Of those that a mesh axis runs over, the one named last changes fastest.
Arguments:
- inputs: bfloat16 [16384, 1024], P(('dp', 'tensor')), may hold values from -6 to 6
- grad_out: bfloat16 [16384, 1024], P(('dp', 'tensor')), may hold values from -6 to 6
- w_query: bfloat16 [1024, 2048], P('dp', 'tensor'), may hold values from -0.1875 to 0.1875
- key_weight: bfloat16 [1024, 1024], P('dp', 'tensor'), may hold values from -0.1875 to 0.1875
- value_weight: bfloat16 [1024, 1024], P('dp', 'tensor'), may hold values from -0.1875 to 0.1875
- w_output: bfloat16 [2048, 1024], P('tensor', 'dp'), may hold values from -1.5 to 1.5
- w_gate: bfloat16 [1024, 3072], P('dp', 'tensor'), may hold values from -0.1875 to 0.1875
- w_up: bfloat16 [1024, 3072], P('dp', 'tensor'), may hold values from -0.1875 to 0.1875
- w_down: bfloat16 [3072, 1024], P('tensor', 'dp'), may hold values from -0.109375 to 0.109375
- gain_attn: float32 [1024], replicated, may hold values from 0.5 to 1.5
- gain_mlp: float32 [1024], replicated, may hold values from 0.5 to 1.5
- gain_query: float32 [128], replicated, may hold values from 0.25 to 1.75
- gain_keys: float32 [128], replicated, may hold values from 0.25 to 1.75
Outputs:
- layer_out: bfloat16 [16384, 1024], P(('dp', 'tensor'))
- grad_inputs: bfloat16 [16384, 1024], P(('dp', 'tensor'))
- grad_w_query: float32 [1024, 2048], P('dp', 'tensor')
- grad_w_keys: float32 [1024, 1024], P('dp', 'tensor')
- grad_w_values: float32 [1024, 1024], P('dp', 'tensor')
- grad_w_output: float32 [2048, 1024], P('tensor', 'dp')
- grad_w_gate: float32 [1024, 3072], P('dp', 'tensor')
- grad_w_up: float32 [1024, 3072], P('dp', 'tensor')
- grad_w_down: float32 [3072, 1024], P('tensor', 'dp')
- grad_gain_attn: float32 [1024], replicated
- grad_gain_mlp: float32 [1024], replicated
- grad_gain_query: float32 [128], replicated
- grad_gain_keys: float32 [128], replicated
All inputs are finite; a program needn't handle non-finite values.
Results may differ from a plain program's by a relative error of at most 0.018.
Values may be sent and summed in bfloat16 or wider, within the bound.
No kernel may reach another device: no remote copies, remote signals or barrier semaphores. Data moves between devices by JAX's collectives and lax.ppermute only.
A program may use at most 192 MiB of HBM per device.

v0:
```python
import jax
import jax.numpy as jnp
from jax import lax
from jax.sharding import PartitionSpec as P

SEQUENCE_TOKENS = 512


EPSILON = 1e-06
THETA = 1000000.0


def row_norm(values, norm_gain):
    return (
        values * lax.rsqrt(jnp.mean(values * values, axis=-1, keepdims=True) + EPSILON) * norm_gain
    )


def rotary(values):
    length = values.shape[1]
    half_width = values.shape[-1] // 2
    places = jnp.arange(length, dtype=jnp.float32)
    inverse = THETA ** (-2.0 * jnp.arange(half_width, dtype=jnp.float32) / values.shape[-1])
    angles = places[:, None] * inverse[None, :]
    cosine = jnp.concatenate([jnp.cos(angles), jnp.cos(angles)], axis=-1)[:, None, :]
    sine = jnp.concatenate([jnp.sin(angles), jnp.sin(angles)], axis=-1)[:, None, :]
    turned = jnp.concatenate([-values[..., half_width:], values[..., :half_width]], axis=-1)
    return values * cosine + turned * sine


def head_prep(raw_heads, norm_gain):
    return rotary(row_norm(raw_heads, norm_gain))


def swiglu(gate_proj, up_proj):
    return jax.nn.silu(gate_proj) * up_proj


def matmul(left, right):
    return jnp.dot(left, right, preferred_element_type=jnp.float32)


def contract(left, right):
    return lax.dot_general(
        left, right, (((0,), (0,)), ((), ())), preferred_element_type=jnp.float32
    )


def against(left, right):
    return lax.dot_general(
        left, right, (((1,), (1,)), ((), ())), preferred_element_type=jnp.float32
    )


def masked_scores(query_rot, keys_rot, scaling, causal):
    raw_scores = (
        jnp.einsum("bqngd,btnd->bngqt", query_rot, keys_rot, preferred_element_type=jnp.float32)
        * scaling
    )
    return jnp.where(causal, raw_scores, -1e30)


def body(
    inputs,
    grad_out,
    w_query,
    key_weight,
    value_weight,
    w_output,
    w_gate,
    w_up,
    w_down,
    gain_attn,
    gain_mlp,
    gain_query,
    gain_keys,
):
    full_query, full_keys, full_values, full_output, full_gate, full_up, full_down = (
        lax.all_gather(w_query, "dp", axis=0, tiled=True),
        lax.all_gather(key_weight, "dp", axis=0, tiled=True),
        lax.all_gather(value_weight, "dp", axis=0, tiled=True),
        lax.all_gather(w_output, "dp", axis=1, tiled=True),
        lax.all_gather(w_gate, "dp", axis=0, tiled=True),
        lax.all_gather(w_up, "dp", axis=0, tiled=True),
        lax.all_gather(w_down, "dp", axis=1, tiled=True),
    )
    head_width = gain_query.shape[0]
    query_heads = full_query.shape[1] // head_width
    key_heads = full_keys.shape[1] // head_width
    grouped_heads = query_heads // key_heads
    scaling = head_width ** (-0.5)
    places = jnp.arange(SEQUENCE_TOKENS)
    causal = places[:, None] >= places[None, :]
    inputs_f = inputs.astype(jnp.float32)
    normed_f, attn_norm_pull = jax.vjp(row_norm, inputs_f, gain_attn)
    normalized_rows = lax.all_gather(normed_f.astype(jnp.bfloat16), "tensor", axis=0, tiled=True)
    group_rows = normalized_rows.shape[0]
    sequence_batch = group_rows // SEQUENCE_TOKENS
    query_proj = matmul(normalized_rows, full_query).reshape(
        sequence_batch, SEQUENCE_TOKENS, query_heads, head_width
    )
    keys_proj = matmul(normalized_rows, full_keys).reshape(
        sequence_batch, SEQUENCE_TOKENS, key_heads, head_width
    )
    values_low = (
        matmul(normalized_rows, full_values)
        .astype(jnp.bfloat16)
        .reshape(sequence_batch, SEQUENCE_TOKENS, key_heads, head_width)
    )
    query_rot_f, query_pull = jax.vjp(head_prep, query_proj, gain_query)
    keys_rot_f, keys_pull = jax.vjp(head_prep, keys_proj, gain_keys)
    query_rot = query_rot_f.astype(jnp.bfloat16).reshape(
        sequence_batch, SEQUENCE_TOKENS, key_heads, grouped_heads, head_width
    )
    keys_rot = keys_rot_f.astype(jnp.bfloat16)
    scores = masked_scores(query_rot, keys_rot, scaling, causal)
    largest = jnp.max(scores, axis=-1, keepdims=True)
    exponents = jnp.exp(scores - largest)
    sums_exp = jnp.sum(exponents, axis=-1, keepdims=True)
    probs_low = (exponents / sums_exp).astype(jnp.bfloat16)
    log_totals = largest + jnp.log(sums_exp)
    head_out = jnp.einsum(
        "bngqt,btnd->bqngd", probs_low, values_low, preferred_element_type=jnp.float32
    )
    head_out = head_out.astype(jnp.bfloat16).reshape(group_rows, query_heads * head_width)
    middle = inputs_f + lax.psum_scatter(
        matmul(head_out, full_output), "tensor", scatter_dimension=0, tiled=True
    )
    normed_mid, mlp_norm_pull = jax.vjp(row_norm, middle, gain_mlp)
    normed_mlp = lax.all_gather(normed_mid.astype(jnp.bfloat16), "tensor", axis=0, tiled=True)
    gate_proj = matmul(normed_mlp, full_gate)
    up_proj = matmul(normed_mlp, full_up)
    hidden_f, swiglu_pull = jax.vjp(swiglu, gate_proj, up_proj)
    hidden = hidden_f.astype(jnp.bfloat16)
    layer_out = (
        middle
        + lax.psum_scatter(
            matmul(hidden, full_down).astype(jnp.bfloat16),
            "tensor",
            scatter_dimension=0,
            tiled=True,
        ).astype(jnp.float32)
    ).astype(jnp.bfloat16)
    full_query, full_keys, full_values, full_output, full_gate, full_up, full_down = (
        lax.all_gather(w_query, "dp", axis=0, tiled=True),
        lax.all_gather(key_weight, "dp", axis=0, tiled=True),
        lax.all_gather(value_weight, "dp", axis=0, tiled=True),
        lax.all_gather(w_output, "dp", axis=1, tiled=True),
        lax.all_gather(w_gate, "dp", axis=0, tiled=True),
        lax.all_gather(w_up, "dp", axis=0, tiled=True),
        lax.all_gather(w_down, "dp", axis=1, tiled=True),
    )
    grad_rows = lax.all_gather(grad_out, "tensor", axis=0, tiled=True)
    grad_down = contract(hidden, grad_rows)
    grad_hidden = against(grad_rows, full_down)
    grad_gate_f, grad_up_f = swiglu_pull(grad_hidden)
    grad_gate_low = grad_gate_f.astype(jnp.bfloat16)
    grad_up_low = grad_up_f.astype(jnp.bfloat16)
    grad_gate_w = contract(normed_mlp, grad_gate_low)
    grad_up_w = contract(normed_mlp, grad_up_low)
    grad_normed_mid = lax.psum_scatter(
        against(grad_gate_low, full_gate) + against(grad_up_low, full_up),
        "tensor",
        scatter_dimension=0,
        tiled=True,
    )
    grad_middle_norm, grad_gain_mlp = mlp_norm_pull(grad_normed_mid)
    grad_middle = grad_out.astype(jnp.float32) + grad_middle_norm
    grad_attended = lax.all_gather(grad_middle.astype(jnp.bfloat16), "tensor", axis=0, tiled=True)
    grad_output_w = contract(head_out, grad_attended)
    grad_head = against(grad_attended, full_output).astype(jnp.bfloat16)
    grad_head = grad_head.reshape(
        sequence_batch, SEQUENCE_TOKENS, key_heads, grouped_heads, head_width
    )
    scores = masked_scores(query_rot, keys_rot, scaling, causal)
    attn_probs = jnp.exp(scores - log_totals)
    probs_again = attn_probs.astype(jnp.bfloat16)
    grad_probs = jnp.einsum(
        "bqngd,btnd->bngqt", grad_head, values_low, preferred_element_type=jnp.float32
    )
    inner = jnp.sum(attn_probs * grad_probs, axis=-1, keepdims=True)
    grad_scores = (attn_probs * (grad_probs - inner)).astype(jnp.bfloat16)
    grad_values = jnp.einsum(
        "bngqt,bqngd->btnd", probs_again, grad_head, preferred_element_type=jnp.float32
    )
    grad_values_low = grad_values.astype(jnp.bfloat16).reshape(group_rows, key_heads * head_width)
    grad_query_rot = (
        jnp.einsum("bngqt,btnd->bqngd", grad_scores, keys_rot, preferred_element_type=jnp.float32)
        * scaling
    )
    grad_query_rot = grad_query_rot.reshape(
        sequence_batch, SEQUENCE_TOKENS, query_heads, head_width
    )
    grad_keys_rot = (
        jnp.einsum("bngqt,bqngd->btnd", grad_scores, query_rot, preferred_element_type=jnp.float32)
        * scaling
    )
    grad_query_f, grad_gain_query = query_pull(grad_query_rot)
    grad_keys_f, grad_gain_keys = keys_pull(grad_keys_rot)
    grad_query_low = grad_query_f.astype(jnp.bfloat16).reshape(group_rows, query_heads * head_width)
    grad_keys_low = grad_keys_f.astype(jnp.bfloat16).reshape(group_rows, key_heads * head_width)
    grad_query_w = contract(normalized_rows, grad_query_low)
    grad_keys_w = contract(normalized_rows, grad_keys_low)
    grad_values_w = contract(normalized_rows, grad_values_low)
    grad_normed = lax.psum_scatter(
        against(grad_query_low, full_query)
        + against(grad_keys_low, full_keys)
        + against(grad_values_low, full_values),
        "tensor",
        scatter_dimension=0,
        tiled=True,
    )
    grad_inputs_norm, grad_gain_attn = attn_norm_pull(grad_normed)
    grad_inputs = (grad_middle + grad_inputs_norm).astype(jnp.bfloat16)
    query_part, keys_part, values_part, output_part, gate_part, up_part, down_part = (
        lax.psum_scatter(
            grad_query_w.astype(jnp.bfloat16), "dp", scatter_dimension=0, tiled=True
        ).astype(jnp.float32),
        lax.psum_scatter(
            grad_keys_w.astype(jnp.bfloat16), "dp", scatter_dimension=0, tiled=True
        ).astype(jnp.float32),
        lax.psum_scatter(
            grad_values_w.astype(jnp.bfloat16), "dp", scatter_dimension=0, tiled=True
        ).astype(jnp.float32),
        lax.psum_scatter(
            grad_output_w.astype(jnp.bfloat16), "dp", scatter_dimension=1, tiled=True
        ).astype(jnp.float32),
        lax.psum_scatter(
            grad_gate_w.astype(jnp.bfloat16), "dp", scatter_dimension=0, tiled=True
        ).astype(jnp.float32),
        lax.psum_scatter(
            grad_up_w.astype(jnp.bfloat16), "dp", scatter_dimension=0, tiled=True
        ).astype(jnp.float32),
        lax.psum_scatter(
            grad_down.astype(jnp.bfloat16), "dp", scatter_dimension=1, tiled=True
        ).astype(jnp.float32),
    )
    attn_gain, mlp_gain, query_gain, keys_gain = lax.psum(
        (grad_gain_attn, grad_gain_mlp, grad_gain_query, grad_gain_keys), ("dp", "tensor")
    )
    return (
        layer_out,
        grad_inputs,
        query_part,
        keys_part,
        values_part,
        output_part,
        gate_part,
        up_part,
        down_part,
        attn_gain,
        mlp_gain,
        query_gain,
        keys_gain,
    )


def solution(mesh):
    in_specs = (
        P(("dp", "tensor"), None),
        P(("dp", "tensor"), None),
        P("dp", "tensor"),
        P("dp", "tensor"),
        P("dp", "tensor"),
        P("tensor", "dp"),
        P("dp", "tensor"),
        P("dp", "tensor"),
        P("tensor", "dp"),
        P(),
        P(),
        P(),
        P(),
    )
    out_specs = (
        P(("dp", "tensor"), None),
        P(("dp", "tensor"), None),
        P("dp", "tensor"),
        P("dp", "tensor"),
        P("dp", "tensor"),
        P("tensor", "dp"),
        P("dp", "tensor"),
        P("dp", "tensor"),
        P("tensor", "dp"),
        P(),
        P(),
        P(),
        P(),
    )
    return jax.shard_map(body, mesh=mesh, in_specs=in_specs, out_specs=out_specs, check_vma=False)
```

profile of v0, /device:TPU:0, one launch (start us, length us, event | category | flops | bytes accessed | tf_op | source)
XLA Modules:
  0.0 1190.4 jit_solution(4453018887241153097)
XLA Ops:
  17.4 33.4 %all-gather.16.cloned.1.call-done = bf16[1024,512]{1,0:T(8,128)(2,1)} async-done(((bf16[64,512]{1,0:T(8,128)(2,1)}), bf16[1024,512]{1,0:T(8,128)(2,1)}) %all-gather.16.cloned.1.call-update) | async-done | bytes 1048592 | tf_op jit(solution)/shard_map/all_gather | solution.py:80
  50.8 34.2 %all-gather.12.cloned.1.call-done = bf16[1024,1024]{1,0:T(8,128)(2,1)} async-done(((bf16[512,1024]{1,0:T(8,128)(2,1)}), bf16[1024,1024]{1,0:T(8,128)(2,1)}) %all-gather.12.cloned.1.call-update) | async-done | bytes 2097168 | tf_op jit(solution)/shard_map/all_gather | solution.py:96
  85.0 4.5 fusion.68
  96.2 29.0 %all-gather.14.cloned.1.call-done = bf16[1024,512]{1,0:T(8,128)(2,1)} async-done(((bf16[64,512]{1,0:T(8,128)(2,1)}), bf16[1024,512]{1,0:T(8,128)(2,1)}) %all-gather.14.cloned.1.call-update) | async-done | bytes 1048592 | tf_op jit(solution)/shard_map/all_gather | solution.py:81
  134.0 33.6 %all-gather.18.cloned.1.call-done = bf16[1024,1024]{1,0:T(8,128)(2,1)} async-done(((bf16[64,1024]{1,0:T(8,128)(2,1)}), bf16[1024,1024]{1,0:T(8,128)(2,1)}) %all-gather.18.cloned.1.call-update) | async-done | bytes 2097168 | tf_op jit(solution)/shard_map/all_gather | solution.py:79
  167.5 6.6 fusion.69
  174.2 6.6 reshape.167
  187.4 5.3 copy.169
  198.1 7.3 copy.168
  209.7 7.7 fusion.67
  217.4 8.3 fusion.3
  225.7 9.2 convert_bitcast_fusion
  234.9 4.8 copy.174
  242.4 6.6 fusion.70
  249.8 52.4 %reduce-scatter.12.cloned.1.call-done = f32[512,1024]{1,0:T(8,128)} async-done(((f32[1024,1024]{1,0:T(8,128)}), f32[512,1024]{1,0:T(8,128)}) %reduce-scatter.12.cloned.1.call-update) | async-done | bytes 2097168 | tf_op jit(solution)/shard_map/reduce_scatter | solution.py:126
  308.0 42.2 %all-gather.26.cloned.1.call-done = bf16[1024,1536]{1,0:T(8,128)(2,1)} async-done(((bf16[64,1536]{1,0:T(8,128)(2,1)}), bf16[1024,1536]{1,0:T(8,128)(2,1)}) %all-gather.26.cloned.1.call-update) | async-done | bytes 3145744 | tf_op jit(solution)/shard_map/all_gather | solution.py:84
  350.2 33.6 %all-gather.22.cloned.1.call-done = bf16[1024,1024]{1,0:T(8,128)(2,1)} async-done(((bf16[512,1024]{1,0:T(8,128)(2,1)}), bf16[1024,1024]{1,0:T(8,128)(2,1)}) %all-gather.22.cloned.1.call-update) | async-done | bytes 2097168 | tf_op jit(solution)/shard_map/all_gather | solution.py:130
  383.8 8.5 fusion.72
  392.3 39.2 %all-gather.24.cloned.1.call-done = bf16[1024,1536]{1,0:T(8,128)(2,1)} async-done(((bf16[64,1536]{1,0:T(8,128)(2,1)}), bf16[1024,1536]{1,0:T(8,128)(2,1)}) %all-gather.24.cloned.1.call-update) | async-done | bytes 3145744 | tf_op jit(solution)/shard_map/all_gather | solution.py:83
  431.6 8.6 fusion.71
  440.2 24.8 %all-gather.30.cloned.1.call-done = bf16[1024,1024]{1,0:T(8,128)(2,1)} async-done(((bf16[512,1024]{1,0:T(8,128)(2,1)}), bf16[1024,1024]{1,0:T(8,128)(2,1)}) %all-gather.30.cloned.1.call-update) | async-done | bytes 2097168 | tf_op jit(solution)/shard_map/all_gather | solution.py:153
  465.0 47.8 %all-gather.28.cloned.1.call-done = bf16[1536,1024]{0,1:T(8,128)(2,1)} async-done(((bf16[1536,64]{0,1:T(8,128)(2,1)}), bf16[1536,1024]{0,1:T(8,128)(2,1)}) %all-gather.28.cloned.1.call-update) | async-done | bytes 3145744 | tf_op jit(solution)/shard_map/all_gather | solution.py:85
  512.8 11.7 multiply_convert_fusion
  528.7 5.1 convolution_add_fusion
  533.8 53.2 %reduce-scatter.16.cloned.1.call-done = f32[512,1024]{1,0:T(8,128)} async-done(((f32[1024,1024]{1,0:T(8,128)}), f32[512,1024]{1,0:T(8,128)}) %reduce-scatter.16.cloned.1.call-update) | async-done | bytes 2097168 | tf_op jit(solution)/shard_map/reduce_scatter | solution.py:161
  591.1 7.7 convolution_convert_fusion.1
  599.0 8.0 convolution_convert_fusion.2
  607.0 7.7 convolution_convert_fusion
  615.0 9.2 all-gather.32.cloned.1.call-done
  624.2 5.9 convolution_convert_fusion.4
  630.1 4.5 reshape.170
  634.6 6.2 copy.185
  640.8 11.0 fusion.41
  657.7 15.8 %fusion = (f32[2,4,2,512]{3,2,1,0:T(2,128)S(1)}, f32[2,4,512,512,2]{3,2,4,1,0:T(8,128)}) fusion(f32[2,4,2,512,512]{3,4,2,1,0:T(8,128)} %get-tuple-element.49, f32[2,4,2,512]{3,2,1,0:T(2,128)S(1)} %bitcast.138, bf16[2,512,4,2,128]{1,4,3,2,0:T(8,128)(2,1)} %copy.185, bf16[2,512,4,128,1]{3,2,1,0,4:T(4,128)(2,1)} %bitcast.131), kind=kOutput, calls=%fused_computation.2 | convolution fusion | flops 1086316544 | bytes 36765696 | tf_op jit(solution)/shard_map/bqngd,btnd->bngqt/dot_general | solution.py:178
  674.0 12.9 %fusion.2 = bf16[2,4,2,512,512]{3,4,2,1,0:T(8,128)(2,1)S(1)} fusion(f32[2,4,512,512,2]{3,2,4,1,0:T(8,128)} %get-tuple-element.51, f32[2,4,2,512,512]{3,4,2,1,0:T(8,128)} %get-tuple-element.49, f32[2,4,2,512]{3,2,1,0:T(2,128)S(1)} %get-tuple-element.50, f32[2,4,2,512]{3,2,1,0:T(2,128)S(1)} %bitcast.139), kind=kLoop, calls=%fused_computation.4 | loop fusion | flops 16777216 | bytes 42008576 | tf_op jit(solution)/shard_map/convert_element_type | solution.py:182
  699.4 5.9 convolution_convert_fusion.3
  706.6 5.0 convolution_multiply_fusion
  724.0 6.3 fusion.34
  740.3 7.7 convolution_convert_fusion.5
  749.8 13.3 %reduce-scatter.28.cloned.1.call-done = bf16[64,1536]{1,0:T(8,128)(2,1)} async-done(((bf16[1024,1536]{1,0:T(8,128)(2,1)}), bf16[64,1536]{1,0:T(8,128)(2,1)}) %reduce-scatter.28.cloned.1.call-update) | async-done | bytes 196624 | tf_op jit(solution)/shard_map/reduce_scatter | solution.py:228
  764.7 67.2 %reduce-scatter.32.cloned.1.call-done = bf16[1536,64]{0,1:T(8,128)(2,1)} async-done(((bf16[1536,1024]{0,1:T(8,128)(2,1)}), bf16[1536,64]{0,1:T(8,128)(2,1)}) %reduce-scatter.32.cloned.1.call-update) | async-done | bytes 196624 | tf_op jit(solution)/shard_map/reduce_scatter | solution.py:234
  833.6 58.1 %reduce-scatter.24.cloned.1.call-done = bf16[64,512]{1,0:T(8,128)(2,1)} async-done(((bf16[1024,512]{1,0:T(8,128)(2,1)}), bf16[64,512]{1,0:T(8,128)(2,1)}) %reduce-scatter.24.cloned.1.call-update) | async-done | bytes 65552 | tf_op jit(solution)/shard_map/reduce_scatter | solution.py:222
  893.3 58.9 %reduce-scatter.22.cloned.1.call-done = bf16[64,512]{1,0:T(8,128)(2,1)} async-done(((bf16[1024,512]{1,0:T(8,128)(2,1)}), bf16[64,512]{1,0:T(8,128)(2,1)}) %reduce-scatter.22.cloned.1.call-update) | async-done | bytes 65552 | tf_op jit(solution)/shard_map/reduce_scatter | solution.py:219
  953.7 62.8 %reduce-scatter.26.cloned.1.call-done = bf16[1024,64]{0,1:T(8,128)(2,1)} async-done(((bf16[1024,1024]{0,1:T(8,128)(2,1)}), bf16[1024,64]{0,1:T(8,128)(2,1)}) %reduce-scatter.26.cloned.1.call-update) | async-done | bytes 131088 | tf_op jit(solution)/shard_map/reduce_scatter | solution.py:225
  1018.1 63.0 %reduce-scatter.20.cloned.1.call-done = bf16[64,1024]{1,0:T(8,128)(2,1)} async-done(((bf16[1024,1024]{1,0:T(8,128)(2,1)}), bf16[64,1024]{1,0:T(8,128)(2,1)}) %reduce-scatter.20.cloned.1.call-update) | async-done | bytes 131088 | tf_op jit(solution)/shard_map/reduce_scatter | solution.py:216
  1082.8 54.0 %reduce-scatter.18.cloned.1.call-done = f32[512,1024]{1,0:T(8,128)} async-done(((f32[1024,1024]{1,0:T(8,128)}), f32[512,1024]{1,0:T(8,128)}) %reduce-scatter.18.cloned.1.call-update) | async-done | bytes 2097168 | tf_op jit(solution)/shard_map/reduce_scatter | solution.py:205
  1139.1 39.8 %all-reduce.4 = (f32[1024]{0:T(1024)}, f32[1024]{0:T(1024)}, f32[128]{0:T(128)}, f32[128]{0:T(128)}) all-reduce(f32[1024]{0:T(1024)S(1)} %get-tuple-element.19, f32[1024]{0:T(1024)S(1)} %get-tuple-element.17, f32[128]{0:T(128)S(1)} %get-tuple-element.13, ...), channel_id=1, replica_groups=mesh['dp'=16,'tensor'=2] {'dp','tensor'}, use_global_device_ids=true, to_apply=%region_23.24 | all-reduce | flops 2304 | bytes 18432 | tf_op jit(solution)/shard_map/psum | solution.py:238
  1179.0 4.4 fusion.23
  (207 shorter events, 115.7 us)
Async XLA Ops:
  7.2 43.7 %all-gather.16.cloned.1.call-start = ((), (), s32[]{:S(2)}) async-start(), calls=%async_computation.13 | async-start | bytes 1114112 | tf_op jit(solution)/shard_map/all_gather | solution.py:80
  7.9 77.1 %all-gather.12.cloned.1.call-start = ((), (), s32[]{:S(2)}) async-start(), calls=%async_computation.11 | async-start | bytes 3145728 | tf_op jit(solution)/shard_map/all_gather | solution.py:96
  13.2 112.0 %all-gather.14.cloned.1.call-start = ((), (), s32[]{:S(2)}) async-start(), calls=%async_computation.12 | async-start | bytes 1114112 | tf_op jit(solution)/shard_map/all_gather | solution.py:81
  13.9 153.6 %all-gather.18.cloned.1.call-start = ((), (), s32[]{:S(2)}) async-start(), calls=%async_computation.14 | async-start | bytes 2228224 | tf_op jit(solution)/shard_map/all_gather | solution.py:79
  14.5 227.9 %all-gather.20.cloned.1.call-start = ((), (), s32[]{:S(2)}) async-start(), calls=%async_computation.15 | async-start | bytes 2228224 | tf_op jit(solution)/shard_map/all_gather | solution.py:82
  15.1 287.2 %reduce-scatter.12.cloned.1.call-start = ((), (), s32[]{:S(2)}) async-start(), calls=%async_computation.16 | async-start | bytes 6291456 | tf_op jit(solution)/shard_map/reduce_scatter | solution.py:126
  96.2 36.3 %copy-start.2 = (f32[2,512,4,128]{1,3,2,0:T(8,128)}, f32[2,512,4,128]{1,3,2,0:T(8,128)S(1)}, u32[]{:S(2)}) copy-start(f32[2,512,4,128]{1,3,2,0:T(8,128)S(1)} %copy.166) | copy-start | bytes 6291460
  134.0 75.7 %copy-start.11 = (bf16[2,512,4,128,1]{1,3,4,2,0:T(8,128)(2,1)}, bf16[2,512,4,128,1]{1,3,4,2,0:T(8,128)(2,1)S(1)}, u32[]{:S(2)}) copy-start(bf16[2,512,4,128,1]{1,3,4,2,0:T(8,128)(2,1)S(1)} %fusion.44) | copy-start | bytes 3145732
  187.4 5.4 copy-start.30
  187.4 5.4 copy-start.26
  187.4 5.3 copy-start.42
  209.6 7.7 copy-start.7
  217.4 8.3 copy-start.20
  249.0 53.3 %copy-start.5 = (bf16[512,1024]{1,0:T(8,128)(2,1)S(1)}, bf16[512,1024]{1,0:T(8,128)(2,1)}, u32[]{:S(2)}) copy-start(bf16[512,1024]{1,0:T(8,128)(2,1)} %param.13) | copy-start | bytes 3145732
  249.0 101.2 %all-gather.26.cloned.1.call-start = ((), (), s32[]{:S(2)}) async-start(), calls=%async_computation.19 | async-start | bytes 3342336 | tf_op jit(solution)/shard_map/all_gather | solution.py:84
  249.8 54.4 %copy-start.34 = (f32[1024]{0:T(1024)S(1)}, f32[1024]{0:T(1024)}, u32[]{:S(2)}) copy-start(f32[1024]{0:T(1024)} %param.23) | copy-start | bytes 12292
  249.8 134.0 %all-gather.22.cloned.1.call-start = ((), (), s32[]{:S(2)}) async-start(), calls=%async_computation.17 | async-start | bytes 3145728 | tf_op jit(solution)/shard_map/all_gather | solution.py:130
  305.4 126.1 %all-gather.24.cloned.1.call-start = ((), (), s32[]{:S(2)}) async-start(), calls=%async_computation.18 | async-start | bytes 3342336 | tf_op jit(solution)/shard_map/all_gather | solution.py:83
  306.2 158.8 %all-gather.30.cloned.1.call-start = ((), (), s32[]{:S(2)}) async-start(), calls=%async_computation.22 | async-start | bytes 3145728 | tf_op jit(solution)/shard_map/all_gather | solution.py:153
  306.8 206.0 %all-gather.28.cloned.1.call-start = ((), (), s32[]{:S(2)}) async-start(), calls=%async_computation.20 | async-start | bytes 3342336 | tf_op jit(solution)/shard_map/all_gather | solution.py:85
  307.5 279.5 %reduce-scatter.16.cloned.1.call-start = ((), (), s32[]{:S(2)}) async-start(), calls=%async_computation.23 | async-start | bytes 6291456 | tf_op jit(solution)/shard_map/reduce_scatter | solution.py:161
  512.8 11.7 copy-start.45
  524.5 3.5 copy-start.48
  524.5 3.5 copy-start.47
  524.5 4.2 copy-start.44
  533.8 55.6 %copy-start.13 = (bf16[512,1024]{1,0:T(8,128)(2,1)S(1)}, bf16[512,1024]{1,0:T(8,128)(2,1)}, u32[]{:S(2)}) copy-start(bf16[512,1024]{1,0:T(8,128)(2,1)} %param.14) | copy-start | bytes 3145732
  533.8 90.4 %all-gather.32.cloned.1.call-start = ((), (), s32[]{:S(2)}) async-start(), calls=%async_computation.24 | async-start | bytes 3145728 | tf_op jit(solution)/shard_map/all_gather | solution.py:169
  590.9 157.1 %reduce-scatter.30.cloned.1.call-start = ((), (), s32[]{:S(2)}) async-start(), calls=%async_computation.31 | async-start | bytes 3342336 | tf_op jit(solution)/shard_map/reduce_scatter | solution.py:231
  598.9 164.1 %reduce-scatter.28.cloned.1.call-start = ((), (), s32[]{:S(2)}) async-start(), calls=%async_computation.30 | async-start | bytes 3342336 | tf_op jit(solution)/shard_map/reduce_scatter | solution.py:228
  606.9 225.0 %reduce-scatter.32.cloned.1.call-start = ((), (), s32[]{:S(2)}) async-start(), calls=%async_computation.32 | async-start | bytes 3342336 | tf_op jit(solution)/shard_map/reduce_scatter | solution.py:234
  614.8 277.0 %reduce-scatter.24.cloned.1.call-start = ((), (), s32[]{:S(2)}) async-start(), calls=%async_computation.28 | async-start | bytes 1114112 | tf_op jit(solution)/shard_map/reduce_scatter | solution.py:222
  653.5 4.3 copy-start.16
  673.6 278.6 %reduce-scatter.22.cloned.1.call-start = ((), (), s32[]{:S(2)}) async-start(), calls=%async_computation.27 | async-start | bytes 1114112 | tf_op jit(solution)/shard_map/reduce_scatter | solution.py:219
  674.0 13.0 %copy-start.8 = (bf16[2,512,4,2,128]{1,4,3,2,0:T(8,128)(2,1)S(1)}, bf16[2,512,4,2,128]{1,4,3,2,0:T(8,128)(2,1)}, u32[]{:S(2)}) copy-start(bf16[2,512,4,2,128]{1,4,3,2,0:T(8,128)(2,1)} %copy-done.7) | copy-start | bytes 6291460
  674.0 13.0 %copy-start.21 = (f32[512,128]{0,1:T(8,128)S(1)}, f32[512,128]{0,1:T(8,128)}, u32[]{:S(2)}) copy-start(f32[512,128]{0,1:T(8,128)} %get-tuple-element.44) | copy-start | bytes 786436
  687.0 3.3 copy-start
  699.3 317.2 %reduce-scatter.26.cloned.1.call-start = ((), (), s32[]{:S(2)}) async-start(), calls=%async_computation.29 | async-start | bytes 2228224 | tf_op jit(solution)/shard_map/reduce_scatter | solution.py:225
  705.4 6.2 copy-start.19
  705.4 375.8 %reduce-scatter.20.cloned.1.call-start = ((), (), s32[]{:S(2)}) async-start(), calls=%async_computation.26 | async-start | bytes 2228224 | tf_op jit(solution)/shard_map/reduce_scatter | solution.py:216
  714.5 2.4 copy-start.31
  730.3 406.5 %reduce-scatter.18.cloned.1.call-start = ((), (), s32[]{:S(2)}) async-start(), calls=%async_computation.25 | async-start | bytes 6291456 | tf_op jit(solution)/shard_map/reduce_scatter | solution.py:205
  731.5 2.7 copy-start.22
  731.5 2.7 copy-start.46
  740.0 439.0 %reduce-scatter.14.cloned.1.call-start = ((), (), s32[]{:S(2)}) async-start(), calls=%async_computation.21 | async-start | bytes 3145728 | tf_op jit(solution)/shard_map/reduce_scatter | solution.py:137
  747.9 388.9 %copy-start.6 = (bf16[512,1024]{1,0:T(8,128)(2,1)S(1)}, bf16[512,1024]{1,0:T(8,128)(2,1)}, u32[]{:S(2)}) copy-start(bf16[512,1024]{1,0:T(8,128)(2,1)} %param.13) | copy-start | bytes 3145732
  747.9 388.9 %copy-start.35 = (f32[1024]{0:T(1024)S(1)}, f32[1024]{0:T(1024)}, u32[]{:S(2)}) copy-start(f32[1024]{0:T(1024)} %param.22) | copy-start | bytes 12292
  747.9 388.9 %copy-start.37 = (f32[512]{0:T(512)S(1)}, f32[512]{0:T(512)}, u32[]{:S(2)}) copy-start(f32[512]{0:T(512)} %copy-done.36) | copy-start | bytes 6148
  893.3 285.7 %copy-start.39 = (f32[512]{0:T(512)S(1)}, f32[512]{0:T(512)}, u32[]{:S(2)}) copy-start(f32[512]{0:T(512)} %copy-done.38) | copy-start | bytes 6148
  (23 other events, 37.1 us)
Sparse Core Ops, SparseCore 0:
  10.2 40.6 all-gather.15
  53.0 32.0 all-gather.11
  87.2 37.9 all-gather.13
  127.2 40.3 all-gather.17
  169.5 40.1 all-gather.19
  249.1 53.0 reduce-scatter.11
  304.8 45.3 all-gather.25
  351.8 31.9 all-gather.21
  386.3 45.1 all-gather.23
  433.0 31.9 all-gather.29
  467.6 45.1 all-gather.27
  533.9 53.0 reduce-scatter.15
  591.0 33.1 all-gather.31
  627.8 66.2 reduce-scatter.29
  697.8 65.2 reduce-scatter.27
  766.7 65.1 reduce-scatter.31
  835.4 56.3 reduce-scatter.23
  895.7 56.4 reduce-scatter.21
  955.9 60.5 reduce-scatter.25
  1020.6 60.5 reduce-scatter.19
  1083.5 53.2 reduce-scatter.17
  1139.1 32.4 reduce-scatter.13
where the time goes:
time: 1190 us
  waiting for transfers between devices  815 us (68%)
  matrix products  177 us (15%)
  other arithmetic  74.4 us (6%)
  local copies, waits for them, and re-layouts  66.6 us (6%)
  blocking collectives  39.8 us (3%)
  between operations  15.2 us (1%)
    reduce_scatter x1, waiting for transfers between devices, body(): lax.psum_scatter(grad_down.astype(jnp.bfloat16), 'dp', scatter_dimension=...  67.2 us
    reduce_scatter x1, waiting for transfers between devices, body(): lax.psum_scatter(grad_query_w.astype(jnp.bfloat16), 'dp', scatter_dimensi...  63 us
    reduce_scatter x1, waiting for transfers between devices, body(): lax.psum_scatter(grad_output_w.astype(jnp.bfloat16), 'dp', scatter_dimens...  62.8 us
    reduce_scatter x1, waiting for transfers between devices, body(): lax.psum_scatter(grad_keys_w.astype(jnp.bfloat16), 'dp', scatter_dimensio...  58.9 us
    reduce_scatter x1, waiting for transfers between devices, body(): lax.psum_scatter(grad_values_w.astype(jnp.bfloat16), 'dp', scatter_dimens...  58.1 us
    reduce_scatter x1, waiting for transfers between devices, body(): lax.psum_scatter(against(grad_query_low, full_query) + against(grad_keys_...  54 us
    reduce_scatter x1, waiting for transfers between devices, body(): lax.psum_scatter(against(grad_gate_low, full_gate) + against(grad_up_low,...  53.2 us
    reduce_scatter x1, waiting for transfers between devices, body(): lax.psum_scatter(matmul(head_out, full_output), 'tensor', scatter_dimensi...  52.4 us
  transfers between devices with their start and end apart: 22, of which 19 were waited for; matrix products, arithmetic and copies ran while one was open for 23% of the time, Pallas kernels for 0%

commit v1 on v0

v1 whole, which is shorter than its diff:
```python
import functools

import jax
import jax.numpy as jnp
import numpy as np
from jax import lax
from jax.experimental import pallas as pl
from jax.experimental.pallas import tpu as pltpu
from jax.sharding import PartitionSpec as P

SEQ = 512
EPSILON = 1e-06
THETA = 1000000.0
F32 = jnp.float32
BF16 = jnp.bfloat16
VMEM_LIMIT = 56 * 1024 * 1024


def dot(left, right):
    return lax.dot_general(left, right, (((1,), (0,)), ((), ())), preferred_element_type=F32)


def dot_t(left, right):
    return lax.dot_general(left, right, (((1,), (1,)), ((), ())), preferred_element_type=F32)


def rope_tables(width):
    half = width // 2
    places = np.arange(SEQ, dtype=np.float32)
    inverse = (THETA ** (-2.0 * np.arange(half, dtype=np.float32) / width)).astype(np.float32)
    angles = places[:, None] * inverse[None, :]
    cosine = np.concatenate([np.cos(angles), np.cos(angles)], axis=-1)
    sine = np.concatenate([-np.sin(angles), np.sin(angles)], axis=-1)
    return cosine.astype(np.float32), sine.astype(np.float32)


def rope(values, cosine, sine):
    half = values.shape[-1] // 2
    return values * cosine + pltpu.roll(values, half, 1) * sine


def rope_back(values, cosine, sine):
    half = values.shape[-1] // 2
    return values * cosine + pltpu.roll(values * sine, half, 1)


def exponents_t(keys_rot, query_rot, factor):
    scores = dot_t(keys_rot, query_rot)
    key_place = lax.broadcasted_iota(jnp.int32, scores.shape, 0)
    query_place = lax.broadcasted_iota(jnp.int32, scores.shape, 1)
    return jnp.where(key_place <= query_place, jnp.exp2(scores * factor), 0.0)


def attend_kernel(
    group, width, normed_ref, weight_ref, cos_ref, sin_ref, gain_q_ref, gain_k_ref, part_ref, kept_ref, total
):
    step = pl.program_id(0)
    rows = normed_ref.shape[0]
    wide = group * width
    factor = float(width**-0.5 * np.log2(np.e))
    proj = dot(normed_ref[...], weight_ref[:, : wide + 2 * width])
    kept_ref[:, : wide + width] = proj[:, : wide + width].astype(BF16)
    values = proj[:, wide + width :].astype(BF16)
    base = 2 * (wide + width)
    kept_ref[:, base : base + width] = values
    for seq in range(rows // SEQ):
        place = slice(seq * SEQ, (seq + 1) * SEQ)
        rotated = []
        for head in range(group + 1):
            raw = proj[place, head * width : (head + 1) * width]
            scale = lax.rsqrt(jnp.mean(raw * raw, axis=-1, keepdims=True) + EPSILON)
            gain = gain_q_ref[...] if head < group else gain_k_ref[...]
            turned = rope(raw * scale * gain, cos_ref[...], sin_ref[...]).astype(BF16)
            kept_ref[place, wide + width + head * width : wide + width + (head + 1) * width] = turned
            rotated.append(turned)
        values_t = values[place].T
        for head in range(group):
            exponents = exponents_t(rotated[group], rotated[head], factor)
            sums = jnp.sum(exponents, axis=0, keepdims=True)
            out_t = dot(values_t, exponents.astype(BF16)) * (1.0 / sums)
            start = base + width + head * width
            kept_ref[place, start : start + width] = out_t.T.astype(BF16)
    out = dot_t(kept_ref[:, base + width :], weight_ref[:, wide + 2 * width :])

    @pl.when(step == 0)
    def _():
        total[...] = out

    @pl.when(step > 0)
    def _():
        total[...] += out

    @pl.when(step == pl.num_programs(0) - 1)
    def _():
        part_ref[...] = total[...].astype(BF16)


def attend(normed, weights, tables, gain_q, gain_k, heads, group, width):
    rows, model = normed.shape
    block = weights.shape[1] // heads
    kept_block = (4 * group + 3) * width - group * width
    whole = lambda *dims: pl.BlockSpec(dims, lambda j: (0,) * len(dims))
    flops = heads * (2 * rows * model * block + 4 * rows * SEQ * group * width)
    return pl.pallas_call(
        functools.partial(attend_kernel, group, width),
        grid=(heads,),
        in_specs=[
            whole(rows, model),
            pl.BlockSpec((model, block), lambda j: (0, j)),
            whole(SEQ, width),
            whole(SEQ, width),
            whole(1, width),
            whole(1, width),
        ],
        out_specs=[whole(rows, model), pl.BlockSpec((rows, kept_block), lambda j: (0, j))],
        out_shape=[
            jax.ShapeDtypeStruct((rows, model), BF16),
            jax.ShapeDtypeStruct((rows, heads * kept_block), BF16),
        ],
        scratch_shapes=[pltpu.VMEM((rows, model), F32)],
        compiler_params=pltpu.CompilerParams(vmem_limit_bytes=VMEM_LIMIT),
        cost_estimate=pl.CostEstimate(
            flops=flops, bytes_accessed=weights.size * 2 + 4 * rows * model * 2, transcendentals=0
        ),
        name="attend",
    )(normed, weights, *tables, gain_q, gain_k)


def mlp_kernel(
    normed_ref,
    grad_ref,
    weight_ref,
    gain_ref,
    out_ref,
    dx_ref,
    dw_ref,
    dgain_ref,
    normed_t,
    grad_t,
    out_total,
    dx_total,
):
    step = pl.program_id(0)
    units = weight_ref.shape[1] // 3

    @pl.when(step == 0)
    def _():
        normed_t[...] = normed_ref[...].T
        grad_t[...] = grad_ref[...].T
        out_total[...] = jnp.zeros_like(out_total)
        dx_total[...] = jnp.zeros_like(dx_total)

    both = dot(normed_ref[...], weight_ref[:, : 2 * units])
    gate, up = both[:, :units], both[:, units:]
    sig = 1.0 / (1.0 + jnp.exp(-gate))
    silu = gate * sig
    hidden = (silu * up).astype(BF16)
    grad_hidden = dot(grad_ref[...], weight_ref[:, 2 * units :])
    grad_gate = (grad_hidden * up * (sig + silu * (1.0 - sig))).astype(BF16)
    grad_up = (grad_hidden * silu).astype(BF16)
    out_total[...] += dot_t(hidden, weight_ref[:, 2 * units :])
    dx_total[...] += dot_t(grad_gate, weight_ref[:, :units]) + dot_t(
        grad_up, weight_ref[:, units : 2 * units]
    )
    dw_ref[:, :units] = dot(normed_t[...], grad_gate).astype(BF16)
    dw_ref[:, units : 2 * units] = dot(normed_t[...], grad_up).astype(BF16)
    dw_ref[:, 2 * units :] = dot(grad_t[...], hidden).astype(BF16)

    @pl.when(step == pl.num_programs(0) - 1)
    def _():
        out_ref[...] = out_total[...].astype(BF16)
        dx_ref[...] = dx_total[...].astype(BF16)
        dgain_ref[...] = (
            jnp.sum(normed_ref[...].astype(F32) * dx_total[...], axis=0, keepdims=True) / gain_ref[...]
        )


def mlp(normed, grad_rows, weights, gain, steps):
    rows, model = normed.shape
    block = weights.shape[1] // steps
    whole = lambda *dims: pl.BlockSpec(dims, lambda j: (0,) * len(dims))
    columns = pl.BlockSpec((model, block), lambda j: (0, j))
    return pl.pallas_call(
        mlp_kernel,
        grid=(steps,),
        in_specs=[whole(rows, model), whole(rows, model), columns, whole(1, model)],
        out_specs=[whole(rows, model), whole(rows, model), columns, whole(1, model)],
        out_shape=[
            jax.ShapeDtypeStruct((rows, model), BF16),
            jax.ShapeDtypeStruct((rows, model), BF16),
            jax.ShapeDtypeStruct(weights.shape, BF16),
            jax.ShapeDtypeStruct((1, model), F32),
        ],
        scratch_shapes=[
            pltpu.VMEM((model, rows), BF16),
            pltpu.VMEM((model, rows), BF16),
            pltpu.VMEM((rows, model), F32),
            pltpu.VMEM((rows, model), F32),
        ],
        compiler_params=pltpu.CompilerParams(vmem_limit_bytes=VMEM_LIMIT),
        cost_estimate=pl.CostEstimate(
            flops=6 * rows * weights.size, bytes_accessed=4 * weights.size + 8 * rows * model, transcendentals=0
        ),
        name="mlp",
    )(normed, grad_rows, weights, gain)


def attend_back_kernel(
    group,
    width,
    normed_ref,
    grad_ref,
    weight_ref,
    kept_ref,
    cos_ref,
    sin_ref,
    gain_q_ref,
    gain_k_ref,
    gain_ref,
    dx_ref,
    dw_ref,
    dgain_ref,
    dgain_heads_ref,
    normed_t,
    grad_t,
    dx_total,
    dproj,
):
    step = pl.program_id(0)
    rows = normed_ref.shape[0]
    wide = group * width
    scaling = float(width**-0.5)
    factor = float(width**-0.5 * np.log2(np.e))
    rot = wide + width
    base = 2 * rot

    @pl.when(step == 0)
    def _():
        normed_t[...] = normed_ref[...].T
        grad_t[...] = grad_ref[...].T
        dx_total[...] = jnp.zeros_like(dx_total)
        dgain_heads_ref[...] = jnp.zeros_like(dgain_heads_ref)

    grad_heads = dot(grad_ref[...], weight_ref[:, wide + 2 * width :]).astype(BF16)
    dw_ref[:, wide + 2 * width :] = dot(grad_t[...], kept_ref[:, base + width :]).astype(BF16)

    def head_back(place, head, cotangent):
        gain = gain_q_ref[...] if head < group else gain_k_ref[...]
        raw = kept_ref[place, head * width : (head + 1) * width].astype(F32)
        scale = lax.rsqrt(jnp.mean(raw * raw, axis=-1, keepdims=True) + EPSILON)
        unit = raw * scale
        cot = rope_back(cotangent * scaling, cos_ref[...], sin_ref[...])
        row = 0 if head < group else 1
        dgain_heads_ref[row : row + 1, :] += jnp.sum(cot * unit, axis=0, keepdims=True)
        cot = cot * gain
        grad = scale * (cot - unit * jnp.mean(unit * cot, axis=-1, keepdims=True))
        dproj[place, head * width : (head + 1) * width] = grad.astype(BF16)

    for seq in range(rows // SEQ):
        place = slice(seq * SEQ, (seq + 1) * SEQ)
        keys_rot = kept_ref[place, rot + wide : rot + wide + width]
        keys_t = keys_rot.T
        values = kept_ref[place, base : base + width]
        dkeys = jnp.zeros((SEQ, width), F32)
        dvalues = jnp.zeros((SEQ, width), F32)
        for head in range(group):
            query_rot = kept_ref[place, rot + head * width : rot + (head + 1) * width]
            grad_head = grad_heads[place, head * width : (head + 1) * width]
            exponents = exponents_t(keys_rot, query_rot, factor)
            probs = exponents * (1.0 / jnp.sum(exponents, axis=0, keepdims=True))
            dprobs = dot_t(values, grad_head)
            inner = jnp.sum(probs * dprobs, axis=0, keepdims=True)
            dscores = (probs * (dprobs - inner)).astype(BF16)
            dvalues += dot(probs.astype(BF16), grad_head)
            dkeys += dot(dscores, query_rot)
            head_back(place, head, dot(keys_t, dscores).T)
        head_back(place, group, dkeys)
        dproj[place, wide + width :] = dvalues.astype(BF16)

    dx_total[...] += dot_t(dproj[...], weight_ref[:, : wide + 2 * width])
    dw_ref[:, : wide + 2 * width] = dot(normed_t[...], dproj[...]).astype(BF16)

    @pl.when(step == pl.num_programs(0) - 1)
    def _():
        dx_ref[...] = dx_total[...].astype(BF16)
        dgain_ref[...] = (
            jnp.sum(normed_ref[...].astype(F32) * dx_total[...], axis=0, keepdims=True) / gain_ref[...]
        )


def attend_back(normed, grad_rows, weights, kept, tables, gain_q, gain_k, gain, heads, group, width):
    rows, model = normed.shape
    block = weights.shape[1] // heads
    kept_block = kept.shape[1] // heads
    whole = lambda *dims: pl.BlockSpec(dims, lambda j: (0,) * len(dims))
    columns = pl.BlockSpec((model, block), lambda j: (0, j))
    flops = heads * (4 * rows * model * block + 10 * rows * SEQ * group * width)
    return pl.pallas_call(
        functools.partial(attend_back_kernel, group, width),
        grid=(heads,),
        in_specs=[
            whole(rows, model),
            whole(rows, model),
            columns,
            pl.BlockSpec((rows, kept_block), lambda j: (0, j)),
            whole(SEQ, width),
            whole(SEQ, width),
            whole(1, width),
            whole(1, width),
            whole(1, model),
        ],
        out_specs=[whole(rows, model), columns, whole(1, model), whole(8, width)],
        out_shape=[
            jax.ShapeDtypeStruct((rows, model), BF16),
            jax.ShapeDtypeStruct(weights.shape, BF16),
            jax.ShapeDtypeStruct((1, model), F32),
            jax.ShapeDtypeStruct((8, width), F32),
        ],
        scratch_shapes=[
            pltpu.VMEM((model, rows), BF16),
            pltpu.VMEM((model, rows), BF16),
            pltpu.VMEM((rows, model), F32),
            pltpu.VMEM((rows, (group + 2) * width), BF16),
        ],
        compiler_params=pltpu.CompilerParams(vmem_limit_bytes=VMEM_LIMIT),
        cost_estimate=pl.CostEstimate(
            flops=flops, bytes_accessed=4 * weights.size + 10 * rows * model, transcendentals=0
        ),
        name="attend_back",
    )(normed, grad_rows, weights, kept, *tables, gain_q, gain_k, gain)


def unit_rows(values):
    scale = lax.rsqrt(jnp.mean(values * values, axis=-1, keepdims=True) + EPSILON)
    return values * scale, scale


def norm_back(unit, scale, cotangent):
    return scale * (cotangent - unit * jnp.mean(unit * cotangent, axis=-1, keepdims=True))


def pack(parts, pieces):
    rows = parts[0].shape[0]
    split = [part.reshape(rows, pieces, part.shape[1] // pieces) for part in parts]
    return jnp.concatenate(split, axis=2).reshape(rows, -1)


def unpack(packed, pieces, widths):
    rows = packed.shape[0]
    split = packed.reshape(rows, pieces, -1).astype(F32)
    ends = np.cumsum([width // pieces for width in widths])
    return [
        split[:, :, end - width // pieces : end].reshape(rows, width) for end, width in zip(ends, widths)
    ]


def body(
    tensor_size,
    inputs,
    grad_out,
    w_query,
    key_weight,
    value_weight,
    w_output,
    w_gate,
    w_up,
    w_down,
    gain_attn,
    gain_mlp,
    gain_query,
    gain_keys,
):
    rows = inputs.shape[0]
    width = gain_query.shape[0]
    heads = key_weight.shape[1] // width
    group = w_query.shape[1] // key_weight.shape[1]
    hidden = w_gate.shape[1]
    steps = max(1, hidden // 256)
    by_pair = tensor_size == 2 and rows % SEQ == 0
    swap = ((0, 1), (1, 0))

    def gather_rows(own):
        if by_pair:
            return jnp.concatenate([own, lax.ppermute(own, "tensor", swap)], axis=0)
        return lax.all_gather(own, "tensor", axis=0, tiled=True)

    def sum_rows(part):
        if by_pair:
            return part[:rows].astype(F32) + lax.ppermute(part[rows:], "tensor", swap).astype(F32)
        return lax.psum_scatter(part, "tensor", scatter_dimension=0, tiled=True).astype(F32)

    tables = rope_tables(width)
    gain_q, gain_k = gain_query[None, :], gain_keys[None, :]
    attn_weights = lax.all_gather(
        pack([w_query, key_weight, value_weight, w_output.T], heads), "dp", axis=0, tiled=True
    )
    mlp_weights = lax.all_gather(pack([w_gate, w_up, w_down.T], steps), "dp", axis=0, tiled=True)

    inputs_f = inputs.astype(F32)
    unit_in, scale_in = unit_rows(inputs_f)
    normed = gather_rows((unit_in * gain_attn).astype(BF16))
    grad_rows = gather_rows(grad_out)
    part, kept = attend(normed, attn_weights, tables, gain_q, gain_k, heads, group, width)
    middle = inputs_f + sum_rows(part)
    unit_mid, scale_mid = unit_rows(middle)
    normed_mlp = gather_rows((unit_mid * gain_mlp).astype(BF16))
    ffn_part, dx_part, dw_mlp, dgain_mlp = mlp(normed_mlp, grad_rows, mlp_weights, gain_mlp[None, :], steps)
    grad_normed_mlp = sum_rows(dx_part)
    grad_middle = grad_out.astype(F32) + norm_back(unit_mid, scale_mid, grad_normed_mlp * gain_mlp)
    grad_attended = gather_rows(grad_middle.astype(BF16))
    layer_out = (middle + sum_rows(ffn_part)).astype(BF16)
    mlp_grads = lax.psum_scatter(dw_mlp, "dp", scatter_dimension=0, tiled=True)
    dx_part, dw_attn, dgain_attn, dgain_heads = attend_back(
        normed, grad_attended, attn_weights, kept, tables, gain_q, gain_k, gain_attn[None, :], heads, group, width
    )
    attn_grads = lax.psum_scatter(dw_attn, "dp", scatter_dimension=0, tiled=True)
    gains = lax.psum(
        jnp.concatenate([dgain_attn[0], dgain_mlp[0], dgain_heads[0], dgain_heads[1]]), ("dp", "tensor")
    )
    grad_normed = sum_rows(dx_part)
    grad_inputs = (grad_middle + norm_back(unit_in, scale_in, grad_normed * gain_attn)).astype(BF16)

    model = inputs.shape[1]
    query_part, keys_part, values_part, output_part = unpack(
        attn_grads, heads, [w_query.shape[1], key_weight.shape[1], value_weight.shape[1], w_output.shape[0]]
    )
    gate_part, up_part, down_part = unpack(mlp_grads, steps, [hidden, hidden, hidden])
    return (
        layer_out,
        grad_inputs,
        query_part,
        keys_part,
        values_part,
        output_part.T,
        gate_part,
        up_part,
        down_part.T,
        gains[:model],
        gains[model : 2 * model],
        gains[2 * model : 2 * model + width],
        gains[2 * model + width :],
    )


def solution(mesh):
    rows = P(("dp", "tensor"), None)
    wide, tall = P("dp", "tensor"), P("tensor", "dp")
    return jax.shard_map(
        functools.partial(body, mesh.shape["tensor"]),
        mesh=mesh,
        in_specs=(rows, rows, wide, wide, wide, tall, wide, wide, tall, P(), P(), P(), P()),
        out_specs=(rows, rows, wide, wide, wide, tall, wide, wide, tall, P(), P(), P(), P()),
        check_vma=False,
    )
```

time: 1190 us -> 519 us (0.44)
  waiting for transfers between devices: 815 us -> 273 us
  matrix products: 177 us -> 0 us
  Pallas kernels: 0 us -> 103 us
  other arithmetic: 74.4 us -> 18.5 us
  local copies, waits for them, and re-layouts: 66.6 us -> 22.6 us
  blocking collectives: 39.8 us -> 75.1 us
    reduce_scatter x11 -> x2, waiting for transfers between devices: 483 us -> 106 us  [the longest x1 106 us: body(): mlp_grads = lax.psum_scatter(dw_mlp, 'dp', scatter_dimension=0, tiled=True)]
    all_gather x11 -> x2, waiting for transfers between devices: 327 us -> 34.4 us  [the longest x1 34.4 us: body(): lax.all_gather(pack([w_query, key_weight, value_weight, w_output.T], head...]
    dot_general x27 -> x0, matrix products: 177 us -> none  [the longest x7 46.6 us: matmul(): return jnp.dot(left, right, preferred_element_type=jnp.float32)]
    ppermute x0 -> x8, waiting for transfers between devices: none -> 132 us  [the longest x4 85.4 us: gather_rows(): return jnp.concatenate([own, lax.ppermute(own, 'tensor', swap)], axis=0)]
    pallas_call x0 -> x3, Pallas kernels: none -> 103 us  [the longest x1 40.1 us: attend_back(): pl.pallas_call(functools.partial(attend_back_kernel, group, width), grid=...]
    convert_element_type x16 -> x4, other arithmetic: 42.3 us -> 6.9 us  [the longest x1 5.02 us: body(): (grad_middle + norm_back(unit_in, scale_in, grad_normed * gain_attn)).ast...]
    psum x1, blocking collectives: 39.8 us -> 75.1 us  [body(): lax.psum(jnp.concatenate([dgain_attn[0], dgain_mlp[0], dgain_heads[0], dg...]
    reshape x9 -> x8, local copies, waits for them, and re-layouts: 38.8 us -> 5.19 us  [the longest x7 4.48 us: pack(): part.reshape(rows, pieces, part.shape[1] // pieces)]
  transfers between devices with their start and end apart: 22 -> 12, of which waited for: 19 -> 8; matrix products, arithmetic and copies ran while one was open for 23% -> 5% of each run, Pallas kernels for 0% -> 5%
where the time goes in v1:
time: 519 us
  waiting for transfers between devices  273 us (53%)
  Pallas kernels  103 us (20%)
  blocking collectives  75.1 us (14%)
  local copies, waits for them, and re-layouts  22.6 us (4%)
  other arithmetic  18.5 us (4%)
  between operations  14.1 us (3%)
  starting transfers between devices  11.9 us (2%)
    reduce_scatter x1, waiting for transfers between devices, body(): mlp_grads = lax.psum_scatter(dw_mlp, 'dp', scatter_dimension=0, tiled=True)  106 us
    ppermute x4, waiting for transfers between devices, gather_rows(): return jnp.concatenate([own, lax.ppermute(own, 'tensor', swap)], axis=0)  85.4 us
    psum x1, blocking collectives, body(): lax.psum(jnp.concatenate([dgain_attn[0], dgain_mlp[0], dgain_heads[0], dg...  75.1 us
    ppermute x4, waiting for transfers between devices, sum_rows(): lax.ppermute(part[rows:], 'tensor', swap).astype(F32)  47 us
    pallas_call x1, Pallas kernels, attend_back(): pl.pallas_call(functools.partial(attend_back_kernel, group, width), grid=...  40.1 us
    pallas_call x1, Pallas kernels, mlp(): pl.pallas_call(mlp_kernel, grid=(steps,), in_specs=[whole(rows, model), w...  39.4 us
    all_gather x1, waiting for transfers between devices, body(): lax.all_gather(pack([w_query, key_weight, value_weight, w_output.T], head...  34.4 us
    pallas_call x1, Pallas kernels, attend(): pl.pallas_call(functools.partial(attend_kernel, group, width), grid=(head...  24 us
  transfers between devices with their start and end apart: 12, of which 8 were waited for; matrix products, arithmetic and copies ran while one was open for 5% of the time, Pallas kernels for 5%

profile of v1, /device:TPU:0, one launch (start us, length us, event | category | flops | bytes accessed | tf_op | source)
XLA Modules:
  0.0 518.8 jit_solution(12456488022128819613)
XLA Ops:
  7.3 1.0 reshape.107
  8.2 0.9 reshape.108
  9.1 1.0 reshape.106
  10.1 1.0 reshape.109
  11.3 0.8 copy.28
  13.0 0.9 copy.29
  14.6 3.0 collective-permute-start
  17.7 23.2 %collective-permute-done = bf16[512,1024]{1,0:T(8,128)(2,1)S(1)} collective-permute-done((bf16[512,1024]{1,0:T(8,128)(2,1)S(1)}, bf16[512,1024]{1,0:T(8,128)(2,1)S(1)}, u32[]{:S(2)}, u32[]{:S(2)}) %collective-permute-start) | collective-permute-done | bytes 1048608 | tf_op jit(solution)/shard_map/ppermute | solution.py:384
  40.8 1.5 pad_maximum_fusion.normed_ref
  42.3 34.4 %all-gather.3.cloned.1.call-done.weight_ref = bf16[1024,3072]{1,0:T(8,128)(2,1)} async-done(((bf16[64,3072]{1,0:T(8,128)(2,1)}), bf16[1024,3072]{1,0:T(8,128)(2,1)}) %all-gather.3.cloned.1.call-update) | async-done | bytes 6291472 | tf_op jit(solution)/shard_map/all_gather | solution.py:394
  76.8 24.0 %attend.1 = (bf16[1024,1024]{1,0:T(8,128)(2,1)}, bf16[1024,4608]{1,0:T(8,128)(2,1)}) custom-call(bf16[1024,1024]{1,0:T(8,128)(2,1)} %pad_maximum_fusion.normed_ref, bf16[1024,3072]{1,0:T(8,128)(2,1)} %all-gather.3.cloned.1.call-done.weight_ref, f32[512,128]{1,0:T(8,128)} %constant.14.clone.cos_ref, f32[512,128]{1,0:T(8,128)} %constant.15.clone.sin_ref, ...), custom_call_target="tpu_custom_call" | custom-call | flops 8589934592 | bytes 14680064 | tf_op jit(solution)/shard_map/attend/pallas_call | solution.py:104
  100.8 1.4 slice.64
  102.2 1.5 collective-permute-start.1
  103.8 0.6 collective-permute-start.3
  104.3 24.0 %collective-permute-done.1 = bf16[512,1024]{1,0:T(8,128)(2,1)S(1)} collective-permute-done((bf16[512,1024]{1,0:T(8,128)(2,1)S(1)}, bf16[512,1024]{1,0:T(8,128)(2,1)S(1)}, u32[]{:S(2)}, u32[]{:S(2)}) %collective-permute-start.1) | collective-permute-done | bytes 1048608 | tf_op jit(solution)/shard_map/ppermute | solution.py:389
  129.4 1.5 collective-permute-start.2
  130.9 19.8 %collective-permute-done.3 = bf16[512,1024]{1,0:T(8,128)(2,1)S(1)} collective-permute-done((bf16[512,1024]{1,0:T(8,128)(2,1)S(1)}, bf16[512,1024]{1,0:T(8,128)(2,1)S(1)}, u32[]{:S(2)}, u32[]{:S(2)}) %collective-permute-start.3) | collective-permute-done | bytes 1048608 | tf_op jit(solution)/shard_map/ppermute | solution.py:384
  150.8 1.6 pad_maximum_fusion.2.grad_ref
  152.3 20.3 %collective-permute-done.2 = bf16[512,1024]{1,0:T(8,128)(2,1)S(1)} collective-permute-done((bf16[512,1024]{1,0:T(8,128)(2,1)S(1)}, bf16[512,1024]{1,0:T(8,128)(2,1)S(1)}, u32[]{:S(2)}, u32[]{:S(2)}) %collective-permute-start.2) | collective-permute-done | bytes 1048608 | tf_op jit(solution)/shard_map/ppermute | solution.py:384
  172.6 1.4 pad_maximum_fusion.1.normed_ref
  174.0 39.4 %mlp.1 = (bf16[1024,1024]{1,0:T(8,128)(2,1)}, bf16[1024,1024]{1,0:T(8,128)(2,1)}, bf16[1024,4608]{1,0:T(8,128)(2,1)}, f32[1,1024]{1,0:T(1,128)}) custom-call(bf16[1024,1024]{1,0:T(8,128)(2,1)} %pad_maximum_fusion.1.normed_ref, bf16[1024,1024]{1,0:T(8,128)(2,1)} %pad_maximum_fusion.2.grad_ref, bf16[1024,4608]{1,0:T(8,128)(2,1)} %all-gather.5.cloned.1.call-done.weight_ref, ...), custom_call_target="tpu_custom_call" | custom-call | flops 28991029248 | bytes 27262976 | tf_op jit(solution)/shard_map/mlp/pallas_call | solution.py:183
  213.4 1.4 slice.68
  214.9 1.5 collective-permute-start.5
  216.4 23.0 %collective-permute-done.5 = bf16[512,1024]{1,0:T(8,128)(2,1)S(1)} collective-permute-done((bf16[512,1024]{1,0:T(8,128)(2,1)S(1)}, bf16[512,1024]{1,0:T(8,128)(2,1)S(1)}, u32[]{:S(2)}, u32[]{:S(2)}) %collective-permute-start.5) | collective-permute-done | bytes 1048608 | tf_op jit(solution)/shard_map/ppermute | solution.py:389
  239.5 2.1 multiply_reduce_fusion
  241.6 1.1 fusion.10
  242.7 1.5 collective-permute-start.6
  244.2 22.1 %collective-permute-done.6 = bf16[512,1024]{1,0:T(8,128)(2,1)S(1)} collective-permute-done((bf16[512,1024]{1,0:T(8,128)(2,1)S(1)}, bf16[512,1024]{1,0:T(8,128)(2,1)S(1)}, u32[]{:S(2)}, u32[]{:S(2)}) %collective-permute-start.6) | collective-permute-done | bytes 1048608 | tf_op jit(solution)/shard_map/ppermute | solution.py:384
  266.3 1.5 pad_maximum_fusion.3.grad_ref
  267.9 40.1 %attend_back.1 = (bf16[1024,1024]{1,0:T(8,128)(2,1)}, bf16[1024,3072]{1,0:T(8,128)(2,1)}, f32[1,1024]{1,0:T(1,128)}, f32[8,128]{1,0:T(8,128)}) custom-call(bf16[1024,1024]{1,0:T(8,128)(2,1)} %pad_maximum_fusion.normed_ref, bf16[1024,1024]{1,0:T(8,128)(2,1)} %pad_maximum_fusion.3.grad_ref, bf16[1024,3072]{1,0:T(8,128)(2,1)} %all-gather.3.cloned.1.call-done.weight_ref, ...), custom_call_target="tpu_custom_call" | custom-call | flops 18253611008 | bytes 23068672 | tf_op jit(solution)/shard_map/attend_back/pallas_call | solution.py:298
  308.6 2.4 slice.70
  311.0 1.5 collective-permute-start.7
  312.5 1.0 slice.66
  313.5 0.6 collective-permute-start.4
  314.1 0.8 slice_bitcast_fusion.1
  314.9 75.1 %psum.7 = f32[2304]{0:T(1024)S(1)} all-reduce(f32[2304]{0:T(1024)S(1)} %pad_maximum_fusion.6), channel_id=1, replica_groups=mesh['dp'=16,'tensor'=2] {'dp','tensor'}, use_global_device_ids=true, to_apply=%region_6.0 | all-reduce | flops 2304 | bytes 18432 | tf_op jit(solution)/shard_map/psum | solution.py:417
  390.5 0.6 fusion.15
  391.1 2.2 fusion.4
  393.4 5.0 fusion.8
  398.4 1.4 reshape.122
  399.8 0.8 copy.33
  400.6 0.8 copy.30
  401.4 0.7 copy_bitcast_fusion
  402.1 105.7 %reduce-scatter.5.cloned.1.call-done = bf16[64,4608]{1,0:T(8,128)(2,1)} async-done(((bf16[1024,4608]{1,0:T(8,128)(2,1)}), bf16[64,4608]{1,0:T(8,128)(2,1)}) %reduce-scatter.5.cloned.1.call-update) | async-done | bytes 589840 | tf_op jit(solution)/shard_map/reduce_scatter | solution.py:412
  507.8 1.7 reshape.123
  509.6 0.9 copy.36
  510.5 0.9 copy.35
  511.4 0.9 copy.34
  (66 shorter events, 4.2 us)
Async XLA Ops:
  7.2 4.9 copy-start.9
  7.2 5.2 copy-start.10
  7.2 5.4 %copy-start.11 = (bf16[1536,64]{0,1:T(8,128)(2,1)S(1)}, bf16[1536,64]{0,1:T(8,128)(2,1)}, u32[]{:S(2)}) copy-start(bf16[1536,64]{0,1:T(8,128)(2,1)} %param.23) | copy-start | bytes 589828
  7.2 69.6 %all-gather.3.cloned.1.call-start = ((), (), s32[]{:S(2)}) async-start(), calls=%async_computation.2 | async-start | bytes 6684672 | tf_op jit(solution)/shard_map/all_gather | solution.py:394
  12.1 162.0 %all-gather.5.cloned.1.call-start = ((), (), s32[]{:S(2)}) async-start(), calls=%async_computation.3 | async-start | bytes 10027008 | tf_op jit(solution)/shard_map/all_gather | solution.py:397
  12.6 1.4 copy-start
  12.9 1.4 copy-start.14
  14.0 384.4 %reduce-scatter.3.cloned.1.call-start = ((), (), s32[]{:S(2)}) async-start(), calls=%async_computation.4 | async-start | bytes 6684672 | tf_op jit(solution)/shard_map/reduce_scatter | solution.py:416
  14.6 26.2 %collective-permute-start = (bf16[512,1024]{1,0:T(8,128)(2,1)S(1)}, bf16[512,1024]{1,0:T(8,128)(2,1)S(1)}, u32[]{:S(2)}, u32[]{:S(2)}) collective-permute-start(bf16[512,1024]{1,0:T(8,128)(2,1)S(1)} %fusion.3), channel_id=1, source_target_pairs={{0,1},{1,0},{2,3},{3,2},{4,5},{5,4},{6,7},{7,6},{8,9},{9,8},{10,11... | collective-permute-start | bytes 3145736 | tf_op jit(solution)/shard_map/ppermute | solution.py:384
  76.8 27.0 %copy-start.4 = (bf16[512,1024]{1,0:T(8,128)(2,1)S(1)}, bf16[512,1024]{1,0:T(8,128)(2,1)}, u32[]{:S(2)}) copy-start(bf16[512,1024]{1,0:T(8,128)(2,1)} %param.16) | copy-start | bytes 3145732
  100.8 27.5 %copy-start.1 = (bf16[1024,1024]{1,0:T(8,128)(2,1)S(1)}, bf16[1024,1024]{1,0:T(8,128)(2,1)}, u32[]{:S(2)}) copy-start(bf16[1024,1024]{1,0:T(8,128)(2,1)} %get-tuple-element.23) | copy-start | bytes 6291460
  102.2 26.6 %copy-start.12 = (f32[1024]{0:T(1024)S(1)}, f32[1024]{0:T(1024)}, u32[]{:S(2)}) copy-start(f32[1024]{0:T(1024)} %param.25) | copy-start | bytes 12292
  102.2 26.1 %collective-permute-start.1 = (bf16[512,1024]{1,0:T(8,128)(2,1)S(1)}, bf16[512,1024]{1,0:T(8,128)(2,1)S(1)}, u32[]{:S(2)}, u32[]{:S(2)}) collective-permute-start(bf16[512,1024]{1,0:T(8,128)(2,1)S(1)} %slice.64), channel_id=1, source_target_pairs={{0,1},{1,0},{2,3},{3,2},{4,5},{5,4},{6,7},{7,6},{8,9},{9,8},{10,11... | collective-permute-start | bytes 3145736 | tf_op jit(solution)/shard_map/ppermute | solution.py:389
  103.8 47.0 %collective-permute-start.3 = (bf16[512,1024]{1,0:T(8,128)(2,1)S(1)}, bf16[512,1024]{1,0:T(8,128)(2,1)S(1)}, u32[]{:S(2)}, u32[]{:S(2)}) collective-permute-start(bf16[512,1024]{1,0:T(8,128)(2,1)S(1)} %copy-done.4), channel_id=1, source_target_pairs={{0,1},{1,0},{2,3},{3,2},{4,5},{5,4},{6,7},{7,6},{8,9},{9,8},{10,11... | collective-permute-start | bytes 3145736 | tf_op jit(solution)/shard_map/ppermute | solution.py:384
  129.4 43.2 %collective-permute-start.2 = (bf16[512,1024]{1,0:T(8,128)(2,1)S(1)}, bf16[512,1024]{1,0:T(8,128)(2,1)S(1)}, u32[]{:S(2)}, u32[]{:S(2)}) collective-permute-start(bf16[512,1024]{1,0:T(8,128)(2,1)S(1)} %multiply_convert_fusion), channel_id=1, source_target_pairs={{0,1},{1,0},{2,3},{3,2},{4,5},{5,4},{6,7},{7,6},{8,9},{9,8},{10,11... | collective-permute-start | bytes 3145736 | tf_op jit(solution)/shard_map/ppermute | solution.py:384
  174.0 65.4 %copy-start.13 = (f32[1024]{0:T(1024)S(1)}, f32[1024]{0:T(1024)}, u32[]{:S(2)}) copy-start(f32[1024]{0:T(1024)} %param.25) | copy-start | bytes 12292
  213.4 26.1 %copy-start.2 = (bf16[1024,1024]{1,0:T(8,128)(2,1)S(1)}, bf16[1024,1024]{1,0:T(8,128)(2,1)}, u32[]{:S(2)}) copy-start(bf16[1024,1024]{1,0:T(8,128)(2,1)} %get-tuple-element.23) | copy-start | bytes 6291460
  214.9 26.7 %copy-start.5 = (bf16[512,1024]{1,0:T(8,128)(2,1)S(1)}, bf16[512,1024]{1,0:T(8,128)(2,1)}, u32[]{:S(2)}) copy-start(bf16[512,1024]{1,0:T(8,128)(2,1)} %param.16) | copy-start | bytes 3145732
  214.9 26.7 %copy-start.7 = (bf16[1024,1024]{1,0:T(8,128)(2,1)S(1)}, bf16[1024,1024]{1,0:T(8,128)(2,1)}, u32[]{:S(2)}) copy-start(bf16[1024,1024]{1,0:T(8,128)(2,1)} %get-tuple-element.25) | copy-start | bytes 6291460
  214.9 24.6 %collective-permute-start.5 = (bf16[512,1024]{1,0:T(8,128)(2,1)S(1)}, bf16[512,1024]{1,0:T(8,128)(2,1)S(1)}, u32[]{:S(2)}, u32[]{:S(2)}) collective-permute-start(bf16[512,1024]{1,0:T(8,128)(2,1)S(1)} %slice.68), channel_id=1, source_target_pairs={{0,1},{1,0},{2,3},{3,2},{4,5},{5,4},{6,7},{7,6},{8,9},{9,8},{10,11... | collective-permute-start | bytes 3145736 | tf_op jit(solution)/shard_map/ppermute | solution.py:389
  242.7 23.7 %collective-permute-start.6 = (bf16[512,1024]{1,0:T(8,128)(2,1)S(1)}, bf16[512,1024]{1,0:T(8,128)(2,1)S(1)}, u32[]{:S(2)}, u32[]{:S(2)}) collective-permute-start(bf16[512,1024]{1,0:T(8,128)(2,1)S(1)} %fusion.10), channel_id=1, source_target_pairs={{0,1},{1,0},{2,3},{3,2},{4,5},{5,4},{6,7},{7,6},{8,9},{9,8},{10,11... | collective-permute-start | bytes 3145736 | tf_op jit(solution)/shard_map/ppermute | solution.py:384
  308.0 199.8 %reduce-scatter.5.cloned.1.call-start = ((), (), s32[]{:S(2)}) async-start(), calls=%async_computation.5 | async-start | bytes 10027008 | tf_op jit(solution)/shard_map/reduce_scatter | solution.py:412
  308.6 3.9 copy-start.8
  308.6 6.3 %copy-start.16 = (f32[1,1024]{1,0:T(1,128)S(1)}, f32[1,1024]{1,0:T(1,128)}, u32[]{:S(2)}) copy-start(f32[1,1024]{1,0:T(1,128)} %get-tuple-element.31) | copy-start | bytes 12292
  308.6 6.3 %copy-start.17 = (f32[1,1024]{1,0:T(1,128)S(1)}, f32[1,1024]{1,0:T(1,128)}, u32[]{:S(2)}) copy-start(f32[1,1024]{1,0:T(1,128)} %get-tuple-element.30) | copy-start | bytes 12292
  308.6 82.5 %copy-start.15 = (f32[1024]{0:T(1024)S(1)}, f32[1024]{0:T(1024)}, u32[]{:S(2)}) copy-start(f32[1024]{0:T(1024)} %param.24) | copy-start | bytes 12292
  311.0 80.1 %collective-permute-start.7 = (bf16[512,1024]{1,0:T(8,128)(2,1)}, bf16[512,1024]{1,0:T(8,128)(2,1)}, u32[]{:S(2)}, u32[]{:S(2)}) collective-permute-start(bf16[512,1024]{1,0:T(8,128)(2,1)} %slice.70), channel_id=1, source_target_pairs={{0,1},{1,0},{2,3},{3,2},{4,5},{5,4},{6,7},{7,6},{8,9},{9,8},{10,11... | collective-permute-start | bytes 3145736 | tf_op jit(solution)/shard_map/ppermute | solution.py:389
  313.5 79.8 %collective-permute-start.4 = (bf16[512,1024]{1,0:T(8,128)(2,1)}, bf16[512,1024]{1,0:T(8,128)(2,1)}, u32[]{:S(2)}, u32[]{:S(2)}) collective-permute-start(bf16[512,1024]{1,0:T(8,128)(2,1)} %slice.66), channel_id=1, source_target_pairs={{0,1},{1,0},{2,3},{3,2},{4,5},{5,4},{6,7},{7,6},{8,9},{9,8},{10,11... | collective-permute-start | bytes 3145736 | tf_op jit(solution)/shard_map/ppermute | solution.py:389
  390.0 3.4 copy-start.3
  390.0 3.4 copy-start.6
Sparse Core Ops, SparseCore 0:
  12.2 64.5 all-gather.2
  79.6 80.0 all-gather.4
  308.1 84.4 reduce-scatter.2
  397.1 110.5 reduce-scatter.4

commit v2 on v1

v2 whole, which is shorter than its diff:
```python
import functools

import jax
import jax.numpy as jnp
import numpy as np
from jax import lax
from jax.experimental import pallas as pl
from jax.experimental.pallas import tpu as pltpu
from jax.sharding import PartitionSpec as P

SEQ = 512
EPSILON = 1e-06
THETA = 1000000.0
F32 = jnp.float32
BF16 = jnp.bfloat16
VMEM_LIMIT = 56 * 1024 * 1024


def dot(left, right):
    return lax.dot_general(left, right, (((1,), (0,)), ((), ())), preferred_element_type=F32)


def dot_t(left, right):
    return lax.dot_general(left, right, (((1,), (1,)), ((), ())), preferred_element_type=F32)


def whole(array):
    dims = array.shape
    return pl.BlockSpec(dims, lambda *_: (0,) * len(dims))


def columns(array, count, first=0):
    return pl.BlockSpec((array.shape[0], array.shape[1] // count), lambda j: (0, first + j))


def kernel_call(kernel, name, grid, inputs, outputs, scratch, flops, after=()):
    known = len(inputs)

    def run(*refs):
        kernel(*refs[:known], *refs[known + len(after) :])

    moved = sum(array.size * array.dtype.itemsize for array, _ in inputs)
    return pl.pallas_call(
        run,
        grid=grid,
        in_specs=[spec for _, spec in inputs] + [pl.BlockSpec(memory_space=pl.ANY)] * len(after),
        out_specs=[spec for _, _, spec in outputs],
        out_shape=[jax.ShapeDtypeStruct(shape, dtype) for shape, dtype, _ in outputs],
        scratch_shapes=scratch,
        compiler_params=pltpu.CompilerParams(vmem_limit_bytes=VMEM_LIMIT),
        cost_estimate=pl.CostEstimate(flops=flops, bytes_accessed=moved, transcendentals=0),
        name=name,
    )(*[array for array, _ in inputs], *after)


def rope_tables(width):
    half = width // 2
    places = np.arange(SEQ, dtype=np.float32)
    inverse = (THETA ** (-2.0 * np.arange(half, dtype=np.float32) / width)).astype(np.float32)
    angles = places[:, None] * inverse[None, :]
    cosine = np.concatenate([np.cos(angles), np.cos(angles)], axis=-1)
    sine = np.concatenate([-np.sin(angles), np.sin(angles)], axis=-1)
    return cosine.astype(np.float32), sine.astype(np.float32)


def rope(values, cosine, sine):
    half = values.shape[-1] // 2
    return values * cosine + pltpu.roll(values, half, 1) * sine


def rope_back(values, cosine, sine):
    half = values.shape[-1] // 2
    return values * cosine + pltpu.roll(values * sine, half, 1)


def exponents_t(keys_rot, query_rot, factor):
    scores = dot_t(keys_rot, query_rot)
    key_place = lax.broadcasted_iota(jnp.int32, scores.shape, 0)
    query_place = lax.broadcasted_iota(jnp.int32, scores.shape, 1)
    return jnp.where(key_place <= query_place, jnp.exp2(scores * factor), 0.0)


def attend_kernel(
    group, width, normed_ref, weight_ref, cos_ref, sin_ref, gain_q_ref, gain_k_ref, part_ref, kept_ref, total
):
    step = pl.program_id(0)
    rows = normed_ref.shape[0]
    wide = group * width
    factor = float(width**-0.5 * np.log2(np.e))
    proj = dot(normed_ref[...], weight_ref[:, : wide + 2 * width])
    kept_ref[:, : wide + width] = proj[:, : wide + width].astype(BF16)
    values = proj[:, wide + width :].astype(BF16)
    base = 2 * (wide + width)
    kept_ref[:, base : base + width] = values
    for seq in range(rows // SEQ):
        place = slice(seq * SEQ, (seq + 1) * SEQ)
        rotated = []
        for head in range(group + 1):
            raw = proj[place, head * width : (head + 1) * width]
            scale = lax.rsqrt(jnp.mean(raw * raw, axis=-1, keepdims=True) + EPSILON)
            gain = gain_q_ref[...] if head < group else gain_k_ref[...]
            turned = rope(raw * scale * gain, cos_ref[...], sin_ref[...]).astype(BF16)
            kept_ref[place, wide + width + head * width : wide + width + (head + 1) * width] = turned
            rotated.append(turned)
        values_t = values[place].T
        for head in range(group):
            exponents = exponents_t(rotated[group], rotated[head], factor)
            sums = jnp.sum(exponents, axis=0, keepdims=True)
            out_t = dot(values_t, exponents.astype(BF16)) * (1.0 / sums)
            start = base + width + head * width
            kept_ref[place, start : start + width] = out_t.T.astype(BF16)
    out = dot_t(kept_ref[:, base + width :], weight_ref[:, wide + 2 * width :])

    @pl.when(step == 0)
    def _():
        total[...] = out

    @pl.when(step > 0)
    def _():
        total[...] += out

    @pl.when(step == pl.num_programs(0) - 1)
    def _():
        part_ref[...] = total[...].astype(BF16)


def attend(normed, weights, tables, gain_q, gain_k, heads, group, width, after=()):
    rows, model = normed.shape
    block = weights.shape[1] // heads
    kept = jax.ShapeDtypeStruct((rows, heads * (3 * group + 3) * width), BF16)
    return kernel_call(
        functools.partial(attend_kernel, group, width),
        "attend",
        (heads,),
        [
            (normed, whole(normed)),
            (weights, columns(weights, heads)),
            *[(array, whole(array)) for array in (*tables, gain_q, gain_k)],
        ],
        [(normed.shape, BF16, whole(normed)), (kept.shape, BF16, columns(kept, heads))],
        [pltpu.VMEM((rows, model), F32)],
        heads * (2 * rows * model * block + 4 * rows * SEQ * group * width),
        after,
    )


def turn_kernel(places_ref, source_ref, target_ref):
    model = target_ref.shape[0]
    count = places_ref.shape[0]
    block = model // count
    for index in range(count):
        start = pl.multiple_of(places_ref[index] * block, block)
        target_ref[pl.ds(start, block), :] = source_ref[:, index * block : (index + 1) * block].T


def turn(places, source, after=()):
    target = jax.ShapeDtypeStruct(source.shape[::-1], BF16)
    return kernel_call(
        turn_kernel,
        "turn",
        (1,),
        [(places, pl.BlockSpec(memory_space=pltpu.SMEM)), (source, whole(source))],
        [(target.shape, BF16, whole(target))],
        [],
        0,
        after,
    )[0]


def mlp_kernel(normed_ref, grad_ref, weight_ref, gain_ref, out_ref, dx_ref, kept_ref, dgain_ref, out_total, dx_total):
    step = pl.program_id(0)
    units = weight_ref.shape[1] // 3

    @pl.when(step == 0)
    def _():
        out_total[...] = jnp.zeros_like(out_total)
        dx_total[...] = jnp.zeros_like(dx_total)

    both = dot(normed_ref[...], weight_ref[:, : 2 * units])
    gate, up = both[:, :units], both[:, units:]
    sig = 1.0 / (1.0 + jnp.exp(-gate))
    silu = gate * sig
    hidden = (silu * up).astype(BF16)
    grad_hidden = dot(grad_ref[...], weight_ref[:, 2 * units :])
    grad_gate = (grad_hidden * up * (sig + silu * (1.0 - sig))).astype(BF16)
    grad_up = (grad_hidden * silu).astype(BF16)
    kept_ref[:, :units] = grad_gate
    kept_ref[:, units : 2 * units] = grad_up
    kept_ref[:, 2 * units :] = hidden
    out_total[...] += dot_t(hidden, weight_ref[:, 2 * units :])
    dx_total[...] += dot_t(kept_ref[:, : 2 * units], weight_ref[:, : 2 * units])

    @pl.when(step == pl.num_programs(0) - 1)
    def _():
        out_ref[...] = out_total[...].astype(BF16)
        dx_ref[...] = dx_total[...].astype(BF16)
        dgain_ref[...] = (
            jnp.sum(normed_ref[...].astype(F32) * dx_total[...], axis=0, keepdims=True) / gain_ref[...]
        )


def mlp(normed, grad_rows, weights, gain, steps, after=()):
    rows, model = normed.shape
    kept = jax.ShapeDtypeStruct((rows, weights.shape[1]), BF16)
    return kernel_call(
        mlp_kernel,
        "mlp",
        (steps,),
        [
            (normed, whole(normed)),
            (grad_rows, whole(grad_rows)),
            (weights, columns(weights, steps)),
            (gain, whole(gain)),
        ],
        [
            (normed.shape, BF16, whole(normed)),
            (normed.shape, BF16, whole(normed)),
            (kept.shape, BF16, columns(kept, steps)),
            (gain.shape, F32, whole(gain)),
        ],
        [pltpu.VMEM((rows, model), F32), pltpu.VMEM((rows, model), F32)],
        4 * rows * weights.size,
        after,
    )


def mlp_grads_kernel(parts, *refs):
    normed_t, grad_t, kept = refs[:parts], refs[parts : 2 * parts], refs[2 * parts : 3 * parts]
    units = kept[0].shape[1] // 3
    half = normed_t[0].shape[0] // 2
    for ref, place in zip(refs[3 * parts :], (slice(0, half), slice(half, 2 * half))):
        both = sum(dot(left[place, :], right[:, : 2 * units]) for left, right in zip(normed_t, kept))
        down = sum(dot(left[place, :], right[:, 2 * units :]) for left, right in zip(grad_t, kept))
        ref[:, : 2 * units] = both.astype(BF16)
        ref[:, 2 * units :] = down.astype(BF16)


def mlp_grads(normed_t, grad_t, kept, steps, first, count, after=()):
    model = normed_t[0].shape[0]
    rows = sum(array.shape[0] for array in kept)
    target = jax.ShapeDtypeStruct((model // 2, count * kept[0].shape[1] // steps), BF16)
    return kernel_call(
        functools.partial(mlp_grads_kernel, len(kept)),
        "mlp_grads",
        (count,),
        [(array, whole(array)) for array in (*normed_t, *grad_t)]
        + [(array, columns(array, steps, first)) for array in kept],
        [(target.shape, BF16, columns(target, count))] * 2,
        [],
        4 * rows * target.size,
        after,
    )


def attend_back_kernel(group, width, parts, first, last, *refs):
    refs = iter(refs)
    normed, grad, normed_t, grad_t, kept = [[next(refs) for _ in range(parts)] for _ in range(5)]
    weight_ref, cos_ref, sin_ref, gain_q_ref, gain_k_ref, gain_ref, dgain_before_ref = [next(refs) for _ in range(7)]
    before = [] if first else [next(refs) for _ in range(parts)]
    dx = [next(refs) for _ in range(parts)]
    keep_ref, send_ref, dgain_ref, dgain_heads_ref = [next(refs) for _ in range(4)]
    total, dproj = [[next(refs) for _ in range(parts)] for _ in range(2)]
    step = pl.program_id(0)
    wide = group * width
    scaling = float(width**-0.5)
    factor = float(width**-0.5 * np.log2(np.e))
    rot = wide + width
    base = 2 * rot
    out_columns = slice(wide + 2 * width, None)
    in_columns = slice(0, wide + 2 * width)

    @pl.when(step == 0)
    def _():
        for part in range(parts):
            total[part][...] = jnp.zeros_like(total[part]) if first else before[part][...]
        dgain_heads_ref[...] = dgain_before_ref[...]

    half = normed_t[0].shape[0] // 2
    halves = ((keep_ref, slice(0, half)), (send_ref, slice(half, 2 * half)))
    for ref, rows in halves:
        ref[:, out_columns] = sum(
            dot(left[rows, :], right[:, base + width :]) for left, right in zip(grad_t, kept)
        ).astype(BF16)

    def head_back(part, place, head, cotangent):
        gain = gain_q_ref[...] if head < group else gain_k_ref[...]
        raw = kept[part][place, head * width : (head + 1) * width].astype(F32)
        scale = lax.rsqrt(jnp.mean(raw * raw, axis=-1, keepdims=True) + EPSILON)
        unit = raw * scale
        cot = rope_back(cotangent * scaling, cos_ref[...], sin_ref[...])
        row = 0 if head < group else 1
        dgain_heads_ref[row : row + 1, :] += jnp.sum(cot * unit, axis=0, keepdims=True)
        cot = cot * gain
        result = scale * (cot - unit * jnp.mean(unit * cot, axis=-1, keepdims=True))
        dproj[part][place, head * width : (head + 1) * width] = result.astype(BF16)

    for part in range(parts):
        grad_heads = dot(grad[part][...], weight_ref[:, out_columns]).astype(BF16)
        for seq in range(grad_heads.shape[0] // SEQ):
            place = slice(seq * SEQ, (seq + 1) * SEQ)
            keys_rot = kept[part][place, rot + wide : rot + wide + width]
            keys_t = keys_rot.T
            values = kept[part][place, base : base + width]
            dkeys = jnp.zeros((SEQ, width), F32)
            dvalues = jnp.zeros((SEQ, width), F32)
            for head in range(group):
                query_rot = kept[part][place, rot + head * width : rot + (head + 1) * width]
                grad_head = grad_heads[place, head * width : (head + 1) * width]
                exponents = exponents_t(keys_rot, query_rot, factor)
                probs = exponents * (1.0 / jnp.sum(exponents, axis=0, keepdims=True))
                dprobs = dot_t(values, grad_head)
                inner = jnp.sum(probs * dprobs, axis=0, keepdims=True)
                dscores = (probs * (dprobs - inner)).astype(BF16)
                dvalues += dot(probs.astype(BF16), grad_head)
                dkeys += dot(dscores, query_rot)
                head_back(part, place, head, dot(keys_t, dscores).T)
            head_back(part, place, group, dkeys)
            dproj[part][place, wide + width :] = dvalues.astype(BF16)
        total[part][...] += dot_t(dproj[part][...], weight_ref[:, in_columns])

    for ref, rows in halves:
        ref[:, in_columns] = sum(dot(left[rows, :], right[...]) for left, right in zip(normed_t, dproj)).astype(BF16)

    @pl.when(step == pl.num_programs(0) - 1)
    def _():
        for part in range(parts):
            dx[part][...] = total[part][...].astype(dx[part].dtype)
        if last:
            dgain_ref[...] = (
                sum(
                    jnp.sum(left[...].astype(F32) * right[...], axis=0, keepdims=True)
                    for left, right in zip(normed, total)
                )
                / gain_ref[...]
            )
        else:
            dgain_ref[...] = jnp.zeros_like(dgain_ref)


def attend_back(
    normed, grad, normed_t, grad_t, kept, weights, tables, gains, heads, group, width, first, count, before, after=()
):
    model = weights.shape[0]
    last = first + count == heads
    dx_before, dgain_before = before
    half = jax.ShapeDtypeStruct((model // 2, count * weights.shape[1] // heads), BF16)
    rows = sum(array.shape[0] for array in normed)
    block = weights.shape[1] // heads
    results = kernel_call(
        functools.partial(attend_back_kernel, group, width, len(normed), not dx_before, last),
        "attend_back",
        (count,),
        [(array, whole(array)) for array in (*normed, *grad, *normed_t, *grad_t)]
        + [(array, columns(array, heads, first)) for array in (*kept, weights)]
        + [(array, whole(array)) for array in (*tables, *gains, dgain_before, *dx_before)],
        [(array.shape, BF16 if last else F32, whole(array)) for array in normed]
        + [(half.shape, BF16, columns(half, count))] * 2
        + [(gains[-1].shape, F32, whole(gains[-1])), (dgain_before.shape, F32, whole(dgain_before))],
        [pltpu.VMEM(array.shape, F32) for array in normed]
        + [pltpu.VMEM((array.shape[0], (group + 2) * width), BF16) for array in normed],
        count * (4 * rows * model * block + 10 * rows * SEQ * group * width),
        after,
    )
    parts = len(normed)
    return results[:parts], *results[parts:]


def unit_rows(values):
    scale = lax.rsqrt(jnp.mean(values * values, axis=-1, keepdims=True) + EPSILON)
    return values * scale, scale


def norm_back(unit, scale, cotangent):
    return scale * (cotangent - unit * jnp.mean(unit * cotangent, axis=-1, keepdims=True))


def pack(parts, pieces):
    rows = parts[0].shape[0]
    split = [part.reshape(rows, pieces, part.shape[1] // pieces) for part in parts]
    return jnp.concatenate(split, axis=2).reshape(rows, -1)


def unpack(packed, pieces, widths):
    rows = packed.shape[0]
    split = packed.reshape(rows, pieces, -1).astype(F32)
    ends = np.cumsum([width // pieces for width in widths])
    return [
        split[:, :, end - width // pieces : end].reshape(rows, width) for end, width in zip(ends, widths)
    ]


def relative_places(size):
    relative = jnp.arange(size, dtype=jnp.int32) ^ lax.axis_index("dp")
    layers = size // 4
    return (relative & 1) * (2 * layers) + ((relative >> 1) & 1) * layers + (relative >> 2)


def exchange(array, axis, size, flip):
    return lax.ppermute(array, axis, [(index, index ^ flip) for index in range(size)])


def add(terms):
    total = terms[0].astype(F32)
    for term in terms[1:]:
        total = total + term.astype(F32)
    return total


class BlockSum:
    def __init__(self, size, keep, send):
        self.size = size
        layers = size // 4
        self.flips = [2] + [4 << bit for bit in reversed(range(layers.bit_length() - 1))]
        got = exchange(send, "dp", size, 1)
        shape = (2,) * len(self.flips) + (-1, keep.shape[1])
        self.terms = [keep.reshape(shape), got.reshape(shape)]

    def halve(self, flip):
        axis = self.flips.index(flip)
        self.flips.pop(axis)
        sent = add([lax.index_in_dim(term, 1, axis, keepdims=False) for term in self.terms]).astype(BF16)
        self.terms = [lax.index_in_dim(term, 0, axis, keepdims=False) for term in self.terms]
        self.terms.append(exchange(sent, "dp", self.size, flip))
        return sent

    def finish(self):
        while self.flips:
            self.halve(self.flips[-1])
        return add(self.terms)


def body(
    dp_size,
    tensor_size,
    inputs,
    grad_out,
    w_query,
    key_weight,
    value_weight,
    w_output,
    w_gate,
    w_up,
    w_down,
    gain_attn,
    gain_mlp,
    gain_query,
    gain_keys,
):
    own_rows, model = inputs.shape
    width = gain_query.shape[0]
    heads = key_weight.shape[1] // width
    group = w_query.shape[1] // key_weight.shape[1]
    hidden = w_gate.shape[1]
    steps = max(1, hidden // 256)
    by_pair = tensor_size == 2 and own_rows % SEQ == 0

    def gather_rows(own):
        if by_pair:
            return [own, exchange(own, "tensor", 2, 1)]
        return [lax.all_gather(own, "tensor", axis=0, tiled=True)]

    def sum_rows(parts):
        if by_pair:
            return add([parts[0], exchange(parts[1], "tensor", 2, 1)])
        return lax.psum_scatter(parts[0], "tensor", scatter_dimension=0, tiled=True).astype(F32)

    tables = rope_tables(width)
    gains = gain_query[None, :], gain_keys[None, :], gain_attn[None, :]
    places = relative_places(dp_size)
    attn_weights = lax.all_gather(
        pack([w_query, key_weight, value_weight, w_output.T], heads), "dp", axis=0, tiled=True
    )
    mlp_weights = lax.all_gather(pack([w_gate, w_up, w_down.T], steps), "dp", axis=0, tiled=True)

    inputs_f = inputs.astype(F32)
    unit_in, scale_in = unit_rows(inputs_f)
    normed = gather_rows((unit_in * gain_attn).astype(BF16))
    grad_rows = gather_rows(grad_out)
    normed_t = [turn(places, array) for array in normed]
    grad_t = [turn(places, array) for array in grad_rows]

    parts, kept = [], []
    after = [*normed_t, *grad_t]
    for array in reversed(normed):
        part, held = attend(array, attn_weights, tables, *gains[:2], heads, group, width, after)
        parts.insert(0, part)
        kept.insert(0, held)
        after = [part]
    middle = inputs_f + sum_rows(parts)
    unit_mid, scale_mid = unit_rows(middle)
    normed_mlp = gather_rows((unit_mid * gain_mlp).astype(BF16))

    ffn_parts, dx_parts, kept_mlp, dgain_mlp, after = [], [], [], 0.0, []
    for array, grad in zip(normed_mlp, grad_rows):
        ffn, dx, held, dgain = mlp(array, grad, mlp_weights, gain_mlp[None, :], steps, after)
        ffn_parts.append(ffn)
        dx_parts.append(dx)
        kept_mlp.append(held)
        dgain_mlp = dgain_mlp + dgain[0]
        after = [dx]
    normed_mlp_t = [turn(places, array, after) for array in normed_mlp]
    grad_normed_mlp = sum_rows(dx_parts)
    grad_middle = grad_out.astype(F32) + norm_back(unit_mid, scale_mid, grad_normed_mlp * gain_mlp)
    grad_attended = gather_rows(grad_middle.astype(BF16))
    grad_attended_t = [turn(places, array) for array in grad_attended]

    first = max(1, steps // 2)
    mlp_sums, after = [], []
    for cut in [(0, first), (first, steps - first)] if steps > 1 else [(0, 1)]:
        keep, send = mlp_grads(normed_mlp_t, grad_t, kept_mlp, steps, *cut, after)
        mlp_sums.append(BlockSum(dp_size, keep, send))
        after = [keep]
    x_flip, z_flip = 2, 4
    after = [block_sum.halve(flip) for block_sum, flip in zip(mlp_sums, (x_flip, z_flip))]

    first = max(1, heads // 2)
    before = ((), jnp.zeros((8, width), F32))
    attn_sums = []
    for cut in [(0, first), (first, heads - first)] if heads > 1 else [(0, 1)]:
        dx_parts, keep, send, dgain_attn, dgain_heads = attend_back(
            normed, grad_attended, normed_t, grad_attended_t, kept, attn_weights, tables, gains,
            heads, group, width, *cut, before, after,
        )
        before = (dx_parts, dgain_heads)
        if not attn_sums:
            after = [block_sum.halve(flip) for block_sum, flip in zip(mlp_sums, (z_flip, x_flip))]
        attn_sums.append(BlockSum(dp_size, keep, send))
        after = [*after, attn_sums[-1].halve(x_flip)]

    sums = jnp.concatenate([dgain_attn[0], dgain_mlp, dgain_heads[0], dgain_heads[1]]).reshape(-1, 128)
    for axis, size in (("dp", dp_size), ("tensor", tensor_size)):
        for bit in range(size.bit_length() - 1):
            sums = sums + exchange(sums, axis, size, 1 << bit)
    sums = sums.reshape(-1)

    grad_normed = sum_rows(dx_parts)
    grad_inputs = (grad_middle + norm_back(unit_in, scale_in, grad_normed * gain_attn)).astype(BF16)
    layer_out = (middle + sum_rows(ffn_parts)).astype(BF16)
    mlp_parts = jnp.concatenate([block_sum.finish() for block_sum in mlp_sums], axis=1)
    attn_parts = jnp.concatenate([block_sum.finish() for block_sum in attn_sums], axis=1)
    query_part, keys_part, values_part, output_part = unpack(
        attn_parts, heads, [w_query.shape[1], key_weight.shape[1], value_weight.shape[1], w_output.shape[0]]
    )
    gate_part, up_part, down_part = unpack(mlp_parts, steps, [hidden, hidden, hidden])
    return (
        layer_out,
        grad_inputs,
        query_part,
        keys_part,
        values_part,
        output_part.T,
        gate_part,
        up_part,
        down_part.T,
        sums[:model],
        sums[model : 2 * model],
        sums[2 * model : 2 * model + width],
        sums[2 * model + width :],
    )


def solution(mesh):
    rows = P(("dp", "tensor"), None)
    wide, tall = P("dp", "tensor"), P("tensor", "dp")
    return jax.shard_map(
        functools.partial(body, mesh.shape["dp"], mesh.shape["tensor"]),
        mesh=mesh,
        in_specs=(rows, rows, wide, wide, wide, tall, wide, wide, tall, P(), P(), P(), P()),
        out_specs=(rows, rows, wide, wide, wide, tall, wide, wide, tall, P(), P(), P(), P()),
        check_vma=False,
    )
```

time: 519 us -> 468 us (0.902); the launches traced: 519 us -> 462 us
  waiting for transfers between devices: 273 us -> 190 us
  blocking collectives: 75.1 us -> 0 us
  Pallas kernels: 103 us -> 166 us
  other arithmetic: 18.5 us -> 38.2 us
  starting transfers between devices: 11.9 us -> 28.8 us
    reduce_scatter x2 -> x0, waiting for transfers between devices: 106 us -> none  [the longest x1 106 us: body(): mlp_grads = lax.psum_scatter(dw_mlp, 'dp', scatter_dimension=0, tiled=True)]
    psum x1 -> x0, blocking collectives: 75.1 us -> none  [body(): lax.psum(jnp.concatenate([dgain_attn[0], dgain_mlp[0], dgain_heads[0], dg...]
    pallas_call x3 -> x16, Pallas kernels: 103 us -> 166 us  [kernel_call(): pl.pallas_call(run, grid=grid, in_specs=[spec for _, spec in inputs] + [p...]
    all_gather x1, waiting for transfers between devices: 0.01 us -> 35.7 us  [body(): lax.all_gather(pack([w_gate, w_up, w_down.T], steps), 'dp', axis=0, tiled...]
    all_gather x1, waiting for transfers between devices: 34.4 us -> 10 us  [body(): lax.all_gather(pack([w_query, key_weight, value_weight, w_output.T], head...]
    ppermute x8 -> x29, starting transfers between devices: 11.8 us -> 28.7 us  [exchange(): lax.ppermute(array, axis, [(index, index ^ flip) for index in range(size)])]
    convert_element_type x0 -> x12, other arithmetic: none -> 16.1 us  [halve(): add([lax.index_in_dim(term, 1, axis, keepdims=False) for term in self.ter...]
    ppermute x8 -> x29, waiting for transfers between devices: 132 us -> 144 us  [exchange(): lax.ppermute(array, axis, [(index, index ^ flip) for index in range(size)])]
  transfers between devices with their start and end apart: 12 -> 31, of which waited for: 8 -> 17; matrix products, arithmetic and copies ran while one was open for 5% -> 11% of each run, Pallas kernels for 5% -> 26%
where the time goes in v2:
time: 468 us; the launch traced here: 462 us
  waiting for transfers between devices  190 us (41%)
  Pallas kernels  166 us (35%)
  other arithmetic  38.2 us (8%)
  starting transfers between devices  28.8 us (6%)
  local copies, waits for them, and re-layouts  24.5 us (5%)
  between operations  14.8 us (3%)
    pallas_call x16, Pallas kernels, kernel_call(): pl.pallas_call(run, grid=grid, in_specs=[spec for _, spec in inputs] + [p...  166 us
    ppermute x29, waiting for transfers between devices, exchange(): lax.ppermute(array, axis, [(index, index ^ flip) for index in range(size)])  144 us
    all_gather x1, waiting for transfers between devices, body(): lax.all_gather(pack([w_gate, w_up, w_down.T], steps), 'dp', axis=0, tiled...  35.7 us
    ppermute x29, starting transfers between devices, exchange(): lax.ppermute(array, axis, [(index, index ^ flip) for index in range(size)])  28.7 us
    convert_element_type x12, other arithmetic, halve(): add([lax.index_in_dim(term, 1, axis, keepdims=False) for term in self.ter...  16.1 us
    all_gather x1, waiting for transfers between devices, body(): lax.all_gather(pack([w_query, key_weight, value_weight, w_output.T], head...  10 us
  transfers between devices with their start and end apart: 31, of which 17 were waited for; matrix products, arithmetic and copies ran while one was open for 11% of the time, Pallas kernels for 26%

profile of v2, /device:TPU:0, one launch (start us, length us, event | category | flops | bytes accessed | tf_op | source)
XLA Modules:
  0.0 462.1 jit_solution(8583479505064099298)
XLA Ops:
  14.6 3.0 collective-permute-start
  18.7 3.4 turn.8.refs_6_.refs_4_
  22.1 3.5 turn.10.refs_8_.refs_2_
  25.5 16.2 %collective-permute-done.refs_1_.refs_0_ = bf16[512,1024]{1,0:T(8,128)(2,1)} collective-permute-done((bf16[512,1024]{1,0:T(8,128)(2,1)S(1)}, bf16[512,1024]{1,0:T(8,128)(2,1)}, u32[]{:S(2)}, u32[]{:S(2)}) %collective-permute-start) | collective-permute-done | bytes 1048608 | tf_op jit(solution)/shard_map/ppermute | solution.py:399
  41.7 3.4 turn.9.refs_7_.refs_5_
  45.2 18.2 %collective-permute-done.1.refs_1_ = bf16[512,1024]{1,0:T(8,128)(2,1)} collective-permute-done((bf16[512,1024]{1,0:T(8,128)(2,1)S(1)}, bf16[512,1024]{1,0:T(8,128)(2,1)}, u32[]{:S(2)}, u32[]{:S(2)}) %collective-permute-start.1) | collective-permute-done | bytes 1048608 | tf_op jit(solution)/shard_map/ppermute | solution.py:399
  63.4 3.4 turn.11.refs_9_.refs_3_
  66.8 10.0 %all-gather.3.cloned.1.call-done.refs_1_.refs_10_ = bf16[1024,3072]{1,0:T(8,128)(2,1)} async-done(((bf16[64,3072]{1,0:T(8,128)(2,1)}), bf16[1024,3072]{1,0:T(8,128)(2,1)}) %all-gather.3.cloned.1.call-update) | async-done | bytes 6291472 | tf_op jit(solution)/shard_map/all_gather | solution.py:470
  76.8 16.3 %attend.2 = (bf16[512,1024]{1,0:T(8,128)(2,1)}, bf16[512,4608]{1,0:T(8,128)(2,1)}) custom-call(bf16[512,1024]{1,0:T(8,128)(2,1)} %collective-permute-done.refs_1_.refs_0_, bf16[1024,3072]{1,0:T(8,128)(2,1)} %all-gather.3.cloned.1.call-done.refs_1_.refs_10_, f32[512,128]{1,0:T(8,128)} %constant.29.clone.refs_2_.refs_11_, ...), custom_call_target="tpu_custom_call" | custom-call | flops 4294967296 | bytes 7865344 | tf_op jit(solution)/shard_map/attend/pallas_call | solution.py:43
  94.6 16.1 %attend.3 = (bf16[512,1024]{1,0:T(8,128)(2,1)}, bf16[512,4608]{1,0:T(8,128)(2,1)}) custom-call(bf16[512,1024]{1,0:T(8,128)(2,1)} %copy-done.3, bf16[1024,3072]{1,0:T(8,128)(2,1)} %all-gather.3.cloned.1.call-done.refs_1_.refs_10_, f32[512,128]{1,0:T(8,128)} %constant.29.clone.refs_2_.refs_11_, f32[512,128]{1,0:T(8,128)} %constant.30.clone.refs_3_.refs_12_, ...), custom_call_target="tpu_custom_call" | custom-call | flops 4294967296 | bytes 7865344 | tf_op jit(solution)/shard_map/attend/pallas_call | solution.py:43
  110.7 8.0 %collective-permute-done.2 = bf16[512,1024]{1,0:T(8,128)(2,1)S(1)} collective-permute-done((bf16[512,1024]{1,0:T(8,128)(2,1)}, bf16[512,1024]{1,0:T(8,128)(2,1)S(1)}, u32[]{:S(2)}, u32[]{:S(2)}) %collective-permute-start.2) | collective-permute-done | bytes 1048608 | tf_op jit(solution)/shard_map/ppermute | solution.py:399
  118.7 1.8 multiply_reduce_fusion.1
  123.5 35.7 %all-gather.5.cloned.1.call-done.refs_2_ = bf16[1024,4608]{1,0:T(8,128)(2,1)} async-done(((bf16[64,4608]{1,0:T(8,128)(2,1)}), bf16[1024,4608]{1,0:T(8,128)(2,1)}) %all-gather.5.cloned.1.call-update) | async-done | bytes 9437200 | tf_op jit(solution)/shard_map/all_gather | solution.py:473
  159.1 16.0 %mlp.2 = (bf16[512,1024]{1,0:T(8,128)(2,1)}, bf16[512,1024]{1,0:T(8,128)(2,1)}, bf16[512,4608]{1,0:T(8,128)(2,1)}, f32[1,1024]{1,0:T(1,128)}) custom-call(bf16[512,1024]{1,0:T(8,128)(2,1)} %multiply_convert_fusion.refs_0_.refs_1_, bf16[512,1024]{1,0:T(8,128)(2,1)} %refs_1_.3, bf16[1024,4608]{1,0:T(8,128)(2,1)} %all-gather.5.cloned.1.call-done.refs_2_, ...), custom_call_target="tpu_custom_call" | custom-call | flops 9663676416 | bytes 11538432 | tf_op jit(solution)/shard_map/mlp/pallas_call | solution.py:43
  175.1 16.4 %mlp.3 = (bf16[512,1024]{1,0:T(8,128)(2,1)}, bf16[512,1024]{1,0:T(8,128)(2,1)}, bf16[512,4608]{1,0:T(8,128)(2,1)}, f32[1,1024]{1,0:T(1,128)}) custom-call(bf16[512,1024]{1,0:T(8,128)(2,1)} %collective-permute-done.3.refs_0_.refs_1_, bf16[512,1024]{1,0:T(8,128)(2,1)} %collective-permute-done.1.refs_1_, ...), custom_call_target="tpu_custom_call" | custom-call | flops 9663676416 | bytes 11538432 | tf_op jit(solution)/shard_map/mlp/pallas_call | solution.py:43
  191.5 1.5 collective-permute-start.5
  193.0 3.4 turn.14.refs_0_
  197.0 3.4 turn.15.refs_1_
  200.4 9.2 %mlp_grads.2 = (bf16[512,2304]{1,0:T(8,128)(2,1)}, bf16[512,2304]{1,0:T(8,128)(2,1)}) custom-call(bf16[1024,512]{1,0:T(8,128)(2,1)} %turn.14.refs_0_, bf16[1024,512]{1,0:T(8,128)(2,1)} %turn.15.refs_1_, bf16[1024,512]{1,0:T(8,128)(2,1)} %turn.10.refs_8_.refs_2_, bf16[1024,512]{1,0:T(8,128)(2,1)} %turn.11.refs_9_.refs_3_, ...), custom_call_target="tpu_custom_call" | custom-call | flops 4831838208 | bytes 13631488 | tf_op jit(solution)/shard_map/mlp_grads/pallas_call | solution.py:43
  209.5 9.2 %mlp_grads.3 = (bf16[512,2304]{1,0:T(8,128)(2,1)}, bf16[512,2304]{1,0:T(8,128)(2,1)}) custom-call(bf16[1024,512]{1,0:T(8,128)(2,1)} %turn.14.refs_0_, bf16[1024,512]{1,0:T(8,128)(2,1)} %turn.15.refs_1_, bf16[1024,512]{1,0:T(8,128)(2,1)} %turn.10.refs_8_.refs_2_, bf16[1024,512]{1,0:T(8,128)(2,1)} %turn.11.refs_9_.refs_3_, ...), custom_call_target="tpu_custom_call" | custom-call | flops 4831838208 | bytes 13631488 | tf_op jit(solution)/shard_map/mlp_grads/pallas_call | solution.py:43
  220.1 19.5 %collective-permute-done.4 = bf16[512,1024]{1,0:T(8,128)(2,1)} collective-permute-done((bf16[512,1024]{1,0:T(8,128)(2,1)S(1)}, bf16[512,1024]{1,0:T(8,128)(2,1)}, u32[]{:S(2)}, u32[]{:S(2)}) %collective-permute-start.4) | collective-permute-done | bytes 1048608 | tf_op jit(solution)/shard_map/ppermute | solution.py:399
  239.7 4.4 fusion.24
  245.5 3.4 turn.12.refs_6_
  248.9 19.7 %collective-permute-done.6.refs_1_.refs_3_ = bf16[512,1024]{1,0:T(8,128)(2,1)S(1)} collective-permute-done((bf16[512,1024]{1,0:T(8,128)(2,1)S(1)}, bf16[512,1024]{1,0:T(8,128)(2,1)S(1)}, u32[]{:S(2)}, u32[]{:S(2)}) %collective-permute-start.6) | collective-permute-done | bytes 1048608 | tf_op jit(solution)/shard_map/ppermute | solution.py:399
  269.6 3.4 turn.13.refs_7_
  273.0 1.7 fusion.10.refs_18_
  275.4 2.6 add_convert_fusion.1
  279.1 27.3 %attend_back.2 = (f32[512,1024]{1,0:T(8,128)}, f32[512,1024]{1,0:T(8,128)}, bf16[512,1536]{1,0:T(8,128)(2,1)}, bf16[512,1536]{1,0:T(8,128)(2,1)}, f32[1,1024]{1,0:T(1,128)}, /*index=5*/f32[8,128]{1,0:T(8,128)}) custom-call(bf16[512,1024]{1,0:T(8,128)(2,1)} %copy-done.3, bf16[512,1024]{1,0:T(8,128)(2,1)} %collective-permute-done.refs_1_.refs_0_, ...), custom_call_target="tpu_custom_call" | custom-call | flops 9126805504 | bytes 24650752 | tf_op jit(solution)/shard_map/attend_back/pallas_call | solution.py:43
  308.4 2.4 fusion.11.refs_20_
  310.9 2.1 fusion.12.refs_19_
  315.2 28.3 %attend_back.3 = (bf16[512,1024]{1,0:T(8,128)(2,1)}, bf16[512,1024]{1,0:T(8,128)(2,1)}, bf16[512,1536]{1,0:T(8,128)(2,1)}, bf16[512,1536]{1,0:T(8,128)(2,1)}, f32[1,1024]{1,0:T(1,128)}, /*index=5*/f32[8,128]{1,0:T(8,128)}) custom-call(bf16[512,1024]{1,0:T(8,128)(2,1)} %copy-done.3, bf16[512,1024]{1,0:T(8,128)(2,1)} %collective-permute-done.refs_1_.refs_0_, ...), custom_call_target="tpu_custom_call" | custom-call | flops 9126805504 | bytes 28845056 | tf_op jit(solution)/shard_map/attend_back/pallas_call | solution.py:43
  349.1 1.7 collective-permute-done.25
  352.9 2.3 collective-permute-done.26
  355.1 1.5 collective-permute-start.27
  356.6 3.1 collective-permute-done.27
  363.9 1.6 collective-permute-start.13
  370.4 1.6 collective-permute-start.23
  372.0 2.5 collective-permute-done.20
  375.6 2.4 collective-permute-start.21
  378.0 15.7 %collective-permute-done.23 = bf16[64,2304]{1,0:T(8,128)(2,1)S(1)} collective-permute-done((bf16[64,2304]{1,0:T(8,128)(2,1)S(1)}, bf16[64,2304]{1,0:T(8,128)(2,1)S(1)}, u32[]{:S(2)}, u32[]{:S(2)}) %collective-permute-start.23) | collective-permute-done | bytes 294944 | tf_op jit(solution)/shard_map/ppermute | solution.py:399
  395.0 4.7 %collective-permute-done.21 = bf16[64,2304]{1,0:T(8,128)(2,1)S(1)} collective-permute-done((bf16[64,2304]{1,0:T(8,128)(2,1)S(1)}, bf16[64,2304]{1,0:T(8,128)(2,1)S(1)}, u32[]{:S(2)}, u32[]{:S(2)}) %collective-permute-start.21) | collective-permute-done | bytes 294944 | tf_op jit(solution)/shard_map/ppermute | solution.py:399
  402.0 1.8 reshape.318
  409.8 2.0 fusion.4
  411.8 3.0 fusion.8
  416.1 12.5 %collective-permute-done.17 = bf16[2,2,64,1536]{3,2,1,0:T(8,128)(2,1)S(1)} collective-permute-done((bf16[2,2,64,1536]{3,2,1,0:T(8,128)(2,1)S(1)}, bf16[2,2,64,1536]{3,2,1,0:T(8,128)(2,1)S(1)}, u32[]{:S(2)}, u32[]{:S(2)}) %collective-permute-start.17) | collective-permute-done | bytes 786464 | tf_op jit(solution)/shard_map/ppermute | solution.py:399
  428.8 1.8 collective-permute-start.18
  431.9 11.1 %collective-permute-done.18 = bf16[2,64,1536]{2,1,0:T(8,128)(2,1)S(1)} collective-permute-done((bf16[2,64,1536]{2,1,0:T(8,128)(2,1)S(1)}, bf16[2,64,1536]{2,1,0:T(8,128)(2,1)S(1)}, u32[]{:S(2)}, u32[]{:S(2)}) %collective-permute-start.18) | collective-permute-done | bytes 393248 | tf_op jit(solution)/shard_map/ppermute | solution.py:399
  444.2 7.9 %collective-permute-done.19 = bf16[64,1536]{1,0:T(8,128)(2,1)S(1)} collective-permute-done((bf16[64,1536]{1,0:T(8,128)(2,1)S(1)}, bf16[64,1536]{1,0:T(8,128)(2,1)S(1)}, u32[]{:S(2)}, u32[]{:S(2)}) %collective-permute-start.19) | collective-permute-done | bytes 196640 | tf_op jit(solution)/shard_map/ppermute | solution.py:399
  (166 shorter events, 57.4 us)
Async XLA Ops:
  7.2 4.9 %copy-start.22 = (bf16[64,1536]{1,0:T(8,128)(2,1)S(1)}, bf16[64,1536]{1,0:T(8,128)(2,1)}, u32[]{:S(2)}) copy-start(bf16[64,1536]{1,0:T(8,128)(2,1)} %param.21) | copy-start | bytes 589828
  7.2 5.2 %copy-start.23 = (bf16[64,1536]{1,0:T(8,128)(2,1)S(1)}, bf16[64,1536]{1,0:T(8,128)(2,1)}, u32[]{:S(2)}) copy-start(bf16[64,1536]{1,0:T(8,128)(2,1)} %param.22) | copy-start | bytes 589828
  7.2 5.4 %copy-start.24 = (bf16[1536,64]{0,1:T(8,128)(2,1)S(1)}, bf16[1536,64]{0,1:T(8,128)(2,1)}, u32[]{:S(2)}) copy-start(bf16[1536,64]{0,1:T(8,128)(2,1)} %param.23) | copy-start | bytes 589828
  7.2 69.6 %all-gather.3.cloned.1.call-start = ((), (), s32[]{:S(2)}) async-start(), calls=%async_computation | async-start | bytes 6684672 | tf_op jit(solution)/shard_map/all_gather | solution.py:470
  12.1 147.1 %all-gather.5.cloned.1.call-start = ((), (), s32[]{:S(2)}) async-start(), calls=%async_computation.1 | async-start | bytes 10027008 | tf_op jit(solution)/shard_map/all_gather | solution.py:473
  14.6 27.1 %collective-permute-start = (bf16[512,1024]{1,0:T(8,128)(2,1)S(1)}, bf16[512,1024]{1,0:T(8,128)(2,1)}, u32[]{:S(2)}, u32[]{:S(2)}) collective-permute-start(bf16[512,1024]{1,0:T(8,128)(2,1)S(1)} %fusion.3.refs_1_.refs_0_), channel_id=1, source_target_pairs={{0,1},{1,0},{2,3},{3,2},{4,5},{5,4},{6,7},{7,6},{8,9},{9,8},{10,11... | collective-permute-start | bytes 3145736 | tf_op jit(solution)/shard_map/ppermute | solution.py:399
  17.6 45.7 %collective-permute-start.1 = (bf16[512,1024]{1,0:T(8,128)(2,1)S(1)}, bf16[512,1024]{1,0:T(8,128)(2,1)}, u32[]{:S(2)}, u32[]{:S(2)}) collective-permute-start(bf16[512,1024]{1,0:T(8,128)(2,1)S(1)} %copy-done.6), channel_id=1, source_target_pairs={{0,1},{1,0},{2,3},{3,2},{4,5},{5,4},{6,7},{7,6},{8,9},{9,8},{10,11... | collective-permute-start | bytes 3145736 | tf_op jit(solution)/shard_map/ppermute | solution.py:399
  93.1 25.5 %collective-permute-start.2 = (bf16[512,1024]{1,0:T(8,128)(2,1)}, bf16[512,1024]{1,0:T(8,128)(2,1)S(1)}, u32[]{:S(2)}, u32[]{:S(2)}) collective-permute-start(bf16[512,1024]{1,0:T(8,128)(2,1)} %get-tuple-element.40.refs_6_), channel_id=1, source_target_pairs={{0,1},{1,0},{2,3},{3,2},{4,5},{5,4},{6,7},{7,6},{8,9},{9,8},{10,11... | collective-permute-start | bytes 3145736 | tf_op jit(solution)/shard_map/ppermute | solution.py:399
  110.7 9.8 %copy-start.1 = (bf16[512,1024]{1,0:T(8,128)(2,1)S(1)}, bf16[512,1024]{1,0:T(8,128)(2,1)}, u32[]{:S(2)}) copy-start(bf16[512,1024]{1,0:T(8,128)(2,1)} %get-tuple-element.41) | copy-start | bytes 3145732
  110.7 9.8 %copy-start.25 = (f32[1024]{0:T(1024)S(1)}, f32[1024]{0:T(1024)}, u32[]{:S(2)}) copy-start(f32[1024]{0:T(1024)} %param.25) | copy-start | bytes 12292
  122.0 53.1 %collective-permute-start.3 = (bf16[512,1024]{1,0:T(8,128)(2,1)}, bf16[512,1024]{1,0:T(8,128)(2,1)}, u32[]{:S(2)}, u32[]{:S(2)}) collective-permute-start(bf16[512,1024]{1,0:T(8,128)(2,1)} %multiply_convert_fusion.refs_0_.refs_1_), channel_id=1, source_target_pairs={{0,1},{1,0},{2,3},{3,2},{4,5},{5,4},{6,7},{7,6},{8,9},{9,8},{10,11... | collective-permute-start | bytes 3145736 | tf_op jit(solution)/shard_map/ppermute | solution.py:399
  191.5 4.9 %copy-start.31 = (bf16[512,1024]{1,0:T(8,128)(2,1)S(1)}, bf16[512,1024]{1,0:T(8,128)(2,1)}, u32[]{:S(2)}) copy-start(bf16[512,1024]{1,0:T(8,128)(2,1)} %get-tuple-element.44) | copy-start | bytes 3145732
  191.5 27.8 %collective-permute-start.5 = (bf16[512,1024]{1,0:T(8,128)(2,1)}, bf16[512,1024]{1,0:T(8,128)(2,1)S(1)}, u32[]{:S(2)}, u32[]{:S(2)}) collective-permute-start(bf16[512,1024]{1,0:T(8,128)(2,1)} %get-tuple-element.45.refs_2_), channel_id=1, source_target_pairs={{0,1},{1,0},{2,3},{3,2},{4,5},{5,4},{6,7},{7,6},{8,9},{9,8},{10,11... | collective-permute-start | bytes 3145736 | tf_op jit(solution)/shard_map/ppermute | solution.py:399
  196.4 43.2 %collective-permute-start.4 = (bf16[512,1024]{1,0:T(8,128)(2,1)S(1)}, bf16[512,1024]{1,0:T(8,128)(2,1)}, u32[]{:S(2)}, u32[]{:S(2)}) collective-permute-start(bf16[512,1024]{1,0:T(8,128)(2,1)S(1)} %copy-done.31), channel_id=1, source_target_pairs={{0,1},{1,0},{2,3},{3,2},{4,5},{5,4},{6,7},{7,6},{8,9},{9,8},{10,11... | collective-permute-start | bytes 3145736 | tf_op jit(solution)/shard_map/ppermute | solution.py:399
  209.5 9.7 %copy-start.5 = (bf16[512,1024]{1,0:T(8,128)(2,1)S(1)}, bf16[512,1024]{1,0:T(8,128)(2,1)}, u32[]{:S(2)}) copy-start(bf16[512,1024]{1,0:T(8,128)(2,1)} %get-tuple-element.43.refs_4_) | copy-start | bytes 3145732
  209.5 9.7 %copy-start.26 = (f32[1024]{0:T(1024)S(1)}, f32[1024]{0:T(1024)}, u32[]{:S(2)}) copy-start(f32[1024]{0:T(1024)} %param.25) | copy-start | bytes 12292
  218.7 54.3 %collective-permute-start.8 = (bf16[512,2304]{1,0:T(8,128)(2,1)}, bf16[512,2304]{1,0:T(8,128)(2,1)}, u32[]{:S(2)}, u32[]{:S(2)}) collective-permute-start(bf16[512,2304]{1,0:T(8,128)(2,1)} %get-tuple-element.53), channel_id=1, source_target_pairs={{0,2},{2,0},{4,6},{6,4},{8,10},{10,8},{12,14},{14,12},{16,18},{18,... | collective-permute-start | bytes 7077896 | tf_op jit(solution)/shard_map/ppermute | solution.py:399
  218.7 20.9 %copy-start.7 = (bf16[512,1024]{1,0:T(8,128)(2,1)S(1)}, bf16[512,1024]{1,0:T(8,128)(2,1)}, u32[]{:S(2)}) copy-start(bf16[512,1024]{1,0:T(8,128)(2,1)} %refs_1_.3) | copy-start | bytes 3145732
  218.7 20.9 %copy-start.20 = (bf16[512,1024]{1,0:T(8,128)(2,1)S(1)}, bf16[512,1024]{1,0:T(8,128)(2,1)}, u32[]{:S(2)}) copy-start(bf16[512,1024]{1,0:T(8,128)(2,1)} %get-tuple-element.42) | copy-start | bytes 3145732
  218.7 56.6 %collective-permute-start.7 = (bf16[512,2304]{1,0:T(8,128)(2,1)}, bf16[512,2304]{1,0:T(8,128)(2,1)}, u32[]{:S(2)}, u32[]{:S(2)}) collective-permute-start(bf16[512,2304]{1,0:T(8,128)(2,1)} %get-tuple-element.51), channel_id=1, source_target_pairs={{0,2},{2,0},{4,6},{6,4},{8,10},{10,8},{12,14},{14,12},{16,18},{18,... | collective-permute-start | bytes 7077896 | tf_op jit(solution)/shard_map/ppermute | solution.py:399
  244.0 28.9 %copy-start.12 = (bf16[512,2304]{1,0:T(8,128)(2,1)S(1)}, bf16[512,2304]{1,0:T(8,128)(2,1)}, u32[]{:S(2)}) copy-start(bf16[512,2304]{1,0:T(8,128)(2,1)} %get-tuple-element.52) | copy-start | bytes 7077892
  244.0 24.5 %collective-permute-start.6 = (bf16[512,1024]{1,0:T(8,128)(2,1)S(1)}, bf16[512,1024]{1,0:T(8,128)(2,1)S(1)}, u32[]{:S(2)}, u32[]{:S(2)}) collective-permute-start(bf16[512,1024]{1,0:T(8,128)(2,1)S(1)} %get-tuple-element.67.refs_1_.refs_2_), channel_id=1, source_target_pairs={{0,1},{1,0},{2,3},{3,2},{4,5},{5,4},{6,7},{7,6},{8,9},{9,8},{10,11... | collective-permute-start | bytes 3145736 | tf_op jit(solution)/shard_map/ppermute | solution.py:399
  274.7 4.4 copy-start.18
  274.7 33.8 %collective-permute-start.10 = (bf16[2,2,64,2304]{3,2,1,0:T(8,128)(2,1)S(1)}, bf16[2,2,64,2304]{3,2,1,0:T(8,128)(2,1)}, u32[]{:S(2)}, u32[]{:S(2)}) collective-permute-start(bf16[2,2,64,2304]{3,2,1,0:T(8,128)(2,1)S(1)} %fusion.10.refs_18_), channel_id=1, source_target_pairs={{0,8},{2,10},{4,12},{6,14},{8,0},{10,2},{12,4},{14,6},{16,24},{18,... | collective-permute-start | bytes 3538952 | tf_op jit(solution)/shard_map/ppermute | solution.py:399
  277.9 32.9 %collective-permute-start.9 = (bf16[2,2,64,2304]{3,2,1,0:T(8,128)(2,1)}, bf16[2,2,64,2304]{3,2,1,0:T(8,128)(2,1)}, u32[]{:S(2)}, u32[]{:S(2)}) collective-permute-start(bf16[2,2,64,2304]{3,2,1,0:T(8,128)(2,1)} %bitcast.6.refs_17_), channel_id=1, source_target_pairs={{0,4},{2,6},{4,0},{6,2},{8,12},{10,14},{12,8},{14,10},{16,20},{18,... | collective-permute-start | bytes 3538952 | tf_op jit(solution)/shard_map/ppermute | solution.py:399
  306.4 6.6 %collective-permute-start.11 = (bf16[512,1536]{1,0:T(8,128)(2,1)}, bf16[512,1536]{1,0:T(8,128)(2,1)S(1)}, u32[]{:S(2)}, u32[]{:S(2)}) collective-permute-start(bf16[512,1536]{1,0:T(8,128)(2,1)} %get-tuple-element.58), channel_id=1, source_target_pairs={{0,2},{2,0},{4,6},{6,4},{8,10},{10,8},{12,14},{14,12},{16,18},{18,... | collective-permute-start | bytes 4718600 | tf_op jit(solution)/shard_map/ppermute | solution.py:399
  308.4 5.7 %copy-start.17 = (bf16[512,1536]{1,0:T(8,128)(2,1)S(1)}, bf16[512,1536]{1,0:T(8,128)(2,1)}, u32[]{:S(2)}) copy-start(bf16[512,1536]{1,0:T(8,128)(2,1)} %get-tuple-element.57) | copy-start | bytes 4718596
  315.2 47.2 %copy-start.21 = (bf16[2,64,2304]{2,1,0:T(8,128)(2,1)S(1)}, bf16[2,64,2304]{2,1,0:T(8,128)(2,1)}, u32[]{:S(2)}) copy-start(bf16[2,64,2304]{2,1,0:T(8,128)(2,1)} %fusion.12.refs_19_) | copy-start | bytes 1769476
  343.5 22.0 %copy-start.13 = (bf16[512,1536]{1,0:T(8,128)(2,1)S(1)}, bf16[512,1536]{1,0:T(8,128)(2,1)}, u32[]{:S(2)}) copy-start(bf16[512,1536]{1,0:T(8,128)(2,1)} %get-tuple-element.61) | copy-start | bytes 4718596
  343.5 23.5 %copy-start.16 = (bf16[512,1536]{1,0:T(8,128)(2,1)S(1)}, bf16[512,1536]{1,0:T(8,128)(2,1)}, u32[]{:S(2)}) copy-start(bf16[512,1536]{1,0:T(8,128)(2,1)} %copy-done.15) | copy-start | bytes 4718596
  345.2 1.2 collective-permute-start.24
  347.0 3.7 collective-permute-start.25
  348.5 20.5 %collective-permute-start.22 = (bf16[2,64,2304]{2,1,0:T(8,128)(2,1)}, bf16[2,64,2304]{2,1,0:T(8,128)(2,1)S(1)}, u32[]{:S(2)}, u32[]{:S(2)}) collective-permute-start(bf16[2,64,2304]{2,1,0:T(8,128)(2,1)} %fusion.11.refs_20_), channel_id=1, source_target_pairs={{0,4},{2,6},{4,0},{6,2},{8,12},{10,14},{12,8},{14,10},{16,20},{18,... | collective-permute-start | bytes 1769480 | tf_op jit(solution)/shard_map/ppermute | solution.py:399
  351.4 3.7 collective-permute-start.26
  355.1 4.6 collective-permute-start.27
  359.7 8.2 %collective-permute-start.28 = (f32[18,128]{1,0:T(8,128)S(1)}, f32[18,128]{1,0:T(8,128)S(1)}, u32[]{:S(2)}, u32[]{:S(2)}) collective-permute-start(f32[18,128]{1,0:T(8,128)S(1)} %add.296), channel_id=1, source_target_pairs={{0,1},{1,0},{2,3},{3,2},{4,5},{5,4},{6,7},{7,6},{8,9},{9,8},{10,11... | collective-permute-start | bytes 27656 | tf_op jit(solution)/shard_map/ppermute | solution.py:399
  362.4 12.0 %collective-permute-start.20 = (bf16[2,64,2304]{2,1,0:T(8,128)(2,1)S(1)}, bf16[2,64,2304]{2,1,0:T(8,128)(2,1)S(1)}, u32[]{:S(2)}, u32[]{:S(2)}) collective-permute-start(bf16[2,64,2304]{2,1,0:T(8,128)(2,1)S(1)} %copy-done.21), channel_id=1, source_target_pairs={{0,8},{2,10},{4,12},{6,14},{8,0},{10,2},{12,4},{14,6},{16,24},{18,... | collective-permute-start | bytes 1769480 | tf_op jit(solution)/shard_map/ppermute | solution.py:399
  363.9 42.7 %collective-permute-start.13 = (bf16[2,2,64,1536]{3,2,1,0:T(8,128)(2,1)}, bf16[2,2,64,1536]{3,2,1,0:T(8,128)(2,1)}, u32[]{:S(2)}, u32[]{:S(2)}) collective-permute-start(bf16[2,2,64,1536]{3,2,1,0:T(8,128)(2,1)} %bitcast.15.refs_21_), channel_id=1, source_target_pairs={{0,4},{2,6},{4,0},{6,2},{8,12},{10,14},{12,8},{14,10},{16,20},{18,... | collective-permute-start | bytes 2359304 | tf_op jit(solution)/shard_map/ppermute | solution.py:399
  366.5 43.3 %collective-permute-start.12 = (bf16[512,1024]{1,0:T(8,128)(2,1)}, bf16[512,1024]{1,0:T(8,128)(2,1)}, u32[]{:S(2)}, u32[]{:S(2)}) collective-permute-start(bf16[512,1024]{1,0:T(8,128)(2,1)} %get-tuple-element.60), channel_id=1, source_target_pairs={{0,1},{1,0},{2,3},{3,2},{4,5},{5,4},{6,7},{7,6},{8,9},{9,8},{10,11... | collective-permute-start | bytes 3145736 | tf_op jit(solution)/shard_map/ppermute | solution.py:399
  367.9 40.0 %collective-permute-start.16 = (bf16[512,1536]{1,0:T(8,128)(2,1)}, bf16[512,1536]{1,0:T(8,128)(2,1)}, u32[]{:S(2)}, u32[]{:S(2)}) collective-permute-start(bf16[512,1536]{1,0:T(8,128)(2,1)} %get-tuple-element.62), channel_id=1, source_target_pairs={{0,2},{2,0},{4,6},{6,4},{8,10},{10,8},{12,14},{14,12},{16,18},{18,... | collective-permute-start | bytes 4718600 | tf_op jit(solution)/shard_map/ppermute | solution.py:399
  370.4 23.3 %collective-permute-start.23 = (bf16[64,2304]{1,0:T(8,128)(2,1)S(1)}, bf16[64,2304]{1,0:T(8,128)(2,1)S(1)}, u32[]{:S(2)}, u32[]{:S(2)}) collective-permute-start(bf16[64,2304]{1,0:T(8,128)(2,1)S(1)} %fusion.13), channel_id=1, source_target_pairs={{0,16},{2,18},{4,20},{6,22},{8,24},{10,26},{12,28},{14,30},{16,0},... | collective-permute-start | bytes 884744 | tf_op jit(solution)/shard_map/ppermute | solution.py:399
  375.6 24.1 %collective-permute-start.21 = (bf16[64,2304]{1,0:T(8,128)(2,1)S(1)}, bf16[64,2304]{1,0:T(8,128)(2,1)S(1)}, u32[]{:S(2)}, u32[]{:S(2)}) collective-permute-start(bf16[64,2304]{1,0:T(8,128)(2,1)S(1)} %fusion.15), channel_id=1, source_target_pairs={{0,16},{2,18},{4,20},{6,22},{8,24},{10,26},{12,28},{14,30},{16,0},... | collective-permute-start | bytes 884744 | tf_op jit(solution)/shard_map/ppermute | solution.py:399
  407.8 22.7 %collective-permute-start.14 = (bf16[2,64,1536]{2,1,0:T(8,128)(2,1)S(1)}, bf16[2,64,1536]{2,1,0:T(8,128)(2,1)S(1)}, u32[]{:S(2)}, u32[]{:S(2)}) collective-permute-start(bf16[2,64,1536]{2,1,0:T(8,128)(2,1)S(1)} %fusion.17), channel_id=1, source_target_pairs={{0,8},{2,10},{4,12},{6,14},{8,0},{10,2},{12,4},{14,6},{16,24},{18,... | collective-permute-start | bytes 1179656 | tf_op jit(solution)/shard_map/ppermute | solution.py:399
  409.3 19.3 %collective-permute-start.17 = (bf16[2,2,64,1536]{3,2,1,0:T(8,128)(2,1)S(1)}, bf16[2,2,64,1536]{3,2,1,0:T(8,128)(2,1)S(1)}, u32[]{:S(2)}, u32[]{:S(2)}) collective-permute-start(bf16[2,2,64,1536]{3,2,1,0:T(8,128)(2,1)S(1)} %bitcast.185), channel_id=1, source_target_pairs={{0,4},{2,6},{4,0},{6,2},{8,12},{10,14},{12,8},{14,10},{16,20},{18,... | collective-permute-start | bytes 2359304 | tf_op jit(solution)/shard_map/ppermute | solution.py:399
  411.8 16.8 %copy-start.9 = (bf16[256,1536]{1,0:T(8,128)(2,1)S(1)}, bf16[256,1536]{1,0:T(8,128)(2,1)}, u32[]{:S(2)}) copy-start(bf16[256,1536]{1,0:T(8,128)(2,1)} %slice.334) | copy-start | bytes 2359300
  428.8 14.2 %collective-permute-start.18 = (bf16[2,64,1536]{2,1,0:T(8,128)(2,1)S(1)}, bf16[2,64,1536]{2,1,0:T(8,128)(2,1)S(1)}, u32[]{:S(2)}, u32[]{:S(2)}) collective-permute-start(bf16[2,64,1536]{2,1,0:T(8,128)(2,1)S(1)} %fusion.18), channel_id=1, source_target_pairs={{0,8},{2,10},{4,12},{6,14},{8,0},{10,2},{12,4},{14,6},{16,24},{18,... | collective-permute-start | bytes 1179656 | tf_op jit(solution)/shard_map/ppermute | solution.py:399
  431.6 11.6 %collective-permute-start.15 = (bf16[64,1536]{1,0:T(8,128)(2,1)S(1)}, bf16[64,1536]{1,0:T(8,128)(2,1)S(1)}, u32[]{:S(2)}, u32[]{:S(2)}) collective-permute-start(bf16[64,1536]{1,0:T(8,128)(2,1)S(1)} %fusion.21), channel_id=1, source_target_pairs={{0,16},{2,18},{4,20},{6,22},{8,24},{10,26},{12,28},{14,30},{16,0},... | collective-permute-start | bytes 589832 | tf_op jit(solution)/shard_map/ppermute | solution.py:399
  443.1 9.0 %collective-permute-start.19 = (bf16[64,1536]{1,0:T(8,128)(2,1)S(1)}, bf16[64,1536]{1,0:T(8,128)(2,1)S(1)}, u32[]{:S(2)}, u32[]{:S(2)}) collective-permute-start(bf16[64,1536]{1,0:T(8,128)(2,1)S(1)} %fusion.19), channel_id=1, source_target_pairs={{0,16},{2,18},{4,20},{6,22},{8,24},{10,26},{12,28},{14,30},{16,0},... | collective-permute-start | bytes 589832 | tf_op jit(solution)/shard_map/ppermute | solution.py:399
  (15 other events, 33.5 us)
Sparse Core Ops, SparseCore 0:
  12.2 64.5 all-gather.2
  79.1 80.0 all-gather.4

commit v3 on v2

v3 whole, which is shorter than its diff:
```python
import functools

import jax
import jax.numpy as jnp
import numpy as np
from jax import lax
from jax.experimental import pallas as pl
from jax.experimental.pallas import tpu as pltpu
from jax.sharding import PartitionSpec as P

SEQ = 512
EPSILON = 1e-06
THETA = 1000000.0
F32 = jnp.float32
BF16 = jnp.bfloat16
VMEM_LIMIT = 56 * 1024 * 1024
QUERY_TILE = 256
KEY_TILE = 128


def dot(left, right):
    return lax.dot_general(left, right, (((1,), (0,)), ((), ())), preferred_element_type=F32)


def dot_t(left, right):
    return lax.dot_general(left, right, (((1,), (1,)), ((), ())), preferred_element_type=F32)


def whole(array):
    dims = array.shape
    return pl.BlockSpec(dims, lambda *_: (0,) * len(dims))


def columns(array, count, first=0):
    return pl.BlockSpec((array.shape[0], array.shape[1] // count), lambda j: (0, first + j))


def kernel_call(kernel, name, grid, inputs, outputs, scratch, flops, after=(), into=(), into_index=0):
    after = [*into, *after]
    known = len(inputs)

    def run(*refs):
        kernel(*refs[:known], *refs[known + len(after) :])

    moved = sum(array.size * array.dtype.itemsize for array, _ in inputs)
    return pl.pallas_call(
        run,
        grid=grid,
        in_specs=[spec for _, spec in inputs] + [pl.BlockSpec(memory_space=pl.ANY)] * len(after),
        out_specs=[spec for _, _, spec in outputs],
        out_shape=[jax.ShapeDtypeStruct(shape, dtype) for shape, dtype, _ in outputs],
        scratch_shapes=scratch,
        input_output_aliases={known + index: into_index + index for index in range(len(into))},
        compiler_params=pltpu.CompilerParams(vmem_limit_bytes=VMEM_LIMIT),
        cost_estimate=pl.CostEstimate(flops=64 * flops, bytes_accessed=64 * moved if flops else 1, transcendentals=0),
        name=name,
    )(*[array for array, _ in inputs], *after)


def sync(*arrays):
    spec = pl.BlockSpec(memory_space=pl.ANY)
    return kernel_call(
        lambda *_: None, "sync", (), [], [(array.shape, array.dtype, spec) for array in arrays], [], 0, (), arrays
    )


def rope_tables(width):
    half = width // 2
    places = np.arange(SEQ, dtype=np.float32)
    inverse = (THETA ** (-2.0 * np.arange(half, dtype=np.float32) / width)).astype(np.float32)
    angles = places[:, None] * inverse[None, :]
    cosine = np.concatenate([np.cos(angles), np.cos(angles)], axis=-1)
    sine = np.concatenate([-np.sin(angles), np.sin(angles)], axis=-1)
    return cosine.astype(np.float32), sine.astype(np.float32)


def rope(values, cosine, sine):
    half = values.shape[-1] // 2
    return values * cosine + pltpu.roll(values, half, 1) * sine


def rope_back(values, cosine, sine):
    half = values.shape[-1] // 2
    return values * cosine + pltpu.roll(values * sine, half, 1)


def score_tiles():
    for query in range(0, SEQ, QUERY_TILE):
        for key in range(0, query + QUERY_TILE, KEY_TILE):
            yield slice(key, key + KEY_TILE), slice(query, query + QUERY_TILE)


def exponents_t(keys_rot, query_rot, factor, keys, queries):
    result = jnp.exp2(dot_t(keys_rot, query_rot) * factor)
    if keys.stop - 1 <= queries.start:
        return result
    key_place = lax.broadcasted_iota(jnp.int32, result.shape, 0) + keys.start
    query_place = lax.broadcasted_iota(jnp.int32, result.shape, 1) + queries.start
    return jnp.where(key_place <= query_place, result, 0.0)


def load_weights(cuts, chunks, weight_ref):
    step = pl.program_id(0)
    for index, (first, count) in enumerate(cuts):
        places_ref, *halves = chunks[3 * index : 3 * index + 3]

        @pl.when((step >= first) & (step < first + count))
        def _():
            blocks = places_ref.shape[0]
            block = weight_ref.shape[0] // blocks
            for position in range(blocks):
                half, inner = halves[2 * position // blocks], position % (blocks // 2)
                place = pl.ds(pl.multiple_of(places_ref[position] * block, block), block)
                weight_ref[place, :] = half[inner * block : (inner + 1) * block, :]


def weight_inputs(cuts, chunks):
    inputs = []
    for (first, count), (places, *halves) in zip(cuts, chunks):
        inputs.append((places, pl.BlockSpec(memory_space=pltpu.SMEM)))
        for half in halves:
            spec = pl.BlockSpec(
                (half.shape[0], half.shape[1] // count),
                lambda j, first=first, count=count: (0, jnp.clip(j - first, 0, count - 1)),
            )
            inputs.append((half, spec))
    return inputs


def attend_kernel(group, width, cuts, normed_ref, cos_ref, sin_ref, gain_q_ref, gain_k_ref, *refs):
    chunks, (part_ref, sums_ref, kept_ref, out_ref, total, weight_ref) = refs[: 3 * len(cuts)], refs[3 * len(cuts) :]
    step = pl.program_id(0)
    load_weights(cuts, chunks, weight_ref)
    rows = normed_ref.shape[0]
    wide = group * width
    factor = float(width**-0.5 * np.log2(np.e))
    proj = dot(normed_ref[...], weight_ref[:, : wide + 2 * width])
    kept_ref[:, : wide + width] = proj[:, : wide + width].astype(BF16)
    values = proj[:, wide + width :].astype(BF16)
    kept_ref[:, 2 * (wide + width) :] = values
    for seq in range(rows // SEQ):
        place = slice(seq * SEQ, (seq + 1) * SEQ)
        rotated = []
        for head in range(group + 1):
            raw = proj[place, head * width : (head + 1) * width]
            scale = lax.rsqrt(jnp.mean(raw * raw, axis=-1, keepdims=True) + EPSILON)
            gain = gain_q_ref[...] if head < group else gain_k_ref[...]
            turned = rope(raw * scale * gain, cos_ref[...], sin_ref[...]).astype(BF16)
            kept_ref[place, wide + width + head * width : wide + width + (head + 1) * width] = turned
            rotated.append(turned)
        values_t = values[place].T
        for head in range(group):
            out_t, sums = {}, {}
            for keys, queries in score_tiles():
                exponents = exponents_t(rotated[group][keys], rotated[head][queries], factor, keys, queries)
                start = queries.start
                sums[start] = sums.get(start, 0.0) + jnp.sum(exponents, axis=0, keepdims=True)
                out_t[start] = out_t.get(start, 0.0) + dot(values_t[:, keys], exponents.astype(BF16))
            for start in out_t:
                scale = 1.0 / sums[start]
                spot = slice(seq * SEQ + start, seq * SEQ + start + QUERY_TILE)
                sums_ref[head : head + 1, spot] = scale
                out_ref[spot, head * width : (head + 1) * width] = (out_t[start] * scale).T.astype(BF16)
    out = dot_t(out_ref[...], weight_ref[:, wide + 2 * width :])

    @pl.when(step == 0)
    def _():
        total[...] = out

    @pl.when(step > 0)
    def _():
        total[...] += out

    @pl.when(step == pl.num_programs(0) - 1)
    def _():
        part_ref[...] = total[...].astype(BF16)


def part_rows(rows, width, steps, part, parts):
    return (parts * rows, width), BF16, pl.BlockSpec((rows, width // steps), lambda j: (part, j))


def attend(normed, cuts, chunks, tables, gain_q, gain_k, group, width, part, parts, after=(), into=()):
    rows, model = normed.shape
    heads = sum(count for _, count in cuts)
    block = (2 * group + 2) * width
    return kernel_call(
        functools.partial(attend_kernel, group, width, cuts),
        "attend",
        (heads,),
        [(array, whole(array)) for array in (normed, *tables, gain_q, gain_k)] + weight_inputs(cuts, chunks),
        [
            (normed.shape, BF16, whole(normed)),
            ((8 * heads, rows), F32, pl.BlockSpec((8, rows), lambda j: (j, 0))),
            part_rows(rows, heads * (2 * group + 3) * width, heads, part, parts),
            part_rows(rows, heads * group * width, heads, part, parts),
        ],
        [pltpu.VMEM((rows, model), F32), pltpu.VMEM((model, block), BF16)],
        heads * (2 * rows * model * block + 4 * rows * SEQ * group * width),
        after,
        into,
        2,
    )


def turn_kernel(places_ref, *refs):
    target_ref = refs[-1]
    count = places_ref.shape[0]
    block = target_ref.shape[0] // count
    for index in range(count):
        place = pl.ds(pl.multiple_of(places_ref[index] * block, block), block)
        begin = 0
        for source_ref in refs[:-1]:
            rows = source_ref.shape[0]
            target_ref[place, begin : begin + rows] = source_ref[:, index * block : (index + 1) * block].T
            begin += rows


def turn(places, sources, part, parts, after=(), into=(), flops=0):
    rows, model = sources[0].shape
    width = rows * len(sources)
    return kernel_call(
        turn_kernel,
        "turn",
        (1,),
        [(places, pl.BlockSpec(memory_space=pltpu.SMEM))] + [(source, whole(source)) for source in sources],
        [((model, rows * parts), BF16, pl.BlockSpec((model, width), lambda j: (0, part // len(sources))))],
        [],
        flops,
        after,
        into,
    )


def mlp_kernel(cuts, normed_ref, grad_ref, gain_ref, *refs):
    chunks = refs[: 3 * len(cuts)]
    out_ref, dx_ref, dgain_ref, both_ref, hidden_ref, out_total, dx_total, weight_ref = refs[3 * len(cuts) :]
    step = pl.program_id(0)
    units = weight_ref.shape[1] // 3
    load_weights(cuts, chunks, weight_ref)

    @pl.when(step == 0)
    def _():
        out_total[...] = jnp.zeros_like(out_total)
        dx_total[...] = jnp.zeros_like(dx_total)

    both = dot(normed_ref[...], weight_ref[:, : 2 * units])
    gate, up = both[:, :units], both[:, units:]
    sig = 1.0 / (1.0 + jnp.exp(-gate))
    silu = gate * sig
    hidden = (silu * up).astype(BF16)
    grad_hidden = dot(grad_ref[...], weight_ref[:, 2 * units :])
    both_ref[:, :units] = (grad_hidden * up * (sig + silu * (1.0 - sig))).astype(BF16)
    both_ref[:, units:] = (grad_hidden * silu).astype(BF16)
    hidden_ref[...] = hidden
    out_total[...] += dot_t(hidden, weight_ref[:, 2 * units :])
    dx_total[...] += dot_t(both_ref[...], weight_ref[:, : 2 * units])

    @pl.when(step == pl.num_programs(0) - 1)
    def _():
        out_ref[...] = out_total[...].astype(BF16)
        dx_ref[...] = dx_total[...].astype(BF16)
        dgain_ref[...] = (
            jnp.sum(normed_ref[...].astype(F32) * dx_total[...], axis=0, keepdims=True) / gain_ref[...]
        )


def mlp(normed, grad_rows, gain, cuts, chunks, part, parts, after=(), into=()):
    rows, model = normed.shape
    steps = sum(count for _, count in cuts)
    units = chunks[0][1].shape[1] // cuts[0][1] // 3
    return kernel_call(
        functools.partial(mlp_kernel, cuts),
        "mlp",
        (steps,),
        [(array, whole(array)) for array in (normed, grad_rows, gain)] + weight_inputs(cuts, chunks),
        [
            (normed.shape, BF16, whole(normed)),
            (normed.shape, BF16, whole(normed)),
            (gain.shape, F32, whole(gain)),
            part_rows(rows, steps * 2 * units, steps, part, parts),
            part_rows(rows, steps * units, steps, part, parts),
        ],
        [pltpu.VMEM((rows, model), F32), pltpu.VMEM((rows, model), F32), pltpu.VMEM((model, 3 * units), BF16)],
        12 * rows * model * steps * units,
        after,
        into,
        3,
    )


def weight_grads_kernel(in_t, out_t, into, outof, *halves):
    wide = into.shape[1]
    half = in_t.shape[0] // 2
    *halves, token_ref = halves
    token_ref[...] = jnp.zeros_like(token_ref)
    for ref, place in zip(halves, (slice(0, half), slice(half, 2 * half))):
        ref[:, :wide] = dot(in_t[place, :], into[...]).astype(BF16)
        ref[:, wide:] = dot(out_t[place, :], outof[...]).astype(BF16)


def weight_grads(in_t, out_t, into, outof, steps, first, count, after=(), hides=True):
    model, rows = in_t.shape
    token = jax.ShapeDtypeStruct((8, 128), F32)
    target = jax.ShapeDtypeStruct((model // 2, count * (into.shape[1] + outof.shape[1]) // steps), BF16)
    return kernel_call(
        weight_grads_kernel,
        "weight_grads",
        (count,),
        [(in_t, whole(in_t)), (out_t, whole(out_t))]
        + [(array, columns(array, steps, first)) for array in (into, outof)],
        [(target.shape, BF16, columns(target, count))] * 2 + [(token.shape, F32, whole(token))],
        [],
        4 * rows * target.size if hides else 0,
        after,
    )


def attend_back_kernel(
    group, width, cuts, grad_ref, kept, out_ref, sums_ref, cos_ref, sin_ref, gain_q_ref, gain_k_ref, *refs
):
    chunks = refs[: 3 * len(cuts)]
    dx_ref, dgain_ref, dproj, total, weight_ref = refs[3 * len(cuts) :]
    step = pl.program_id(0)
    load_weights(cuts, chunks, weight_ref)
    wide = group * width
    scaling = float(width**-0.5)
    factor = float(width**-0.5 * np.log2(np.e))
    rot = wide + width
    base = 2 * rot

    @pl.when(step == 0)
    def _():
        total[...] = jnp.zeros_like(total)
        dgain_ref[...] = jnp.zeros_like(dgain_ref)

    def head_back(place, head, cotangent):
        gain = gain_q_ref[...] if head < group else gain_k_ref[...]
        raw = kept[place, head * width : (head + 1) * width].astype(F32)
        scale = lax.rsqrt(jnp.mean(raw * raw, axis=-1, keepdims=True) + EPSILON)
        unit = raw * scale
        cot = rope_back(cotangent * scaling, cos_ref[...], sin_ref[...])
        row = 0 if head < group else 1
        dgain_ref[row : row + 1, :] += jnp.sum(cot * unit, axis=0, keepdims=True)
        cot = cot * gain
        result = scale * (cot - unit * jnp.mean(unit * cot, axis=-1, keepdims=True))
        dproj[place, head * width : (head + 1) * width] = result.astype(BF16)

    grad_heads = dot(grad_ref[...], weight_ref[:, wide + 2 * width :]).astype(BF16)
    for seq in range(grad_heads.shape[0] // SEQ):
        place = slice(seq * SEQ, (seq + 1) * SEQ)
        keys_rot = kept[place, rot + wide : rot + wide + width]
        keys_t = keys_rot.T
        values = kept[place, base : base + width]
        dkeys, dvalues = [{key: 0.0 for key in range(0, SEQ, KEY_TILE)} for _ in range(2)]
        for head in range(group):
            query_rot = kept[place, rot + head * width : rot + (head + 1) * width]
            grad_head = grad_heads[place, head * width : (head + 1) * width]
            weighted = grad_head.astype(F32) * out_ref[place, head * width : (head + 1) * width].astype(F32)
            inner = jnp.sum(weighted.T, axis=0, keepdims=True)
            scale = sums_ref[head : head + 1, place]
            dqueries = {}
            for keys, queries in score_tiles():
                exponents = exponents_t(keys_rot[keys], query_rot[queries], factor, keys, queries)
                probs = exponents * scale[:, queries]
                dprobs = dot_t(values[keys], grad_head[queries])
                dscores = (probs * (dprobs - inner[:, queries])).astype(BF16)
                dvalues[keys.start] += dot(probs.astype(BF16), grad_head[queries])
                dkeys[keys.start] += dot(dscores, query_rot[queries])
                start = queries.start
                dqueries[start] = dqueries.get(start, 0.0) + dot(keys_t[:, keys], dscores)
            head_back(place, head, jnp.concatenate([dqueries[start].T for start in dqueries], axis=0))
        dkeys = jnp.concatenate(list(dkeys.values()), axis=0)
        dvalues = jnp.concatenate(list(dvalues.values()), axis=0)
        head_back(place, group, dkeys)
        dproj[place, wide + width :] = dvalues.astype(BF16)
    total[...] += dot_t(dproj[...], weight_ref[:, : wide + 2 * width])

    @pl.when(step == pl.num_programs(0) - 1)
    def _():
        dx_ref[...] = total[...].astype(BF16)


def attend_back(grad, kept, head_out, sums, cuts, chunks, tables, gain_q, gain_k, group, width, part, parts, after=(), into=()):
    rows, model = grad.shape
    heads = sum(count for _, count in cuts)
    block = (2 * group + 2) * width
    return kernel_call(
        functools.partial(attend_back_kernel, group, width, cuts),
        "attend_back",
        (heads,),
        [
            (grad, whole(grad)),
            (kept, pl.BlockSpec((rows, kept.shape[1] // heads), lambda j: (part, j))),
            (head_out, pl.BlockSpec((rows, head_out.shape[1] // heads), lambda j: (part, j))),
            (sums, pl.BlockSpec((8, rows), lambda j: (j, 0))),
            *[(array, whole(array)) for array in (*tables, gain_q, gain_k)],
            *weight_inputs(cuts, chunks),
        ],
        [
            (grad.shape, BF16, whole(grad)),
            ((8, width), F32, pl.BlockSpec((8, width), lambda j: (0, 0))),
            part_rows(rows, heads * (group + 2) * width, heads, part, parts),
        ],
        [pltpu.VMEM((rows, model), F32), pltpu.VMEM((model, block), BF16)],
        heads * (2 * rows * model * block + 10 * rows * SEQ * group * width),
        after,
        into,
        2,
    )


def unit_rows(values):
    scale = lax.rsqrt(jnp.mean(values * values, axis=-1, keepdims=True) + EPSILON)
    return values * scale, scale


def norm_back(unit, scale, cotangent):
    return scale * (cotangent - unit * jnp.mean(unit * cotangent, axis=-1, keepdims=True))


def pack(parts, pieces):
    rows = parts[0].shape[0]
    split = [part.reshape(rows, pieces, part.shape[1] // pieces) for part in parts]
    return jnp.concatenate(split, axis=2).reshape(rows, -1)


def unpack(packed, pieces, widths):
    rows = packed.shape[0]
    split = packed.reshape(rows, pieces, -1).astype(F32)
    ends = np.cumsum([width // pieces for width in widths])
    return [
        split[:, :, end - width // pieces : end].reshape(rows, width) for end, width in zip(ends, widths)
    ]


def relative_places(size):
    relative = jnp.arange(size, dtype=jnp.int32) ^ lax.axis_index("dp")
    layers = size // 4
    return (relative & 1) * (2 * layers) + ((relative >> 1) & 1) * layers + (relative >> 2)


def exchange(array, axis, size, flip):
    return lax.ppermute(array, axis, [(index, index ^ flip) for index in range(size)])


def z_bits(size):
    return [4 << bit for bit in reversed(range((size // 4).bit_length() - 1))]


class BlockGather:
    def __init__(self, size, block, flips):
        self.size, self.flips = size, list(flips)
        self.held, self.done, self.got = block, 0, None

    def start(self):
        self.got = exchange(self.held, "dp", self.size, self.flips[self.done])
        self.done += 1

    def join(self):
        self.held = jnp.concatenate([self.held, self.got], axis=0)

    def chunk(self):
        position = jnp.arange(self.size, dtype=jnp.int32)
        place = lax.axis_index("dp") ^ sum(
            ((position >> bit) & 1) * flip for bit, flip in enumerate(self.flips)
        )
        return place, self.held, self.got


class BlockSum:
    def __init__(self, size, keep, send, flips):
        self.size, self.flips = size, list(flips)
        self.bits = [2, *z_bits(size)]
        self.left = list(self.bits)
        self.shape = (2,) * len(self.bits) + (-1, keep.shape[1])
        self.terms = [(keep.reshape(self.shape), self.bits)]
        self.got = exchange(send, "dp", size, 1)

    def part(self, flip=None):
        total = 0.0
        for array, bits in self.terms:
            start = [int(bit == flip) for bit in bits] + [0, 0]
            stop = [
                int(bit == flip) + 1 if bit == flip or bit not in self.left else 2 for bit in bits
            ] + list(array.shape[-2:])
            piece = lax.slice(array, start, stop)
            total = total + piece.reshape((2,) * (len(self.left) - (flip is not None)) + piece.shape[-2:]).astype(F32)
        return total

    def take(self):
        if len(self.terms) == 1:
            self.got = self.got.reshape(self.shape)
        self.terms.append((self.got, list(self.left)))

    def halve(self):
        self.take()
        flip = self.flips.pop(0)
        sent = self.part(flip).astype(BF16)
        self.left.remove(flip)
        self.got = exchange(sent, "dp", self.size, flip)
        return sent

    def finish(self):
        self.take()
        return self.part()


def arrive(movers, *others):
    results = sync(*[mover.got for mover in movers], *others)
    for mover, got in zip(movers, results):
        mover.got = got
    return results[len(movers) :]


def body(
    dp_size,
    tensor_size,
    inputs,
    grad_out,
    w_query,
    key_weight,
    value_weight,
    w_output,
    w_gate,
    w_up,
    w_down,
    gain_attn,
    gain_mlp,
    gain_query,
    gain_keys,
):
    own_rows, model = inputs.shape
    width = gain_query.shape[0]
    heads = key_weight.shape[1] // width
    group = w_query.shape[1] // key_weight.shape[1]
    hidden = w_gate.shape[1]
    steps = max(1, hidden // 256)
    by_pair = tensor_size == 2 and own_rows % SEQ == 0
    part_count = 2 if by_pair else 1

    def start_rows(own):
        if by_pair:
            return exchange(own, "tensor", 2, 1)
        return lax.all_gather(own, "tensor", axis=0, tiled=True)

    def all_rows(own, got):
        return [own, got] if by_pair else [got]

    def start_sum(parts):
        if by_pair:
            return exchange(parts[1], "tensor", 2, 1)
        return lax.psum_scatter(parts[0], "tensor", scatter_dimension=0, tiled=True)

    def add_sum(parts, got, base=0.0):
        total = base + got.astype(F32)
        return total + parts[0].astype(F32) if by_pair else total

    tables = rope_tables(width)
    gains = gain_query[None, :], gain_keys[None, :]
    places = relative_places(dp_size)
    z_flips = z_bits(dp_size)
    x_flip, z_flip, z_first = 2, z_flips[-1], z_flips[:-1]

    def gather_start(packed, steps):
        first = max(1, steps // 2)
        cuts = [(0, first), (first, steps - first)] if steps > 1 else [(0, 1)]
        unit = packed.shape[1] // steps
        orders = [*z_first, z_flip, x_flip, 1], [*z_first, x_flip, z_flip, 1]
        return cuts, [
            BlockGather(dp_size, packed[:, start * unit : (start + count) * unit], flips)
            for (start, count), flips in zip(cuts, orders)
        ]

    attn_cuts, attn_gathers = gather_start(pack([w_query, key_weight, value_weight, w_output.T], heads), heads)
    inputs_f = inputs.astype(F32)
    unit_in, scale_in = unit_rows(inputs_f)
    normed_own = (unit_in * gain_attn).astype(BF16)
    for gather in attn_gathers:
        gather.start()
    grad_t = turn(places, [grad_out], 0, part_count) if by_pair else ()
    normed_t = turn(places, [normed_own], 0, part_count) if by_pair else ()
    half = own_rows // 2
    grad_half = start_rows(grad_out[:half]) if by_pair else start_rows(grad_out)
    grad_half, packed, *turned = arrive(
        attn_gathers, grad_half, pack([w_gate, w_up, w_down.T], steps), *grad_t, *normed_t
    )
    grad_t, normed_t = turned[:1], turned[1:]

    mlp_cuts, mlp_gathers = gather_start(packed, steps)
    while attn_gathers[0].done < len(attn_gathers[0].flips) - 2:
        for gather in attn_gathers:
            gather.join()
            gather.start()
        arrive(attn_gathers)
    for gather in attn_gathers:
        gather.join()
        gather.start()
    for gather in mlp_gathers:
        gather.start()
    normed_got = start_rows(normed_own)
    (normed_got,) = arrive([*attn_gathers, *mlp_gathers], normed_got)
    normed = all_rows(normed_own, normed_got)
    for gather in attn_gathers:
        gather.join()
        gather.start()
    arrive(attn_gathers)
    attn_chunks = [gather.chunk() for gather in attn_gathers]

    def grow_mlp():
        sent = []
        if mlp_gathers[0].done < len(mlp_gathers[0].flips):
            for gather in mlp_gathers:
                gather.join()
                gather.start()
                sent.append(gather.held)
        return sent

    parts, row_sums, kept = [None] * part_count, [None] * part_count, ()
    grad_rest = start_rows(grad_out[half:]) if by_pair else None
    for index in reversed(range(part_count)):
        after = grow_mlp()
        parts[index], row_sums[index], *kept = attend(
            normed[index], attn_cuts, attn_chunks, tables, *gains, group, width, index, part_count, after, kept
        )
        if index == part_count - 1:
            if by_pair:
                parts[index], grad_rest = arrive(mlp_gathers, parts[index], grad_rest)
            else:
                (parts[index],) = arrive(mlp_gathers, parts[index])
            part_got = start_sum(parts)
    parts[0], part_got = arrive(mlp_gathers, parts[0], part_got)
    kept, head_out = kept
    while mlp_gathers[0].done < len(mlp_gathers[0].flips):
        grow_mlp()
        arrive(mlp_gathers)
    mlp_chunks = [gather.chunk() for gather in mlp_gathers]
    grad_rows = [grad_out, jnp.concatenate([grad_half, grad_rest], axis=0)] if by_pair else [grad_half]
    middle = add_sum(parts, part_got, inputs_f)
    unit_mid, scale_mid = unit_rows(middle)
    normed_own = (unit_mid * gain_mlp).astype(BF16)
    normed_got = start_rows(normed_own)

    def run_mlp(index, array, after, into):
        return mlp(
            array, grad_rows[index], gain_mlp[None, :], mlp_cuts, mlp_chunks, index, part_count, after, into
        )

    if by_pair:
        ffn, dx, dgain, *kept_mlp = run_mlp(0, normed_own, [normed_own], ())
        grad_t = turn(places, grad_rows[1:], 1, part_count, [dx], grad_t)
        normed_t = turn(places, normed[1:], 1, part_count, grad_t, normed_t)
        dx, normed_got, *turned = sync(dx, normed_got, *grad_t, *normed_t)
        grad_t, normed_t = turned[:1], turned[1:]
        ffn_parts, dx_parts, dgain_mlp = [ffn], [dx], dgain[0]
        ffn, dx, dgain, *kept_mlp = run_mlp(1, normed_got, [dx], kept_mlp)
        ffn_parts.append(ffn)
        dx_parts.append(dx)
        dgain_mlp = dgain_mlp + dgain[0]
        after = [dx]
    else:
        grad_t = turn(places, grad_rows, 0, 1)
        normed_t = turn(places, normed, 0, 1)
        ffn, dx, dgain, *kept_mlp = run_mlp(0, normed_got, (), ())
        ffn_parts, dx_parts, dgain_mlp = [ffn], [dx], dgain[0]
        after = [dx]
    normed_mlp_t = turn(places, all_rows(normed_own, normed_got), 0, part_count, after, flops=10**9)

    dx_got = start_sum(dx_parts)
    orders = [x_flip, z_flip, *z_first], [z_flip, x_flip, *z_first]

    def mlp_weight_grads(index, after):
        keep, send, token = weight_grads(
            *normed_mlp_t, *grad_t, *kept_mlp, steps, *mlp_cuts[index], after, index > 0
        )
        return token, BlockSum(dp_size, keep, send, orders[index])

    keep, block_sum = mlp_weight_grads(0, after)
    mlp_sums = [block_sum]
    keep, dx_got = sync(keep, dx_got)
    grad_middle = grad_out.astype(F32) + norm_back(unit_mid, scale_mid, add_sum(dx_parts, dx_got) * gain_mlp)
    attended_own = grad_middle.astype(BF16)
    attended_got = start_rows(attended_own)
    after = [attended_own]
    if len(mlp_cuts) > 1:
        keep, block_sum = mlp_weight_grads(1, after)
        mlp_sums.append(block_sum)
        after = [keep]
    attended_t = turn(places, [attended_own], 0, part_count, after) if by_pair else ()
    keep, *attended_t = arrive(mlp_sums, keep, *attended_t)
    after = [keep, *attended_t, *[block_sum.halve() for block_sum in mlp_sums]]

    dx_parts, dproj, dgain_heads = [], (), 0.0
    if not by_pair:
        (attended_got,) = sync(attended_got)
    for index in range(part_count):
        grad = attended_own if by_pair and index == 0 else attended_got
        dx, dgain, *dproj = attend_back(
            grad, kept, head_out, row_sums[index], attn_cuts, attn_chunks, tables, *gains, group, width, index, part_count, after, dproj
        )
        dgain_heads = dgain_heads + dgain
        if by_pair and index == 0:
            dx, attended_got, ffn_parts[1] = arrive(mlp_sums, dx, attended_got, ffn_parts[1])
            ffn_first = start_rows(ffn_parts[1][:half])
        elif by_pair:
            dx, ffn_first = arrive(mlp_sums, dx, ffn_first)
            ffn_rest = start_rows(ffn_parts[1][half:])
        else:
            (dx,) = arrive(mlp_sums, dx)
            ffn_rest = start_sum(ffn_parts)
        dx_parts.append(dx)
        after = [block_sum.halve() for block_sum in mlp_sums]
    dx_got = start_sum(dx_parts)
    if by_pair:
        attended_t = turn(places, [attended_got], 1, part_count, after, attended_t, 10**9)
    else:
        attended_t = turn(places, [attended_got], 0, 1, after)
    dgain_attn = sum(
        jnp.sum(array.astype(F32) * dx.astype(F32), axis=0) for array, dx in zip(normed, dx_parts)
    ) / gain_attn
    sums = jnp.concatenate([dgain_attn, dgain_mlp, dgain_heads[0], dgain_heads[1]]).reshape(-1, 128)
    hops = [("dp", dp_size, 1 << bit) for bit in range(dp_size.bit_length() - 1)]
    hops += [("tensor", tensor_size, 1 << bit) for bit in range(tensor_size.bit_length() - 1)]
    attn_sums, after = [], [*after, sums]
    for index, cut in enumerate(attn_cuts):
        sums_got = exchange(sums, *hops.pop(0))
        keep, send, token = weight_grads(*normed_t, *attended_t, *dproj, head_out, heads, *cut, after, index > 0)
        attn_sums.append(BlockSum(dp_size, keep, send, orders[index]))
        token, sums_got, ffn_rest = arrive(mlp_sums[index : index + 1], token, sums_got, ffn_rest)
        sums = sums + sums_got
        after = [token, sums]
    ffn_got = jnp.concatenate([ffn_first, ffn_rest], axis=0) if by_pair else ffn_rest

    sums_got = exchange(sums, *hops.pop(0))
    (sums_got,) = arrive(attn_sums, sums_got)
    sums = sums + sums_got
    sent = [block_sum.halve() for block_sum in attn_sums]
    sums_got = exchange(sums, *hops.pop(0))
    (sums_got,) = arrive(attn_sums, sums_got)
    sums = sums + sums_got
    sent = [block_sum.halve() for block_sum in attn_sums]
    dx_got, *_ = sync(dx_got, *sent)
    grad_normed = add_sum(dx_parts, dx_got)
    grad_inputs = (grad_middle + norm_back(unit_in, scale_in, grad_normed * gain_attn)).astype(BF16)
    grad_inputs, sums = arrive(attn_sums, grad_inputs, sums)
    while any(block_sum.flips for block_sum in attn_sums):
        for block_sum in attn_sums:
            block_sum.halve()
    for hop in hops:
        sums = sums + exchange(sums, *hop)
    sums = sums.reshape(-1)
    layer_out = add_sum(ffn_parts, ffn_got, middle).astype(BF16)
    while any(block_sum.flips for block_sum in mlp_sums):
        for block_sum in mlp_sums:
            block_sum.halve()
    mlp_parts = jnp.concatenate([block_sum.finish() for block_sum in mlp_sums], axis=1)
    attn_parts = jnp.concatenate([block_sum.finish() for block_sum in attn_sums], axis=1)
    query_part, keys_part, values_part, output_part = unpack(
        attn_parts, heads, [w_query.shape[1], key_weight.shape[1], value_weight.shape[1], w_output.shape[0]]
    )
    gate_part, up_part, down_part = unpack(mlp_parts, steps, [hidden, hidden, hidden])
    return (
        layer_out,
        grad_inputs,
        query_part,
        keys_part,
        values_part,
        output_part.T,
        gate_part,
        up_part,
        down_part.T,
        sums[:model],
        sums[model : 2 * model],
        sums[2 * model : 2 * model + width],
        sums[2 * model + width :],
    )


def solution(mesh):
    rows = P(("dp", "tensor"), None)
    wide, tall = P("dp", "tensor"), P("tensor", "dp")
    return jax.shard_map(
        functools.partial(body, mesh.shape["dp"], mesh.shape["tensor"]),
        mesh=mesh,
        in_specs=(rows, rows, wide, wide, wide, tall, wide, wide, tall, P(), P(), P(), P()),
        out_specs=(rows, rows, wide, wide, wide, tall, wide, wide, tall, P(), P(), P(), P()),
        check_vma=False,
    )
```

time: 468 us -> 442 us (0.944)
  waiting for transfers between devices: 190 us -> 103 us
  other arithmetic: 38.2 us -> 70.1 us
  starting transfers between devices: 28.8 us -> 48.5 us
  local copies, waits for them, and re-layouts: 24.5 us -> 41.4 us
  between operations: 14.8 us -> 2.23 us
    all_gather x2 -> x0, waiting for transfers between devices: 45.7 us -> none  [the longest x1 35.7 us: body(): lax.all_gather(pack([w_gate, w_up, w_down.T], steps), 'dp', axis=0, tiled...]
    ppermute x29 -> x47, waiting for transfers between devices: 144 us -> 103 us  [exchange(): lax.ppermute(array, axis, [(index, index ^ flip) for index in range(size)])]
    ppermute x29 -> x47, starting transfers between devices: 28.7 us -> 48.5 us  [exchange(): lax.ppermute(array, axis, [(index, index ^ flip) for index in range(size)])]
    concatenate x0 -> x12, other arithmetic: none -> 15.7 us  [join(): self.held = jnp.concatenate([self.held, self.got], axis=0)]
    unnamed x71 -> x220, local copies, waits for them, and re-layouts: 8.65 us -> 23.9 us
    convert_element_type x15, other arithmetic: 22.3 us -> 27.3 us  [the longest x12 19.3 us: halve(): sent = self.part(flip).astype(BF16)]
    pallas_call x16 -> x35, Pallas kernels: 166 us -> 170 us  [kernel_call(): pl.pallas_call(run, grid=grid, in_specs=[spec for _, spec in inputs] + [p...]
  transfers between devices with their start and end apart: 31 -> 47, of which waited for: 17 -> 20; matrix products, arithmetic and copies ran while one was open for 11% -> 16% of each run, Pallas kernels for 26% -> 35%
where the time goes in v3:
time: 442 us; the launch traced here: 436 us
  Pallas kernels  170 us (38%)
  waiting for transfers between devices  103 us (23%)
  other arithmetic  70.1 us (16%)
  starting transfers between devices  48.5 us (11%)
  local copies, waits for them, and re-layouts  41.4 us (9%)
    pallas_call x35, Pallas kernels, kernel_call(): pl.pallas_call(run, grid=grid, in_specs=[spec for _, spec in inputs] + [p...  170 us
    ppermute x47, waiting for transfers between devices, exchange(): lax.ppermute(array, axis, [(index, index ^ flip) for index in range(size)])  103 us
    ppermute x47, starting transfers between devices, exchange(): lax.ppermute(array, axis, [(index, index ^ flip) for index in range(size)])  48.5 us
    unnamed x220, local copies, waits for them, and re-layouts  23.9 us
    convert_element_type x12, other arithmetic, halve(): sent = self.part(flip).astype(BF16)  19.3 us
    concatenate x12, other arithmetic, join(): self.held = jnp.concatenate([self.held, self.got], axis=0)  15.7 us
  transfers between devices with their start and end apart: 47, of which 20 were waited for; matrix products, arithmetic and copies ran while one was open for 16% of the time, Pallas kernels for 35%

profile of v3, /device:TPU:0, one launch (start us, length us, event | category | flops | bytes accessed | tf_op | source)
XLA Modules:
  0.0 435.7 jit_solution(2610177647937983495)
XLA Ops:
  4.7 4.1 collective-permute-start.1
  19.5 3.5 turn.7.refs_4_
  24.3 3.4 turn.8.refs_5_
  34.4 6.5 %collective-permute-done.4.refs_1_ = bf16[128,1536]{1,0:T(8,128)(2,1)S(1)} collective-permute-done((bf16[128,1536]{1,0:T(8,128)(2,1)S(1)}, bf16[128,1536]{1,0:T(8,128)(2,1)S(1)}, u32[]{:S(2)}, u32[]{:S(2)}) %collective-permute-start.4) | collective-permute-done | bytes 393248 | tf_op jit(solution)/shard_map/ppermute | solution.py:444
  47.6 2.6 collective-permute-start.8
  50.6 20.2 %collective-permute-done.8.refs_3_ = bf16[64,2304]{1,0:T(8,128)(2,1)S(1)} collective-permute-done((bf16[64,2304]{1,0:T(8,128)(2,1)S(1)}, bf16[64,2304]{1,0:T(8,128)(2,1)S(1)}, u32[]{:S(2)}, u32[]{:S(2)}) %collective-permute-start.8) | collective-permute-done | bytes 294944 | tf_op jit(solution)/shard_map/ppermute | solution.py:444
  70.8 3.1 collective-permute-done.7.refs_2_
  83.0 4.0 collective-permute-start.10
  88.2 17.0 %attend.2 = (bf16[512,1024]{1,0:T(8,128)(2,1)}, f32[32,512]{1,0:T(8,128)}, bf16[1024,3584]{1,0:T(8,128)(2,1)}, bf16[1024,1024]{1,0:T(8,128)(2,1)}) custom-call(bf16[512,1024]{1,0:T(8,128)(2,1)} %get-tuple-element.117.refs_0_.refs_1_, f32[512,128]{1,0:T(8,128)} %constant.32.clone.refs_1_.refs_4_, f32[512,128]{1,0:T(8,128)} %constant.33.clone.refs_2_.refs_5_, ...), custom_call_target="tpu_custom_call" | custom-call | flops 274877906944 | bytes 503390208 | tf_op jit(solution)/shard_map/attend/pallas_call | solution.py:46
  106.2 2.2 pad_maximum_fusion.4.refs_13_
  108.4 2.2 pad_maximum_fusion.5.refs_14_
  111.7 16.4 %attend.3 = (bf16[512,1024]{1,0:T(8,128)(2,1)}, f32[32,512]{1,0:T(8,128)}, bf16[1024,3584]{1,0:T(8,128)(2,1)}, bf16[1024,1024]{1,0:T(8,128)(2,1)}) custom-call(bf16[512,1024]{1,0:T(8,128)(2,1)} %fusion.5.refs_1_.refs_0_, f32[512,128]{1,0:T(8,128)} %constant.32.clone.refs_1_.refs_4_, ...), custom_call_target="tpu_custom_call", output_to_operand_aliasing={{2}: (11, {}), {3}: (12, {})} | custom-call | flops 274877906944 | bytes 503390208 | tf_op jit(solution)/shard_map/attend/pallas_call | solution.py:46
  129.9 8.1 %collective-permute-done.16.refs_1_ = bf16[256,2304]{1,0:T(8,128)(2,1)} collective-permute-done((bf16[256,2304]{1,0:T(8,128)(2,1)}, bf16[256,2304]{1,0:T(8,128)(2,1)}, u32[]{:S(2)}, u32[]{:S(2)}) %collective-permute-start.16) | collective-permute-done | bytes 1179680 | tf_op jit(solution)/shard_map/ppermute | solution.py:444
  140.9 2.4 pad_maximum_fusion.1.refs_7_
  144.8 2.1 constant_dynamic-update-slice_fusion.refs_1_
  148.7 2.7 multiply_convert_fusion.refs_0_.refs_9_.refs_1_
  154.0 17.9 %mlp.2 = (bf16[512,1024]{1,0:T(8,128)(2,1)}, bf16[512,1024]{1,0:T(8,128)(2,1)}, f32[1,1024]{1,0:T(1,128)}, bf16[1024,3072]{1,0:T(8,128)(2,1)}, bf16[1024,1536]{1,0:T(8,128)(2,1)}) custom-call(bf16[512,1024]{1,0:T(8,128)(2,1)} %multiply_convert_fusion.refs_0_.refs_9_.refs_1_, bf16[512,1024]{1,0:T(8,128)(2,1)} %refs_1_.5, f32[1,1024]{1,0:T(1,128)} %bitcast.222, ...), custom_call_target="tpu_custom_call" | custom-call | flops 618475290624 | bytes 738467840 | tf_op jit(solution)/shard_map/mlp/pallas_call | solution.py:46
  171.9 3.5 turn.9.refs_3_.refs_2_
  175.3 3.4 turn.10.refs_3_
  178.8 17.7 %mlp.3 = (bf16[512,1024]{1,0:T(8,128)(2,1)}, bf16[512,1024]{1,0:T(8,128)(2,1)}, f32[1,1024]{1,0:T(1,128)}, bf16[1024,3072]{1,0:T(8,128)(2,1)}, bf16[1024,1536]{1,0:T(8,128)(2,1)}) custom-call(bf16[512,1024]{1,0:T(8,128)(2,1)} %get-tuple-element.140.refs_0_.refs_2_, ...), custom_call_target="tpu_custom_call", output_to_operand_aliasing={{3}: (9, {}), {4}: (10, {})} | custom-call | flops 618475290624 | bytes 738467840 | tf_op jit(solution)/shard_map/mlp/pallas_call | solution.py:46
  197.4 5.2 %turn.11.refs_0_ = bf16[1024,1024]{1,0:T(8,128)(2,1)} custom-call(s32[16]{0:T(128)} %shift-right-arithmetic_add_fusion.refs_0_, bf16[512,1024]{1,0:T(8,128)(2,1)} %multiply_convert_fusion.refs_0_.refs_9_.refs_1_, bf16[512,1024]{1,0:T(8,128)(2,1)} %get-tuple-element.140.refs_0_.refs_2_, bf16[512,1024]{1,0:T(8,128)(2,1)} %get-tuple-element.144.refs_3_.refs_4_), custom_call_target="tpu_custom_call" | custom-call | flops 64000000000 | bytes 134221824 | tf_op jit(solution)/shard_map/turn/pallas_call | solution.py:46
  202.6 9.2 %weight_grads.4 = (bf16[512,2304]{1,0:T(8,128)(2,1)}, bf16[512,2304]{1,0:T(8,128)(2,1)}, f32[8,128]{1,0:T(8,128)}) custom-call(bf16[1024,1024]{1,0:T(8,128)(2,1)} %turn.11.refs_0_, bf16[1024,1024]{1,0:T(8,128)(2,1)} %get-tuple-element.145.refs_1_, bf16[1024,3072]{1,0:T(8,128)(2,1)} %get-tuple-element.146.refs_2_, ...), custom_call_target="tpu_custom_call" | custom-call | bytes 1 | tf_op jit(solution)/shard_map/weight_grads/pallas_call | solution.py:46
  211.9 9.6 %collective-permute-done.22.refs_1_ = bf16[512,1024]{1,0:T(8,128)(2,1)S(1)} collective-permute-done((bf16[512,1024]{1,0:T(8,128)(2,1)}, bf16[512,1024]{1,0:T(8,128)(2,1)S(1)}, u32[]{:S(2)}, u32[]{:S(2)}) %collective-permute-start.22) | collective-permute-done | bytes 1048608 | tf_op jit(solution)/shard_map/ppermute | solution.py:444
  222.4 2.6 multiply_reduce_fusion.1
  225.1 4.0 fusion.33
  229.1 9.4 %weight_grads.5 = (bf16[512,2304]{1,0:T(8,128)(2,1)}, bf16[512,2304]{1,0:T(8,128)(2,1)}, f32[8,128]{1,0:T(8,128)}) custom-call(bf16[1024,1024]{1,0:T(8,128)(2,1)} %turn.11.refs_0_, bf16[1024,1024]{1,0:T(8,128)(2,1)} %get-tuple-element.145.refs_1_, bf16[1024,3072]{1,0:T(8,128)(2,1)} %get-tuple-element.146.refs_2_, ...), custom_call_target="tpu_custom_call" | custom-call | flops 309237645312 | bytes 872415232 | tf_op jit(solution)/shard_map/weight_grads/pallas_call | solution.py:46
  240.0 3.5 turn.12.refs_3_
  246.0 3.0 add_convert_fusion.1
  252.7 20.7 %attend_back.2 = (bf16[512,1024]{1,0:T(8,128)(2,1)}, f32[8,128]{1,0:T(8,128)}, bf16[1024,2048]{1,0:T(8,128)(2,1)}) custom-call(bf16[512,1024]{1,0:T(8,128)(2,1)} %get-tuple-element.207.refs_4_.refs_1_.refs_0_, bf16[1024,3584]{1,0:T(8,128)(2,1)} %get-tuple-element.157.refs_1_, bf16[1024,1024]{1,0:T(8,128)(2,1)} %get-tuple-element.158.refs_2_.refs_3_, ...), custom_call_target="tpu_custom_call" | custom-call | flops 377957122048 | bytes 1111564288 | tf_op jit(solution)/shard_map/attend_back/pallas_call | solution.py:46
  273.4 4.1 collective-permute-done.24.refs_0_
  277.4 2.4 collective-permute-done.25.refs_1_
  279.8 2.3 fusion.35
  284.1 2.5 fusion.14.refs_16_
  287.3 2.5 fusion.15.refs_15_
  291.3 21.0 %attend_back.3 = (bf16[512,1024]{1,0:T(8,128)(2,1)}, f32[8,128]{1,0:T(8,128)}, bf16[1024,2048]{1,0:T(8,128)(2,1)}) custom-call(bf16[512,1024]{1,0:T(8,128)(2,1)} %get-tuple-element.166.refs_0_.refs_1_, bf16[1024,3584]{1,0:T(8,128)(2,1)} %get-tuple-element.157.refs_1_, ...), custom_call_target="tpu_custom_call", output_to_operand_aliasing={{2}: (14, {})} | custom-call | flops 377957122048 | bytes 1111564288 | tf_op jit(solution)/shard_map/attend_back/pallas_call | solution.py:46
  320.9 3.5 turn.13.refs_1_
  324.4 7.3 %weight_grads.6 = (bf16[512,1536]{1,0:T(8,128)(2,1)}, bf16[512,1536]{1,0:T(8,128)(2,1)}, f32[8,128]{1,0:T(8,128)}) custom-call(bf16[1024,1024]{1,0:T(8,128)(2,1)} %get-tuple-element.173.refs_0_, bf16[1024,1024]{1,0:T(8,128)(2,1)} %turn.13.refs_1_, bf16[1024,2048]{1,0:T(8,128)(2,1)} %get-tuple-element.175.refs_2_, ...), custom_call_target="tpu_custom_call" | custom-call | bytes 1 | tf_op jit(solution)/shard_map/weight_grads/pallas_call | solution.py:46
  331.9 4.2 collective-permute-done.31.refs_0_
  338.2 7.5 %weight_grads.7 = (bf16[512,1536]{1,0:T(8,128)(2,1)}, bf16[512,1536]{1,0:T(8,128)(2,1)}, f32[8,128]{1,0:T(8,128)}) custom-call(bf16[1024,1024]{1,0:T(8,128)(2,1)} %get-tuple-element.173.refs_0_, bf16[1024,1024]{1,0:T(8,128)(2,1)} %turn.13.refs_1_, bf16[1024,2048]{1,0:T(8,128)(2,1)} %get-tuple-element.175.refs_2_, ...), custom_call_target="tpu_custom_call" | custom-call | flops 206158430208 | bytes 671088640 | tf_op jit(solution)/shard_map/weight_grads/pallas_call | solution.py:46
  346.6 14.3 %collective-permute-done.30.refs_0_ = bf16[64,2304]{1,0:T(8,128)(2,1)S(1)} collective-permute-done((bf16[64,2304]{1,0:T(8,128)(2,1)S(1)}, bf16[64,2304]{1,0:T(8,128)(2,1)S(1)}, u32[]{:S(2)}, u32[]{:S(2)}) %collective-permute-start.30) | collective-permute-done | bytes 294944 | tf_op jit(solution)/shard_map/ppermute | solution.py:444
  363.8 2.4 collective-permute-done.37.refs_2_
  372.5 2.6 collective-permute-start.40
  376.6 10.7 %collective-permute-done.40.refs_2_ = f32[18,128]{1,0:T(8,128)S(1)} collective-permute-done((f32[18,128]{1,0:T(8,128)S(1)}, f32[18,128]{1,0:T(8,128)S(1)}, u32[]{:S(2)}, u32[]{:S(2)}) %collective-permute-start.40) | collective-permute-done | bytes 9248 | tf_op jit(solution)/shard_map/ppermute | solution.py:444
  393.7 2.3 collective-permute-start.41
  403.3 2.2 fusion.6
  405.6 4.6 %fusion.10 = (bf16[512,1024]{1,0:T(8,128)(2,1)}, bf16[512,1024]{1,0:T(8,128)(2,1)}) fusion(f32[512,1024]{1,0:T(8,128)S(1)} %copy-done.21, bf16[512,1024]{1,0:T(8,128)(2,1)S(1)} %copy-done.4, bf16[512,1024]{1,0:T(8,128)(2,1)S(1)} %copy-done.9, bf16[512,1024]{1,0:T(8,128)(2,1)S(1)} %copy-done.12, f32[512]{0:T(512)S(1)} %broadcast_multiply_fusion, ...), kind=kLoop, calls=%fused_computation.19 | loop fusion | flops 12058624 | bytes 11542528 | tf_op jit(solution)/shard_map/convert_element_type | solution.py:744
  418.4 8.2 %collective-permute-done.45 = bf16[64,1536]{1,0:T(8,128)(2,1)S(1)} collective-permute-done((bf16[64,1536]{1,0:T(8,128)(2,1)S(1)}, bf16[64,1536]{1,0:T(8,128)(2,1)S(1)}, u32[]{:S(2)}, u32[]{:S(2)}) %collective-permute-start.45) | collective-permute-done | bytes 196640 | tf_op jit(solution)/shard_map/ppermute | solution.py:444
  427.8 2.9 collective-permute-done.44
  (378 shorter events, 116.2 us)
Async XLA Ops:
  4.7 23.0 %collective-permute-start.1 = (bf16[64,1536]{1,0:T(8,128)(2,1)S(1)}, bf16[64,1536]{1,0:T(8,128)(2,1)S(1)}, u32[]{:S(2)}, u32[]{:S(2)}) collective-permute-start(bf16[64,1536]{1,0:T(8,128)(2,1)S(1)} %get-tuple-element.224), channel_id=1, source_target_pairs={{0,16},{2,18},{4,20},{6,22},{8,24},{10,26},{12,28},{14,30},{16,0},... | collective-permute-start | bytes 589832 | tf_op jit(solution)/shard_map/ppermute | solution.py:444
  8.8 18.9 %collective-permute-start = (bf16[64,1536]{1,0:T(8,128)(2,1)S(1)}, bf16[64,1536]{1,0:T(8,128)(2,1)S(1)}, u32[]{:S(2)}, u32[]{:S(2)}) collective-permute-start(bf16[64,1536]{1,0:T(8,128)(2,1)S(1)} %get-tuple-element.225), channel_id=1, source_target_pairs={{0,16},{2,18},{4,20},{6,22},{8,24},{10,26},{12,28},{14,30},{16,0},... | collective-permute-start | bytes 589832 | tf_op jit(solution)/shard_map/ppermute | solution.py:444
  10.0 17.8 %collective-permute-start.2 = (bf16[256,1024]{1,0:T(8,128)(2,1)}, bf16[256,1024]{1,0:T(8,128)(2,1)S(1)}, u32[]{:S(2)}, u32[]{:S(2)}) collective-permute-start(bf16[256,1024]{1,0:T(8,128)(2,1)} %get-tuple-element.217), channel_id=1, source_target_pairs={{0,1},{1,0},{2,3},{3,2},{4,5},{5,4},{6,7},{7,6},{8,9},{9,8},{10,11... | collective-permute-start | bytes 1572872 | tf_op jit(solution)/shard_map/ppermute | solution.py:444
  30.7 10.1 %collective-permute-start.4 = (bf16[128,1536]{1,0:T(8,128)(2,1)S(1)}, bf16[128,1536]{1,0:T(8,128)(2,1)S(1)}, u32[]{:S(2)}, u32[]{:S(2)}) collective-permute-start(bf16[128,1536]{1,0:T(8,128)(2,1)S(1)} %pad_maximum_fusion.15), channel_id=1, source_target_pairs={{0,4},{2,6},{4,0},{6,2},{8,12},{10,14},{12,8},{14,10},{16,20},{18,... | collective-permute-start | bytes 1179656 | tf_op jit(solution)/shard_map/ppermute | solution.py:444
  32.3 9.8 %collective-permute-start.3 = (bf16[128,1536]{1,0:T(8,128)(2,1)S(1)}, bf16[128,1536]{1,0:T(8,128)(2,1)S(1)}, u32[]{:S(2)}, u32[]{:S(2)}) collective-permute-start(bf16[128,1536]{1,0:T(8,128)(2,1)S(1)} %pad_maximum_fusion.14), channel_id=1, source_target_pairs={{0,8},{2,10},{4,12},{6,14},{8,0},{10,2},{12,4},{14,6},{16,24},{18,... | collective-permute-start | bytes 1179656 | tf_op jit(solution)/shard_map/ppermute | solution.py:444
  33.8 40.1 %collective-permute-start.9 = (bf16[512,1024]{1,0:T(8,128)(2,1)S(1)}, bf16[512,1024]{1,0:T(8,128)(2,1)S(1)}, u32[]{:S(2)}, u32[]{:S(2)}) collective-permute-start(bf16[512,1024]{1,0:T(8,128)(2,1)S(1)} %copy-done.39), channel_id=1, source_target_pairs={{0,1},{1,0},{2,3},{3,2},{4,5},{5,4},{6,7},{7,6},{8,9},{9,8},{10,11... | collective-permute-start | bytes 3145736 | tf_op jit(solution)/shard_map/ppermute | solution.py:444
  44.9 30.0 %collective-permute-start.6 = (bf16[256,1536]{1,0:T(8,128)(2,1)S(1)}, bf16[256,1536]{1,0:T(8,128)(2,1)S(1)}, u32[]{:S(2)}, u32[]{:S(2)}) collective-permute-start(bf16[256,1536]{1,0:T(8,128)(2,1)S(1)} %pad_maximum_fusion.9), channel_id=1, source_target_pairs={{0,8},{2,10},{4,12},{6,14},{8,0},{10,2},{12,4},{14,6},{16,24},{18,... | collective-permute-start | bytes 2359304 | tf_op jit(solution)/shard_map/ppermute | solution.py:444
  46.5 28.3 %collective-permute-start.5 = (bf16[256,1536]{1,0:T(8,128)(2,1)S(1)}, bf16[256,1536]{1,0:T(8,128)(2,1)S(1)}, u32[]{:S(2)}, u32[]{:S(2)}) collective-permute-start(bf16[256,1536]{1,0:T(8,128)(2,1)S(1)} %pad_maximum_fusion.8), channel_id=1, source_target_pairs={{0,4},{2,6},{4,0},{6,2},{8,12},{10,14},{12,8},{14,10},{16,20},{18,... | collective-permute-start | bytes 2359304 | tf_op jit(solution)/shard_map/ppermute | solution.py:444
  47.6 40.5 %copy-start.33 = (bf16[64,2304]{1,0:T(8,128)(2,1)}, bf16[64,2304]{1,0:T(8,128)(2,1)S(1)}, u32[]{:S(2)}) copy-start(bf16[64,2304]{1,0:T(8,128)(2,1)S(1)} %get-tuple-element.222) | copy-start | bytes 884740
  47.6 23.2 %collective-permute-start.8 = (bf16[64,2304]{1,0:T(8,128)(2,1)S(1)}, bf16[64,2304]{1,0:T(8,128)(2,1)S(1)}, u32[]{:S(2)}, u32[]{:S(2)}) collective-permute-start(bf16[64,2304]{1,0:T(8,128)(2,1)S(1)} %get-tuple-element.222), channel_id=1, source_target_pairs={{0,16},{2,18},{4,20},{6,22},{8,24},{10,26},{12,28},{14,30},{16,0},... | collective-permute-start | bytes 884744 | tf_op jit(solution)/shard_map/ppermute | solution.py:444
  50.3 23.7 %collective-permute-start.7 = (bf16[64,2304]{1,0:T(8,128)(2,1)S(1)}, bf16[64,2304]{1,0:T(8,128)(2,1)S(1)}, u32[]{:S(2)}, u32[]{:S(2)}) collective-permute-start(bf16[64,2304]{1,0:T(8,128)(2,1)S(1)} %get-tuple-element.223), channel_id=1, source_target_pairs={{0,16},{2,18},{4,20},{6,22},{8,24},{10,26},{12,28},{14,30},{16,0},... | collective-permute-start | bytes 884744 | tf_op jit(solution)/shard_map/ppermute | solution.py:444
  78.3 8.7 %collective-permute-start.13 = (bf16[512,1536]{1,0:T(8,128)(2,1)S(1)}, bf16[512,1536]{1,0:T(8,128)(2,1)S(1)}, u32[]{:S(2)}, u32[]{:S(2)}) collective-permute-start(bf16[512,1536]{1,0:T(8,128)(2,1)S(1)} %pad_maximum_fusion.3.refs_9_.refs_12_), channel_id=1, source_target_pairs={{0,2},{2,0},{4,6},{6,4},{8,10},{10,8},{12,14},{14,12},{16,18},{18,... | collective-permute-start | bytes 4718600 | tf_op jit(solution)/shard_map/ppermute | solution.py:444
  78.4 8.6 %collective-permute-start.12 = (bf16[512,1536]{1,0:T(8,128)(2,1)S(1)}, bf16[512,1536]{1,0:T(8,128)(2,1)}, u32[]{:S(2)}, u32[]{:S(2)}) collective-permute-start(bf16[512,1536]{1,0:T(8,128)(2,1)S(1)} %pad_maximum_fusion.2.refs_6_.refs_9_), channel_id=1, source_target_pairs={{0,2},{2,0},{4,6},{6,4},{8,10},{10,8},{12,14},{14,12},{16,18},{18,... | collective-permute-start | bytes 4718600 | tf_op jit(solution)/shard_map/ppermute | solution.py:444
  78.9 26.3 %collective-permute-start.14 = (bf16[256,1024]{1,0:T(8,128)(2,1)}, bf16[256,1024]{1,0:T(8,128)(2,1)}, u32[]{:S(2)}, u32[]{:S(2)}) collective-permute-start(bf16[256,1024]{1,0:T(8,128)(2,1)} %get-tuple-element.216), channel_id=1, source_target_pairs={{0,1},{1,0},{2,3},{3,2},{4,5},{5,4},{6,7},{7,6},{8,9},{9,8},{10,11... | collective-permute-start | bytes 1572872 | tf_op jit(solution)/shard_map/ppermute | solution.py:444
  80.9 24.3 %collective-permute-start.11 = (bf16[128,2304]{1,0:T(8,128)(2,1)}, bf16[128,2304]{1,0:T(8,128)(2,1)}, u32[]{:S(2)}, u32[]{:S(2)}) collective-permute-start(bf16[128,2304]{1,0:T(8,128)(2,1)} %pad_maximum_fusion.12.refs_12_), channel_id=1, source_target_pairs={{0,4},{2,6},{4,0},{6,2},{8,12},{10,14},{12,8},{14,10},{16,20},{18,... | collective-permute-start | bytes 1769480 | tf_op jit(solution)/shard_map/ppermute | solution.py:444
  83.0 22.2 %collective-permute-start.10 = (bf16[128,2304]{1,0:T(8,128)(2,1)}, bf16[128,2304]{1,0:T(8,128)(2,1)}, u32[]{:S(2)}, u32[]{:S(2)}) collective-permute-start(bf16[128,2304]{1,0:T(8,128)(2,1)} %pad_maximum_fusion.11.refs_11_), channel_id=1, source_target_pairs={{0,8},{2,10},{4,12},{6,14},{8,0},{10,2},{12,4},{14,6},{16,24},{18,... | collective-permute-start | bytes 1769480 | tf_op jit(solution)/shard_map/ppermute | solution.py:444
  105.2 24.7 %collective-permute-start.17 = (bf16[512,1024]{1,0:T(8,128)(2,1)}, bf16[512,1024]{1,0:T(8,128)(2,1)}, u32[]{:S(2)}, u32[]{:S(2)}) collective-permute-start(bf16[512,1024]{1,0:T(8,128)(2,1)} %get-tuple-element.128), channel_id=1, source_target_pairs={{0,1},{1,0},{2,3},{3,2},{4,5},{5,4},{6,7},{7,6},{8,9},{9,8},{10,11... | collective-permute-start | bytes 3145736 | tf_op jit(solution)/shard_map/ppermute | solution.py:444
  110.6 27.4 %collective-permute-start.16 = (bf16[256,2304]{1,0:T(8,128)(2,1)}, bf16[256,2304]{1,0:T(8,128)(2,1)}, u32[]{:S(2)}, u32[]{:S(2)}) collective-permute-start(bf16[256,2304]{1,0:T(8,128)(2,1)} %pad_maximum_fusion.5.refs_14_), channel_id=1, source_target_pairs={{0,8},{2,10},{4,12},{6,14},{8,0},{10,2},{12,4},{14,6},{16,24},{18,... | collective-permute-start | bytes 3538952 | tf_op jit(solution)/shard_map/ppermute | solution.py:444
  110.6 27.6 %collective-permute-start.15 = (bf16[256,2304]{1,0:T(8,128)(2,1)}, bf16[256,2304]{1,0:T(8,128)(2,1)}, u32[]{:S(2)}, u32[]{:S(2)}) collective-permute-start(bf16[256,2304]{1,0:T(8,128)(2,1)} %pad_maximum_fusion.4.refs_13_), channel_id=1, source_target_pairs={{0,4},{2,6},{4,0},{6,2},{8,12},{10,14},{12,8},{14,10},{16,20},{18,... | collective-permute-start | bytes 3538952 | tf_op jit(solution)/shard_map/ppermute | solution.py:444
  143.3 9.3 %collective-permute-start.19 = (bf16[512,2304]{1,0:T(8,128)(2,1)S(1)}, bf16[512,2304]{1,0:T(8,128)(2,1)S(1)}, u32[]{:S(2)}, u32[]{:S(2)}) collective-permute-start(bf16[512,2304]{1,0:T(8,128)(2,1)S(1)} %pad_maximum_fusion.1.refs_7_), channel_id=1, source_target_pairs={{0,2},{2,0},{4,6},{6,4},{8,10},{10,8},{12,14},{14,12},{16,18},{18,... | collective-permute-start | bytes 7077896 | tf_op jit(solution)/shard_map/ppermute | solution.py:444
  143.4 9.2 %collective-permute-start.18 = (bf16[512,2304]{1,0:T(8,128)(2,1)S(1)}, bf16[512,2304]{1,0:T(8,128)(2,1)}, u32[]{:S(2)}, u32[]{:S(2)}) collective-permute-start(bf16[512,2304]{1,0:T(8,128)(2,1)S(1)} %pad_maximum_fusion.refs_4_), channel_id=1, source_target_pairs={{0,2},{2,0},{4,6},{6,4},{8,10},{10,8},{12,14},{14,12},{16,18},{18,... | collective-permute-start | bytes 7077896 | tf_op jit(solution)/shard_map/ppermute | solution.py:444
  151.4 27.4 %collective-permute-start.20 = (bf16[512,1024]{1,0:T(8,128)(2,1)}, bf16[512,1024]{1,0:T(8,128)(2,1)}, u32[]{:S(2)}, u32[]{:S(2)}) collective-permute-start(bf16[512,1024]{1,0:T(8,128)(2,1)} %multiply_convert_fusion.refs_0_.refs_9_.refs_1_), channel_id=1, source_target_pairs={{0,1},{1,0},{2,3},{3,2},{4,5},{5,4},{6,7},{7,6},{8,9},{9,8},{10,11... | collective-permute-start | bytes 3145736 | tf_op jit(solution)/shard_map/ppermute | solution.py:444
  196.5 24.9 %collective-permute-start.22 = (bf16[512,1024]{1,0:T(8,128)(2,1)}, bf16[512,1024]{1,0:T(8,128)(2,1)S(1)}, u32[]{:S(2)}, u32[]{:S(2)}) collective-permute-start(bf16[512,1024]{1,0:T(8,128)(2,1)} %get-tuple-element.144.refs_3_.refs_4_), channel_id=1, source_target_pairs={{0,1},{1,0},{2,3},{3,2},{4,5},{5,4},{6,7},{7,6},{8,9},{9,8},{10,11... | collective-permute-start | bytes 3145736 | tf_op jit(solution)/shard_map/ppermute | solution.py:444
  211.8 31.7 %collective-permute-start.21 = (bf16[512,2304]{1,0:T(8,128)(2,1)}, bf16[512,2304]{1,0:T(8,128)(2,1)}, u32[]{:S(2)}, u32[]{:S(2)}) collective-permute-start(bf16[512,2304]{1,0:T(8,128)(2,1)} %get-tuple-element.149), channel_id=1, source_target_pairs={{0,2},{2,0},{4,6},{6,4},{8,10},{10,8},{12,14},{14,12},{16,18},{18,... | collective-permute-start | bytes 7077896 | tf_op jit(solution)/shard_map/ppermute | solution.py:444
  238.4 5.1 %collective-permute-start.23 = (bf16[512,2304]{1,0:T(8,128)(2,1)}, bf16[512,2304]{1,0:T(8,128)(2,1)S(1)}, u32[]{:S(2)}, u32[]{:S(2)}) collective-permute-start(bf16[512,2304]{1,0:T(8,128)(2,1)} %get-tuple-element.152), channel_id=1, source_target_pairs={{0,2},{2,0},{4,6},{6,4},{8,10},{10,8},{12,14},{14,12},{16,18},{18,... | collective-permute-start | bytes 7077896 | tf_op jit(solution)/shard_map/ppermute | solution.py:444
  239.1 34.2 %collective-permute-start.26 = (bf16[512,1024]{1,0:T(8,128)(2,1)}, bf16[512,1024]{1,0:T(8,128)(2,1)}, u32[]{:S(2)}, u32[]{:S(2)}) collective-permute-start(bf16[512,1024]{1,0:T(8,128)(2,1)} %get-tuple-element.207.refs_4_.refs_1_.refs_0_), channel_id=1, source_target_pairs={{0,1},{1,0},{2,3},{3,2},{4,5},{5,4},{6,7},{7,6},{8,9},{9,8},{10,11... | collective-permute-start | bytes 3145736 | tf_op jit(solution)/shard_map/ppermute | solution.py:444
  249.0 28.4 %collective-permute-start.24 = (bf16[2,2,64,2304]{3,2,1,0:T(8,128)(2,1)}, bf16[2,2,64,2304]{3,2,1,0:T(8,128)(2,1)}, u32[]{:S(2)}, u32[]{:S(2)}) collective-permute-start(bf16[2,2,64,2304]{3,2,1,0:T(8,128)(2,1)} %bitcast.8.refs_16_), channel_id=1, source_target_pairs={{0,4},{2,6},{4,0},{6,2},{8,12},{10,14},{12,8},{14,10},{16,20},{18,... | collective-permute-start | bytes 3538952 | tf_op jit(solution)/shard_map/ppermute | solution.py:444
  251.7 28.1 %collective-permute-start.25 = (bf16[2,2,64,2304]{3,2,1,0:T(8,128)(2,1)}, bf16[2,2,64,2304]{3,2,1,0:T(8,128)(2,1)}, u32[]{:S(2)}, u32[]{:S(2)}) collective-permute-start(bf16[2,2,64,2304]{3,2,1,0:T(8,128)(2,1)} %fusion.13.refs_17_), channel_id=1, source_target_pairs={{0,8},{2,10},{4,12},{6,14},{8,0},{10,2},{12,4},{14,6},{16,24},{18,... | collective-permute-start | bytes 3538952 | tf_op jit(solution)/shard_map/ppermute | solution.py:444
  282.1 49.9 %collective-permute-start.33 = (bf16[256,1024]{1,0:T(8,128)(2,1)}, bf16[256,1024]{1,0:T(8,128)(2,1)}, u32[]{:S(2)}, u32[]{:S(2)}) collective-permute-start(bf16[256,1024]{1,0:T(8,128)(2,1)} %get-tuple-element.214), channel_id=1, source_target_pairs={{0,1},{1,0},{2,3},{3,2},{4,5},{5,4},{6,7},{7,6},{8,9},{9,8},{10,11... | collective-permute-start | bytes 1572872 | tf_op jit(solution)/shard_map/ppermute | solution.py:444
  283.2 30.4 %collective-permute-start.29 = (bf16[256,1024]{1,0:T(8,128)(2,1)}, bf16[256,1024]{1,0:T(8,128)(2,1)}, u32[]{:S(2)}, u32[]{:S(2)}) collective-permute-start(bf16[256,1024]{1,0:T(8,128)(2,1)} %get-tuple-element.215), channel_id=1, source_target_pairs={{0,1},{1,0},{2,3},{3,2},{4,5},{5,4},{6,7},{7,6},{8,9},{9,8},{10,11... | collective-permute-start | bytes 1572872 | tf_op jit(solution)/shard_map/ppermute | solution.py:444
  286.5 27.1 %collective-permute-start.28 = (bf16[2,64,2304]{2,1,0:T(8,128)(2,1)}, bf16[2,64,2304]{2,1,0:T(8,128)(2,1)}, u32[]{:S(2)}, u32[]{:S(2)}) collective-permute-start(bf16[2,64,2304]{2,1,0:T(8,128)(2,1)} %fusion.14.refs_16_), channel_id=1, source_target_pairs={{0,4},{2,6},{4,0},{6,2},{8,12},{10,14},{12,8},{14,10},{16,20},{18,... | collective-permute-start | bytes 1769480 | tf_op jit(solution)/shard_map/ppermute | solution.py:444
  289.7 23.9 %collective-permute-start.27 = (bf16[2,64,2304]{2,1,0:T(8,128)(2,1)}, bf16[2,64,2304]{2,1,0:T(8,128)(2,1)}, u32[]{:S(2)}, u32[]{:S(2)}) collective-permute-start(bf16[2,64,2304]{2,1,0:T(8,128)(2,1)} %fusion.15.refs_15_), channel_id=1, source_target_pairs={{0,8},{2,10},{4,12},{6,14},{8,0},{10,2},{12,4},{14,6},{16,24},{18,... | collective-permute-start | bytes 1769480 | tf_op jit(solution)/shard_map/ppermute | solution.py:444
  316.0 16.0 %collective-permute-start.32 = (f32[18,128]{1,0:T(8,128)S(1)}, f32[18,128]{1,0:T(8,128)S(1)}, u32[]{:S(2)}, u32[]{:S(2)}) collective-permute-start(f32[18,128]{1,0:T(8,128)S(1)} %maximum_bitcast_fusion.refs_6_), channel_id=1, source_target_pairs={{0,2},{2,0},{4,6},{6,4},{8,10},{10,8},{12,14},{14,12},{16,18},{18,... | collective-permute-start | bytes 27656 | tf_op jit(solution)/shard_map/ppermute | solution.py:444
  319.5 16.6 %collective-permute-start.31 = (bf16[64,2304]{1,0:T(8,128)(2,1)S(1)}, bf16[64,2304]{1,0:T(8,128)(2,1)S(1)}, u32[]{:S(2)}, u32[]{:S(2)}) collective-permute-start(bf16[64,2304]{1,0:T(8,128)(2,1)S(1)} %fusion.21.refs_3_.refs_4_), channel_id=1, source_target_pairs={{0,16},{2,18},{4,20},{6,22},{8,24},{10,26},{12,28},{14,30},{16,0},... | collective-permute-start | bytes 884744 | tf_op jit(solution)/shard_map/ppermute | solution.py:444
  331.7 34.5 %collective-permute-start.35 = (bf16[512,1536]{1,0:T(8,128)(2,1)}, bf16[512,1536]{1,0:T(8,128)(2,1)}, u32[]{:S(2)}, u32[]{:S(2)}) collective-permute-start(bf16[512,1536]{1,0:T(8,128)(2,1)} %get-tuple-element.190), channel_id=1, source_target_pairs={{0,2},{2,0},{4,6},{6,4},{8,10},{10,8},{12,14},{14,12},{16,18},{18,... | collective-permute-start | bytes 4718600 | tf_op jit(solution)/shard_map/ppermute | solution.py:444
  345.7 20.5 %collective-permute-start.36 = (bf16[512,1536]{1,0:T(8,128)(2,1)}, bf16[512,1536]{1,0:T(8,128)(2,1)S(1)}, u32[]{:S(2)}, u32[]{:S(2)}) collective-permute-start(bf16[512,1536]{1,0:T(8,128)(2,1)} %get-tuple-element.191), channel_id=1, source_target_pairs={{0,2},{2,0},{4,6},{6,4},{8,10},{10,8},{12,14},{14,12},{16,18},{18,... | collective-permute-start | bytes 4718600 | tf_op jit(solution)/shard_map/ppermute | solution.py:444
  345.7 15.2 %collective-permute-start.30 = (bf16[64,2304]{1,0:T(8,128)(2,1)S(1)}, bf16[64,2304]{1,0:T(8,128)(2,1)S(1)}, u32[]{:S(2)}, u32[]{:S(2)}) collective-permute-start(bf16[64,2304]{1,0:T(8,128)(2,1)S(1)} %copy-done.69), channel_id=1, source_target_pairs={{0,16},{2,18},{4,20},{6,22},{8,24},{10,26},{12,28},{14,30},{16,0},... | collective-permute-start | bytes 884744 | tf_op jit(solution)/shard_map/ppermute | solution.py:444
  345.8 15.2 %collective-permute-start.34 = (f32[18,128]{1,0:T(8,128)S(1)}, f32[18,128]{1,0:T(8,128)S(1)}, u32[]{:S(2)}, u32[]{:S(2)}) collective-permute-start(f32[18,128]{1,0:T(8,128)S(1)} %copy-done.97), channel_id=1, source_target_pairs={{0,4},{2,6},{4,0},{6,2},{8,12},{10,14},{12,8},{14,10},{16,20},{18,... | collective-permute-start | bytes 27656 | tf_op jit(solution)/shard_map/ppermute | solution.py:444
  362.4 3.8 collective-permute-start.37
  362.5 39.8 %collective-permute-start.43 = (bf16[512,1024]{1,0:T(8,128)(2,1)}, bf16[512,1024]{1,0:T(8,128)(2,1)S(1)}, u32[]{:S(2)}, u32[]{:S(2)}) collective-permute-start(bf16[512,1024]{1,0:T(8,128)(2,1)} %get-tuple-element.177), channel_id=1, source_target_pairs={{0,1},{1,0},{2,3},{3,2},{4,5},{5,4},{6,7},{7,6},{8,9},{9,8},{10,11... | collective-permute-start | bytes 3145736 | tf_op jit(solution)/shard_map/ppermute | solution.py:444
  369.4 18.4 %collective-permute-start.38 = (bf16[2,2,64,1536]{3,2,1,0:T(8,128)(2,1)S(1)}, bf16[2,2,64,1536]{3,2,1,0:T(8,128)(2,1)S(1)}, u32[]{:S(2)}, u32[]{:S(2)}) collective-permute-start(bf16[2,2,64,1536]{3,2,1,0:T(8,128)(2,1)S(1)} %bitcast.207), channel_id=1, source_target_pairs={{0,4},{2,6},{4,0},{6,2},{8,12},{10,14},{12,8},{14,10},{16,20},{18,... | collective-permute-start | bytes 2359304 | tf_op jit(solution)/shard_map/ppermute | solution.py:444
  371.0 18.4 %collective-permute-start.39 = (bf16[2,2,64,1536]{3,2,1,0:T(8,128)(2,1)S(1)}, bf16[2,2,64,1536]{3,2,1,0:T(8,128)(2,1)S(1)}, u32[]{:S(2)}, u32[]{:S(2)}) collective-permute-start(bf16[2,2,64,1536]{3,2,1,0:T(8,128)(2,1)S(1)} %fusion.16), channel_id=1, source_target_pairs={{0,8},{2,10},{4,12},{6,14},{8,0},{10,2},{12,4},{14,6},{16,24},{18,... | collective-permute-start | bytes 2359304 | tf_op jit(solution)/shard_map/ppermute | solution.py:444
  372.5 14.7 %collective-permute-start.40 = (f32[18,128]{1,0:T(8,128)S(1)}, f32[18,128]{1,0:T(8,128)S(1)}, u32[]{:S(2)}, u32[]{:S(2)}) collective-permute-start(f32[18,128]{1,0:T(8,128)S(1)} %add.299), channel_id=1, source_target_pairs={{0,16},{2,18},{4,20},{6,22},{8,24},{10,26},{12,28},{14,30},{16,0},... | collective-permute-start | bytes 27656 | tf_op jit(solution)/shard_map/ppermute | solution.py:444
  391.7 10.6 %collective-permute-start.42 = (bf16[2,64,1536]{2,1,0:T(8,128)(2,1)S(1)}, bf16[2,64,1536]{2,1,0:T(8,128)(2,1)}, u32[]{:S(2)}, u32[]{:S(2)}) collective-permute-start(bf16[2,64,1536]{2,1,0:T(8,128)(2,1)S(1)} %fusion.17.refs_2_), channel_id=1, source_target_pairs={{0,4},{2,6},{4,0},{6,2},{8,12},{10,14},{12,8},{14,10},{16,20},{18,... | collective-permute-start | bytes 1179656 | tf_op jit(solution)/shard_map/ppermute | solution.py:444
  393.7 9.1 %collective-permute-start.41 = (bf16[2,64,1536]{2,1,0:T(8,128)(2,1)S(1)}, bf16[2,64,1536]{2,1,0:T(8,128)(2,1)}, u32[]{:S(2)}, u32[]{:S(2)}) collective-permute-start(bf16[2,64,1536]{2,1,0:T(8,128)(2,1)S(1)} %fusion.18.refs_1_), channel_id=1, source_target_pairs={{0,8},{2,10},{4,12},{6,14},{8,0},{10,2},{12,4},{14,6},{16,24},{18,... | collective-permute-start | bytes 1179656 | tf_op jit(solution)/shard_map/ppermute | solution.py:444
  410.1 6.4 %collective-permute-start.46 = (f32[18,128]{1,0:T(8,128)}, f32[18,128]{1,0:T(8,128)S(1)}, u32[]{:S(2)}, u32[]{:S(2)}) collective-permute-start(f32[18,128]{1,0:T(8,128)} %get-tuple-element.206), channel_id=1, source_target_pairs={{0,1},{1,0},{2,3},{3,2},{4,5},{5,4},{6,7},{7,6},{8,9},{9,8},{10,11... | collective-permute-start | bytes 27656 | tf_op jit(solution)/shard_map/ppermute | solution.py:444
  413.5 13.0 %collective-permute-start.45 = (bf16[64,1536]{1,0:T(8,128)(2,1)S(1)}, bf16[64,1536]{1,0:T(8,128)(2,1)S(1)}, u32[]{:S(2)}, u32[]{:S(2)}) collective-permute-start(bf16[64,1536]{1,0:T(8,128)(2,1)S(1)} %fusion.23), channel_id=1, source_target_pairs={{0,16},{2,18},{4,20},{6,22},{8,24},{10,26},{12,28},{14,30},{16,0},... | collective-permute-start | bytes 589832 | tf_op jit(solution)/shard_map/ppermute | solution.py:444
  414.7 15.9 %collective-permute-start.44 = (bf16[64,1536]{1,0:T(8,128)(2,1)S(1)}, bf16[64,1536]{1,0:T(8,128)(2,1)S(1)}, u32[]{:S(2)}, u32[]{:S(2)}) collective-permute-start(bf16[64,1536]{1,0:T(8,128)(2,1)S(1)} %fusion.25), channel_id=1, source_target_pairs={{0,16},{2,18},{4,20},{6,22},{8,24},{10,26},{12,28},{14,30},{16,0},... | collective-permute-start | bytes 589832 | tf_op jit(solution)/shard_map/ppermute | solution.py:444
  (104 other events, 786.9 us)

commit v4 on v3

--- a/solution.py
+++ b/solution.py
@@ -207,13 +207,16 @@
     target_ref = refs[-1]
     count = places_ref.shape[0]
     block = target_ref.shape[0] // count
-    for index in range(count):
-        place = pl.ds(pl.multiple_of(places_ref[index] * block, block), block)
-        begin = 0
-        for source_ref in refs[:-1]:
-            rows = source_ref.shape[0]
-            target_ref[place, begin : begin + rows] = source_ref[:, index * block : (index + 1) * block].T
-            begin += rows
+    together = max(1, min(count, 128 // block))
+    begin = 0
+    for source_ref in refs[:-1]:
+        rows = source_ref.shape[0]
+        for first in range(0, count, together):
+            turned = source_ref[:, first * block : (first + together) * block].T
+            for index in range(together):
+                place = pl.ds(pl.multiple_of(places_ref[first + index] * block, block), block)
+                target_ref[place, begin : begin + rows] = turned[index * block : (index + 1) * block]
+        begin += rows
 
 
 def turn(places, sources, part, parts, after=(), into=(), flops=0):
@@ -726,7 +729,7 @@
         sums_got = exchange(sums, *hops.pop(0))
         keep, send, token = weight_grads(*normed_t, *attended_t, *dproj, head_out, heads, *cut, after, index > 0)
         attn_sums.append(BlockSum(dp_size, keep, send, orders[index]))
-        token, sums_got, ffn_rest = arrive(mlp_sums[index : index + 1], token, sums_got, ffn_rest)
+        token, sums_got, ffn_rest = arrive([] if index else mlp_sums[:1], token, sums_got, ffn_rest)
         sums = sums + sums_got
         after = [token, sums]
     ffn_got = jnp.concatenate([ffn_first, ffn_rest], axis=0) if by_pair else ffn_rest
@@ -736,13 +739,13 @@
     sums = sums + sums_got
     sent = [block_sum.halve() for block_sum in attn_sums]
     sums_got = exchange(sums, *hops.pop(0))
-    (sums_got,) = arrive(attn_sums, sums_got)
+    (sums_got,) = arrive([*attn_sums, *mlp_sums[1:]], sums_got)
     sums = sums + sums_got
     sent = [block_sum.halve() for block_sum in attn_sums]
     dx_got, *_ = sync(dx_got, *sent)
     grad_normed = add_sum(dx_parts, dx_got)
     grad_inputs = (grad_middle + norm_back(unit_in, scale_in, grad_normed * gain_attn)).astype(BF16)
-    grad_inputs, sums = arrive(attn_sums, grad_inputs, sums)
+    (sums,) = arrive(attn_sums, sums)
     while any(block_sum.flips for block_sum in attn_sums):
         for block_sum in attn_sums:
             block_sum.halve()

time: 442 us -> 430 us (0.973)
  Pallas kernels: 170 us -> 163 us
    pallas_call x35, Pallas kernels: 170 us -> 163 us  [kernel_call(): pl.pallas_call(run, grid=grid, in_specs=[spec for _, spec in inputs] + [p...]
    unnamed x220 -> x218, local copies, waits for them, and re-layouts: 23.9 us -> 22.1 us
  transfers between devices with their start and end apart: 47 -> 47, of which waited for: 20 -> 23; matrix products, arithmetic and copies ran while one was open for 16% -> 17% of each run, Pallas kernels for 35% -> 34%
where the time goes in v4:
time: 430 us; the launch traced here: 425 us
  Pallas kernels  163 us (38%)
  waiting for transfers between devices  100 us (23%)
  other arithmetic  70.5 us (16%)
  starting transfers between devices  49.8 us (12%)
  local copies, waits for them, and re-layouts  39.6 us (9%)
    pallas_call x35, Pallas kernels, kernel_call(): pl.pallas_call(run, grid=grid, in_specs=[spec for _, spec in inputs] + [p...  163 us
    ppermute x47, waiting for transfers between devices, exchange(): lax.ppermute(array, axis, [(index, index ^ flip) for index in range(size)])  100 us
    ppermute x47, starting transfers between devices, exchange(): lax.ppermute(array, axis, [(index, index ^ flip) for index in range(size)])  49.8 us
    unnamed x218, local copies, waits for them, and re-layouts  22.1 us
    convert_element_type x12, other arithmetic, halve(): sent = self.part(flip).astype(BF16)  20.6 us
    concatenate x12, other arithmetic, join(): self.held = jnp.concatenate([self.held, self.got], axis=0)  15.7 us
    reshape x7, local copies, waits for them, and re-layouts, pack(): part.reshape(rows, pieces, part.shape[1] // pieces)  8.64 us
  transfers between devices with their start and end apart: 47, of which 23 were waited for; matrix products, arithmetic and copies ran while one was open for 17% of the time, Pallas kernels for 34%

profile of v4, /device:TPU:0, one launch (start us, length us, event | category | flops | bytes accessed | tf_op | source)
XLA Modules:
  0.0 425.1 jit_solution(8293221305959437153)
XLA Ops:
  4.7 4.1 collective-permute-start.1
  19.5 2.6 turn.7.refs_4_
  23.4 2.6 turn.8.refs_5_
  33.1 6.6 %collective-permute-done.4.refs_1_ = bf16[128,1536]{1,0:T(8,128)(2,1)S(1)} collective-permute-done((bf16[128,1536]{1,0:T(8,128)(2,1)S(1)}, bf16[128,1536]{1,0:T(8,128)(2,1)S(1)}, u32[]{:S(2)}, u32[]{:S(2)}) %collective-permute-start.4) | collective-permute-done | bytes 393248 | tf_op jit(solution)/shard_map/ppermute | solution.py:447
  46.4 3.4 collective-permute-start.8
  49.9 19.7 %collective-permute-done.8.refs_3_ = bf16[64,2304]{1,0:T(8,128)(2,1)S(1)} collective-permute-done((bf16[64,2304]{1,0:T(8,128)(2,1)S(1)}, bf16[64,2304]{1,0:T(8,128)(2,1)S(1)}, u32[]{:S(2)}, u32[]{:S(2)}) %collective-permute-start.8) | collective-permute-done | bytes 294944 | tf_op jit(solution)/shard_map/ppermute | solution.py:447
  69.6 3.6 collective-permute-done.7.refs_2_
  83.6 3.8 collective-permute-start.10
  88.6 16.8 %attend.2 = (bf16[512,1024]{1,0:T(8,128)(2,1)}, f32[32,512]{1,0:T(8,128)}, bf16[1024,3584]{1,0:T(8,128)(2,1)}, bf16[1024,1024]{1,0:T(8,128)(2,1)}) custom-call(bf16[512,1024]{1,0:T(8,128)(2,1)} %get-tuple-element.116.refs_0_.refs_1_, f32[512,128]{1,0:T(8,128)} %constant.32.clone.refs_1_.refs_4_, f32[512,128]{1,0:T(8,128)} %constant.33.clone.refs_2_.refs_5_, ...), custom_call_target="tpu_custom_call" | custom-call | flops 274877906944 | bytes 503390208 | tf_op jit(solution)/shard_map/attend/pallas_call | solution.py:46
  106.4 2.2 pad_maximum_fusion.4.refs_13_
  108.6 2.2 pad_maximum_fusion.5.refs_14_
  111.9 16.5 %attend.3 = (bf16[512,1024]{1,0:T(8,128)(2,1)}, f32[32,512]{1,0:T(8,128)}, bf16[1024,3584]{1,0:T(8,128)(2,1)}, bf16[1024,1024]{1,0:T(8,128)(2,1)}) custom-call(bf16[512,1024]{1,0:T(8,128)(2,1)} %fusion.5.refs_1_.refs_0_, f32[512,128]{1,0:T(8,128)} %constant.32.clone.refs_1_.refs_4_, ...), custom_call_target="tpu_custom_call", output_to_operand_aliasing={{2}: (11, {}), {3}: (12, {})} | custom-call | flops 274877906944 | bytes 503390208 | tf_op jit(solution)/shard_map/attend/pallas_call | solution.py:46
  130.1 8.1 %collective-permute-done.16.refs_1_ = bf16[256,2304]{1,0:T(8,128)(2,1)} collective-permute-done((bf16[256,2304]{1,0:T(8,128)(2,1)}, bf16[256,2304]{1,0:T(8,128)(2,1)}, u32[]{:S(2)}, u32[]{:S(2)}) %collective-permute-start.16) | collective-permute-done | bytes 1179680 | tf_op jit(solution)/shard_map/ppermute | solution.py:447
  141.4 2.4 pad_maximum_fusion.1.refs_7_
  145.2 2.1 constant_dynamic-update-slice_fusion.refs_1_
  149.2 2.7 multiply_convert_fusion.refs_0_.refs_9_.refs_1_
  154.5 17.7 %mlp.2 = (bf16[512,1024]{1,0:T(8,128)(2,1)}, bf16[512,1024]{1,0:T(8,128)(2,1)}, f32[1,1024]{1,0:T(1,128)}, bf16[1024,3072]{1,0:T(8,128)(2,1)}, bf16[1024,1536]{1,0:T(8,128)(2,1)}) custom-call(bf16[512,1024]{1,0:T(8,128)(2,1)} %multiply_convert_fusion.refs_0_.refs_9_.refs_1_, bf16[512,1024]{1,0:T(8,128)(2,1)} %refs_1_.5, f32[1,1024]{1,0:T(1,128)} %bitcast.222, ...), custom_call_target="tpu_custom_call" | custom-call | flops 618475290624 | bytes 738467840 | tf_op jit(solution)/shard_map/mlp/pallas_call | solution.py:46
  172.2 2.6 turn.9.refs_3_.refs_2_
  174.8 2.6 turn.10.refs_3_
  177.4 18.3 %mlp.3 = (bf16[512,1024]{1,0:T(8,128)(2,1)}, bf16[512,1024]{1,0:T(8,128)(2,1)}, f32[1,1024]{1,0:T(1,128)}, bf16[1024,3072]{1,0:T(8,128)(2,1)}, bf16[1024,1536]{1,0:T(8,128)(2,1)}) custom-call(bf16[512,1024]{1,0:T(8,128)(2,1)} %get-tuple-element.139.refs_0_.refs_2_, ...), custom_call_target="tpu_custom_call", output_to_operand_aliasing={{3}: (9, {}), {4}: (10, {})} | custom-call | flops 618475290624 | bytes 738467840 | tf_op jit(solution)/shard_map/mlp/pallas_call | solution.py:46
  196.7 3.4 turn.11.refs_0_
  200.1 9.2 %weight_grads.4 = (bf16[512,2304]{1,0:T(8,128)(2,1)}, bf16[512,2304]{1,0:T(8,128)(2,1)}, f32[8,128]{1,0:T(8,128)}) custom-call(bf16[1024,1024]{1,0:T(8,128)(2,1)} %turn.11.refs_0_, bf16[1024,1024]{1,0:T(8,128)(2,1)} %get-tuple-element.144.refs_1_, bf16[1024,3072]{1,0:T(8,128)(2,1)} %get-tuple-element.145.refs_2_, ...), custom_call_target="tpu_custom_call" | custom-call | bytes 1 | tf_op jit(solution)/shard_map/weight_grads/pallas_call | solution.py:46
  209.4 11.2 %collective-permute-done.22.refs_1_ = bf16[512,1024]{1,0:T(8,128)(2,1)S(1)} collective-permute-done((bf16[512,1024]{1,0:T(8,128)(2,1)}, bf16[512,1024]{1,0:T(8,128)(2,1)S(1)}, u32[]{:S(2)}, u32[]{:S(2)}) %collective-permute-start.22) | collective-permute-done | bytes 1048608 | tf_op jit(solution)/shard_map/ppermute | solution.py:447
  221.6 2.6 multiply_reduce_fusion.1
  224.2 4.0 fusion.33
  228.2 9.1 %weight_grads.5 = (bf16[512,2304]{1,0:T(8,128)(2,1)}, bf16[512,2304]{1,0:T(8,128)(2,1)}, f32[8,128]{1,0:T(8,128)}) custom-call(bf16[1024,1024]{1,0:T(8,128)(2,1)} %turn.11.refs_0_, bf16[1024,1024]{1,0:T(8,128)(2,1)} %get-tuple-element.144.refs_1_, bf16[1024,3072]{1,0:T(8,128)(2,1)} %get-tuple-element.145.refs_2_, ...), custom_call_target="tpu_custom_call" | custom-call | flops 309237645312 | bytes 872415232 | tf_op jit(solution)/shard_map/weight_grads/pallas_call | solution.py:46
  238.8 2.7 turn.12.refs_3_
  243.5 2.7 add_convert_fusion.1
  250.6 20.8 %attend_back.2 = (bf16[512,1024]{1,0:T(8,128)(2,1)}, f32[8,128]{1,0:T(8,128)}, bf16[1024,2048]{1,0:T(8,128)(2,1)}) custom-call(bf16[512,1024]{1,0:T(8,128)(2,1)} %get-tuple-element.205.refs_4_.refs_1_.refs_0_, bf16[1024,3584]{1,0:T(8,128)(2,1)} %get-tuple-element.156.refs_1_, bf16[1024,1024]{1,0:T(8,128)(2,1)} %get-tuple-element.157.refs_2_.refs_3_, ...), custom_call_target="tpu_custom_call" | custom-call | flops 377957122048 | bytes 1111564288 | tf_op jit(solution)/shard_map/attend_back/pallas_call | solution.py:46
  271.4 3.2 collective-permute-done.24.refs_0_
  274.6 2.3 collective-permute-done.25.refs_1_
  277.0 2.2 fusion.35
  281.2 2.4 fusion.14.refs_16_
  284.7 2.5 fusion.15.refs_15_
  288.9 20.8 %attend_back.3 = (bf16[512,1024]{1,0:T(8,128)(2,1)}, f32[8,128]{1,0:T(8,128)}, bf16[1024,2048]{1,0:T(8,128)(2,1)}) custom-call(bf16[512,1024]{1,0:T(8,128)(2,1)} %get-tuple-element.165.refs_0_.refs_1_, bf16[1024,3584]{1,0:T(8,128)(2,1)} %get-tuple-element.156.refs_1_, ...), custom_call_target="tpu_custom_call", output_to_operand_aliasing={{2}: (14, {})} | custom-call | flops 377957122048 | bytes 1111564288 | tf_op jit(solution)/shard_map/attend_back/pallas_call | solution.py:46
  314.8 2.2 fusion.21.refs_4_.refs_5_
  318.3 2.6 turn.13.refs_1_
  320.9 7.3 %weight_grads.6 = (bf16[512,1536]{1,0:T(8,128)(2,1)}, bf16[512,1536]{1,0:T(8,128)(2,1)}, f32[8,128]{1,0:T(8,128)}) custom-call(bf16[1024,1024]{1,0:T(8,128)(2,1)} %get-tuple-element.171.refs_0_, bf16[1024,1024]{1,0:T(8,128)(2,1)} %turn.13.refs_1_, bf16[1024,2048]{1,0:T(8,128)(2,1)} %get-tuple-element.174.refs_2_, ...), custom_call_target="tpu_custom_call" | custom-call | bytes 1 | tf_op jit(solution)/shard_map/weight_grads/pallas_call | solution.py:46
  328.5 4.9 %collective-permute-done.30.refs_0_ = bf16[64,2304]{1,0:T(8,128)(2,1)S(1)} collective-permute-done((bf16[64,2304]{1,0:T(8,128)(2,1)S(1)}, bf16[64,2304]{1,0:T(8,128)(2,1)S(1)}, u32[]{:S(2)}, u32[]{:S(2)}) %collective-permute-start.30) | collective-permute-done | bytes 294944 | tf_op jit(solution)/shard_map/ppermute | solution.py:447
  335.4 7.6 %weight_grads.7 = (bf16[512,1536]{1,0:T(8,128)(2,1)}, bf16[512,1536]{1,0:T(8,128)(2,1)}, f32[8,128]{1,0:T(8,128)}) custom-call(bf16[1024,1024]{1,0:T(8,128)(2,1)} %get-tuple-element.171.refs_0_, bf16[1024,1024]{1,0:T(8,128)(2,1)} %turn.13.refs_1_, bf16[1024,2048]{1,0:T(8,128)(2,1)} %get-tuple-element.174.refs_2_, ...), custom_call_target="tpu_custom_call" | custom-call | flops 206158430208 | bytes 671088640 | tf_op jit(solution)/shard_map/weight_grads/pallas_call | solution.py:46
  344.1 2.7 collective-permute-done.33.refs_1_
  348.2 3.7 collective-permute-done.37.refs_2_
  361.4 16.7 %collective-permute-done.40.refs_2_ = bf16[64,2304]{1,0:T(8,128)(2,1)S(1)} collective-permute-done((bf16[64,2304]{1,0:T(8,128)(2,1)S(1)}, bf16[64,2304]{1,0:T(8,128)(2,1)S(1)}, u32[]{:S(2)}, u32[]{:S(2)}) %collective-permute-start.40) | collective-permute-done | bytes 294944 | tf_op jit(solution)/shard_map/ppermute | solution.py:447
  378.2 2.2 collective-permute-done.39.refs_1_
  395.2 2.6 collective-permute-done.42.refs_0_
  406.0 4.5 %fusion.10 = (bf16[512,1024]{1,0:T(8,128)(2,1)}, bf16[512,1024]{1,0:T(8,128)(2,1)}) fusion(f32[512,1024]{1,0:T(8,128)S(1)} %copy-done.21, bf16[512,1024]{1,0:T(8,128)(2,1)S(1)} %copy-done.4, bf16[512,1024]{1,0:T(8,128)(2,1)S(1)} %copy-done.9, bf16[512,1024]{1,0:T(8,128)(2,1)S(1)} %copy-done.12, f32[512]{0:T(512)S(1)} %broadcast_multiply_fusion, ...), kind=kLoop, calls=%fused_computation.19 | loop fusion | flops 12058624 | bytes 11542528 | tf_op jit(solution)/shard_map/convert_element_type | solution.py:747
  411.6 4.7 %collective-permute-done.45 = bf16[64,1536]{1,0:T(8,128)(2,1)S(1)} collective-permute-done((bf16[64,1536]{1,0:T(8,128)(2,1)S(1)}, bf16[64,1536]{1,0:T(8,128)(2,1)S(1)}, u32[]{:S(2)}, u32[]{:S(2)}) %collective-permute-start.45) | collective-permute-done | bytes 196640 | tf_op jit(solution)/shard_map/ppermute | solution.py:447
  417.5 2.7 collective-permute-done.44
  (376 shorter events, 119.2 us)
Async XLA Ops:
  4.7 21.3 %collective-permute-start.1 = (bf16[64,1536]{1,0:T(8,128)(2,1)S(1)}, bf16[64,1536]{1,0:T(8,128)(2,1)S(1)}, u32[]{:S(2)}, u32[]{:S(2)}) collective-permute-start(bf16[64,1536]{1,0:T(8,128)(2,1)S(1)} %get-tuple-element.222), channel_id=1, source_target_pairs={{0,16},{2,18},{4,20},{6,22},{8,24},{10,26},{12,28},{14,30},{16,0},... | collective-permute-start | bytes 589832 | tf_op jit(solution)/shard_map/ppermute | solution.py:447
  8.8 17.5 %collective-permute-start = (bf16[64,1536]{1,0:T(8,128)(2,1)S(1)}, bf16[64,1536]{1,0:T(8,128)(2,1)S(1)}, u32[]{:S(2)}, u32[]{:S(2)}) collective-permute-start(bf16[64,1536]{1,0:T(8,128)(2,1)S(1)} %get-tuple-element.223), channel_id=1, source_target_pairs={{0,16},{2,18},{4,20},{6,22},{8,24},{10,26},{12,28},{14,30},{16,0},... | collective-permute-start | bytes 589832 | tf_op jit(solution)/shard_map/ppermute | solution.py:447
  10.0 16.4 %collective-permute-start.2 = (bf16[256,1024]{1,0:T(8,128)(2,1)}, bf16[256,1024]{1,0:T(8,128)(2,1)S(1)}, u32[]{:S(2)}, u32[]{:S(2)}) collective-permute-start(bf16[256,1024]{1,0:T(8,128)(2,1)} %get-tuple-element.215), channel_id=1, source_target_pairs={{0,1},{1,0},{2,3},{3,2},{4,5},{5,4},{6,7},{7,6},{8,9},{9,8},{10,11... | collective-permute-start | bytes 1572872 | tf_op jit(solution)/shard_map/ppermute | solution.py:447
  29.3 10.4 %collective-permute-start.4 = (bf16[128,1536]{1,0:T(8,128)(2,1)S(1)}, bf16[128,1536]{1,0:T(8,128)(2,1)S(1)}, u32[]{:S(2)}, u32[]{:S(2)}) collective-permute-start(bf16[128,1536]{1,0:T(8,128)(2,1)S(1)} %pad_maximum_fusion.15), channel_id=1, source_target_pairs={{0,4},{2,6},{4,0},{6,2},{8,12},{10,14},{12,8},{14,10},{16,20},{18,... | collective-permute-start | bytes 1179656 | tf_op jit(solution)/shard_map/ppermute | solution.py:447
  30.9 9.7 %collective-permute-start.3 = (bf16[128,1536]{1,0:T(8,128)(2,1)S(1)}, bf16[128,1536]{1,0:T(8,128)(2,1)S(1)}, u32[]{:S(2)}, u32[]{:S(2)}) collective-permute-start(bf16[128,1536]{1,0:T(8,128)(2,1)S(1)} %pad_maximum_fusion.14), channel_id=1, source_target_pairs={{0,8},{2,10},{4,12},{6,14},{8,0},{10,2},{12,4},{14,6},{16,24},{18,... | collective-permute-start | bytes 1179656 | tf_op jit(solution)/shard_map/ppermute | solution.py:447
  32.1 41.0 %collective-permute-start.9 = (bf16[512,1024]{1,0:T(8,128)(2,1)S(1)}, bf16[512,1024]{1,0:T(8,128)(2,1)S(1)}, u32[]{:S(2)}, u32[]{:S(2)}) collective-permute-start(bf16[512,1024]{1,0:T(8,128)(2,1)S(1)} %copy-done.39), channel_id=1, source_target_pairs={{0,1},{1,0},{2,3},{3,2},{4,5},{5,4},{6,7},{7,6},{8,9},{9,8},{10,11... | collective-permute-start | bytes 3145736 | tf_op jit(solution)/shard_map/ppermute | solution.py:447
  43.5 30.4 %collective-permute-start.6 = (bf16[256,1536]{1,0:T(8,128)(2,1)S(1)}, bf16[256,1536]{1,0:T(8,128)(2,1)S(1)}, u32[]{:S(2)}, u32[]{:S(2)}) collective-permute-start(bf16[256,1536]{1,0:T(8,128)(2,1)S(1)} %pad_maximum_fusion.9), channel_id=1, source_target_pairs={{0,8},{2,10},{4,12},{6,14},{8,0},{10,2},{12,4},{14,6},{16,24},{18,... | collective-permute-start | bytes 2359304 | tf_op jit(solution)/shard_map/ppermute | solution.py:447
  45.3 28.6 %collective-permute-start.5 = (bf16[256,1536]{1,0:T(8,128)(2,1)S(1)}, bf16[256,1536]{1,0:T(8,128)(2,1)S(1)}, u32[]{:S(2)}, u32[]{:S(2)}) collective-permute-start(bf16[256,1536]{1,0:T(8,128)(2,1)S(1)} %pad_maximum_fusion.8), channel_id=1, source_target_pairs={{0,4},{2,6},{4,0},{6,2},{8,12},{10,14},{12,8},{14,10},{16,20},{18,... | collective-permute-start | bytes 2359304 | tf_op jit(solution)/shard_map/ppermute | solution.py:447
  46.3 42.3 %copy-start.33 = (bf16[64,2304]{1,0:T(8,128)(2,1)}, bf16[64,2304]{1,0:T(8,128)(2,1)S(1)}, u32[]{:S(2)}) copy-start(bf16[64,2304]{1,0:T(8,128)(2,1)S(1)} %get-tuple-element.220) | copy-start | bytes 884740
  46.4 23.2 %collective-permute-start.8 = (bf16[64,2304]{1,0:T(8,128)(2,1)S(1)}, bf16[64,2304]{1,0:T(8,128)(2,1)S(1)}, u32[]{:S(2)}, u32[]{:S(2)}) collective-permute-start(bf16[64,2304]{1,0:T(8,128)(2,1)S(1)} %get-tuple-element.220), channel_id=1, source_target_pairs={{0,16},{2,18},{4,20},{6,22},{8,24},{10,26},{12,28},{14,30},{16,0},... | collective-permute-start | bytes 884744 | tf_op jit(solution)/shard_map/ppermute | solution.py:447
  49.8 23.3 %collective-permute-start.7 = (bf16[64,2304]{1,0:T(8,128)(2,1)S(1)}, bf16[64,2304]{1,0:T(8,128)(2,1)S(1)}, u32[]{:S(2)}, u32[]{:S(2)}) collective-permute-start(bf16[64,2304]{1,0:T(8,128)(2,1)S(1)} %get-tuple-element.221), channel_id=1, source_target_pairs={{0,16},{2,18},{4,20},{6,22},{8,24},{10,26},{12,28},{14,30},{16,0},... | collective-permute-start | bytes 884744 | tf_op jit(solution)/shard_map/ppermute | solution.py:447
  77.3 10.2 %collective-permute-start.13 = (bf16[512,1536]{1,0:T(8,128)(2,1)S(1)}, bf16[512,1536]{1,0:T(8,128)(2,1)S(1)}, u32[]{:S(2)}, u32[]{:S(2)}) collective-permute-start(bf16[512,1536]{1,0:T(8,128)(2,1)S(1)} %pad_maximum_fusion.3.refs_9_.refs_12_), channel_id=1, source_target_pairs={{0,2},{2,0},{4,6},{6,4},{8,10},{10,8},{12,14},{14,12},{16,18},{18,... | collective-permute-start | bytes 4718600 | tf_op jit(solution)/shard_map/ppermute | solution.py:447
  77.4 10.1 %collective-permute-start.12 = (bf16[512,1536]{1,0:T(8,128)(2,1)S(1)}, bf16[512,1536]{1,0:T(8,128)(2,1)}, u32[]{:S(2)}, u32[]{:S(2)}) collective-permute-start(bf16[512,1536]{1,0:T(8,128)(2,1)S(1)} %pad_maximum_fusion.2.refs_6_.refs_9_), channel_id=1, source_target_pairs={{0,2},{2,0},{4,6},{6,4},{8,10},{10,8},{12,14},{14,12},{16,18},{18,... | collective-permute-start | bytes 4718600 | tf_op jit(solution)/shard_map/ppermute | solution.py:447
  77.9 27.5 %collective-permute-start.14 = (bf16[256,1024]{1,0:T(8,128)(2,1)}, bf16[256,1024]{1,0:T(8,128)(2,1)}, u32[]{:S(2)}, u32[]{:S(2)}) collective-permute-start(bf16[256,1024]{1,0:T(8,128)(2,1)} %get-tuple-element.214), channel_id=1, source_target_pairs={{0,1},{1,0},{2,3},{3,2},{4,5},{5,4},{6,7},{7,6},{8,9},{9,8},{10,11... | collective-permute-start | bytes 1572872 | tf_op jit(solution)/shard_map/ppermute | solution.py:447
  81.4 24.0 %collective-permute-start.11 = (bf16[128,2304]{1,0:T(8,128)(2,1)}, bf16[128,2304]{1,0:T(8,128)(2,1)}, u32[]{:S(2)}, u32[]{:S(2)}) collective-permute-start(bf16[128,2304]{1,0:T(8,128)(2,1)} %pad_maximum_fusion.12.refs_12_), channel_id=1, source_target_pairs={{0,4},{2,6},{4,0},{6,2},{8,12},{10,14},{12,8},{14,10},{16,20},{18,... | collective-permute-start | bytes 1769480 | tf_op jit(solution)/shard_map/ppermute | solution.py:447
  83.6 21.8 %collective-permute-start.10 = (bf16[128,2304]{1,0:T(8,128)(2,1)}, bf16[128,2304]{1,0:T(8,128)(2,1)}, u32[]{:S(2)}, u32[]{:S(2)}) collective-permute-start(bf16[128,2304]{1,0:T(8,128)(2,1)} %pad_maximum_fusion.11.refs_11_), channel_id=1, source_target_pairs={{0,8},{2,10},{4,12},{6,14},{8,0},{10,2},{12,4},{14,6},{16,24},{18,... | collective-permute-start | bytes 1769480 | tf_op jit(solution)/shard_map/ppermute | solution.py:447
  105.4 24.7 %collective-permute-start.17 = (bf16[512,1024]{1,0:T(8,128)(2,1)}, bf16[512,1024]{1,0:T(8,128)(2,1)}, u32[]{:S(2)}, u32[]{:S(2)}) collective-permute-start(bf16[512,1024]{1,0:T(8,128)(2,1)} %get-tuple-element.127), channel_id=1, source_target_pairs={{0,1},{1,0},{2,3},{3,2},{4,5},{5,4},{6,7},{7,6},{8,9},{9,8},{10,11... | collective-permute-start | bytes 3145736 | tf_op jit(solution)/shard_map/ppermute | solution.py:447
  110.8 27.4 %collective-permute-start.16 = (bf16[256,2304]{1,0:T(8,128)(2,1)}, bf16[256,2304]{1,0:T(8,128)(2,1)}, u32[]{:S(2)}, u32[]{:S(2)}) collective-permute-start(bf16[256,2304]{1,0:T(8,128)(2,1)} %pad_maximum_fusion.5.refs_14_), channel_id=1, source_target_pairs={{0,8},{2,10},{4,12},{6,14},{8,0},{10,2},{12,4},{14,6},{16,24},{18,... | collective-permute-start | bytes 3538952 | tf_op jit(solution)/shard_map/ppermute | solution.py:447
  110.8 27.8 %collective-permute-start.15 = (bf16[256,2304]{1,0:T(8,128)(2,1)}, bf16[256,2304]{1,0:T(8,128)(2,1)}, u32[]{:S(2)}, u32[]{:S(2)}) collective-permute-start(bf16[256,2304]{1,0:T(8,128)(2,1)} %pad_maximum_fusion.4.refs_13_), channel_id=1, source_target_pairs={{0,4},{2,6},{4,0},{6,2},{8,12},{10,14},{12,8},{14,10},{16,20},{18,... | collective-permute-start | bytes 3538952 | tf_op jit(solution)/shard_map/ppermute | solution.py:447
  143.8 9.3 %collective-permute-start.19 = (bf16[512,2304]{1,0:T(8,128)(2,1)S(1)}, bf16[512,2304]{1,0:T(8,128)(2,1)S(1)}, u32[]{:S(2)}, u32[]{:S(2)}) collective-permute-start(bf16[512,2304]{1,0:T(8,128)(2,1)S(1)} %pad_maximum_fusion.1.refs_7_), channel_id=1, source_target_pairs={{0,2},{2,0},{4,6},{6,4},{8,10},{10,8},{12,14},{14,12},{16,18},{18,... | collective-permute-start | bytes 7077896 | tf_op jit(solution)/shard_map/ppermute | solution.py:447
  143.9 9.2 %collective-permute-start.18 = (bf16[512,2304]{1,0:T(8,128)(2,1)S(1)}, bf16[512,2304]{1,0:T(8,128)(2,1)}, u32[]{:S(2)}, u32[]{:S(2)}) collective-permute-start(bf16[512,2304]{1,0:T(8,128)(2,1)S(1)} %pad_maximum_fusion.refs_4_), channel_id=1, source_target_pairs={{0,2},{2,0},{4,6},{6,4},{8,10},{10,8},{12,14},{14,12},{16,18},{18,... | collective-permute-start | bytes 7077896 | tf_op jit(solution)/shard_map/ppermute | solution.py:447
  151.9 25.4 %collective-permute-start.20 = (bf16[512,1024]{1,0:T(8,128)(2,1)}, bf16[512,1024]{1,0:T(8,128)(2,1)}, u32[]{:S(2)}, u32[]{:S(2)}) collective-permute-start(bf16[512,1024]{1,0:T(8,128)(2,1)} %multiply_convert_fusion.refs_0_.refs_9_.refs_1_), channel_id=1, source_target_pairs={{0,1},{1,0},{2,3},{3,2},{4,5},{5,4},{6,7},{7,6},{8,9},{9,8},{10,11... | collective-permute-start | bytes 3145736 | tf_op jit(solution)/shard_map/ppermute | solution.py:447
  195.6 24.9 %collective-permute-start.22 = (bf16[512,1024]{1,0:T(8,128)(2,1)}, bf16[512,1024]{1,0:T(8,128)(2,1)S(1)}, u32[]{:S(2)}, u32[]{:S(2)}) collective-permute-start(bf16[512,1024]{1,0:T(8,128)(2,1)} %get-tuple-element.143.refs_3_.refs_4_), channel_id=1, source_target_pairs={{0,1},{1,0},{2,3},{3,2},{4,5},{5,4},{6,7},{7,6},{8,9},{9,8},{10,11... | collective-permute-start | bytes 3145736 | tf_op jit(solution)/shard_map/ppermute | solution.py:447
  209.4 32.1 %collective-permute-start.21 = (bf16[512,2304]{1,0:T(8,128)(2,1)}, bf16[512,2304]{1,0:T(8,128)(2,1)}, u32[]{:S(2)}, u32[]{:S(2)}) collective-permute-start(bf16[512,2304]{1,0:T(8,128)(2,1)} %get-tuple-element.148), channel_id=1, source_target_pairs={{0,2},{2,0},{4,6},{6,4},{8,10},{10,8},{12,14},{14,12},{16,18},{18,... | collective-permute-start | bytes 7077896 | tf_op jit(solution)/shard_map/ppermute | solution.py:447
  237.3 4.7 %collective-permute-start.23 = (bf16[512,2304]{1,0:T(8,128)(2,1)}, bf16[512,2304]{1,0:T(8,128)(2,1)S(1)}, u32[]{:S(2)}, u32[]{:S(2)}) collective-permute-start(bf16[512,2304]{1,0:T(8,128)(2,1)} %get-tuple-element.151), channel_id=1, source_target_pairs={{0,2},{2,0},{4,6},{6,4},{8,10},{10,8},{12,14},{14,12},{16,18},{18,... | collective-permute-start | bytes 7077896 | tf_op jit(solution)/shard_map/ppermute | solution.py:447
  238.0 33.4 %collective-permute-start.26 = (bf16[512,1024]{1,0:T(8,128)(2,1)}, bf16[512,1024]{1,0:T(8,128)(2,1)}, u32[]{:S(2)}, u32[]{:S(2)}) collective-permute-start(bf16[512,1024]{1,0:T(8,128)(2,1)} %get-tuple-element.205.refs_4_.refs_1_.refs_0_), channel_id=1, source_target_pairs={{0,1},{1,0},{2,3},{3,2},{4,5},{5,4},{6,7},{7,6},{8,9},{9,8},{10,11... | collective-permute-start | bytes 3145736 | tf_op jit(solution)/shard_map/ppermute | solution.py:447
  246.2 28.4 %collective-permute-start.24 = (bf16[2,2,64,2304]{3,2,1,0:T(8,128)(2,1)}, bf16[2,2,64,2304]{3,2,1,0:T(8,128)(2,1)}, u32[]{:S(2)}, u32[]{:S(2)}) collective-permute-start(bf16[2,2,64,2304]{3,2,1,0:T(8,128)(2,1)} %bitcast.8.refs_16_), channel_id=1, source_target_pairs={{0,4},{2,6},{4,0},{6,2},{8,12},{10,14},{12,8},{14,10},{16,20},{18,... | collective-permute-start | bytes 3538952 | tf_op jit(solution)/shard_map/ppermute | solution.py:447
  248.6 28.4 %collective-permute-start.25 = (bf16[2,2,64,2304]{3,2,1,0:T(8,128)(2,1)}, bf16[2,2,64,2304]{3,2,1,0:T(8,128)(2,1)}, u32[]{:S(2)}, u32[]{:S(2)}) collective-permute-start(bf16[2,2,64,2304]{3,2,1,0:T(8,128)(2,1)} %fusion.13.refs_17_), channel_id=1, source_target_pairs={{0,8},{2,10},{4,12},{6,14},{8,0},{10,2},{12,4},{14,6},{16,24},{18,... | collective-permute-start | bytes 3538952 | tf_op jit(solution)/shard_map/ppermute | solution.py:447
  279.2 49.3 %collective-permute-start.32 = (bf16[256,1024]{1,0:T(8,128)(2,1)}, bf16[256,1024]{1,0:T(8,128)(2,1)}, u32[]{:S(2)}, u32[]{:S(2)}) collective-permute-start(bf16[256,1024]{1,0:T(8,128)(2,1)} %get-tuple-element.212), channel_id=1, source_target_pairs={{0,1},{1,0},{2,3},{3,2},{4,5},{5,4},{6,7},{7,6},{8,9},{9,8},{10,11... | collective-permute-start | bytes 1572872 | tf_op jit(solution)/shard_map/ppermute | solution.py:447
  280.9 30.1 %collective-permute-start.29 = (bf16[256,1024]{1,0:T(8,128)(2,1)}, bf16[256,1024]{1,0:T(8,128)(2,1)}, u32[]{:S(2)}, u32[]{:S(2)}) collective-permute-start(bf16[256,1024]{1,0:T(8,128)(2,1)} %get-tuple-element.213), channel_id=1, source_target_pairs={{0,1},{1,0},{2,3},{3,2},{4,5},{5,4},{6,7},{7,6},{8,9},{9,8},{10,11... | collective-permute-start | bytes 1572872 | tf_op jit(solution)/shard_map/ppermute | solution.py:447
  283.7 27.3 %collective-permute-start.28 = (bf16[2,64,2304]{2,1,0:T(8,128)(2,1)}, bf16[2,64,2304]{2,1,0:T(8,128)(2,1)}, u32[]{:S(2)}, u32[]{:S(2)}) collective-permute-start(bf16[2,64,2304]{2,1,0:T(8,128)(2,1)} %fusion.14.refs_16_), channel_id=1, source_target_pairs={{0,4},{2,6},{4,0},{6,2},{8,12},{10,14},{12,8},{14,10},{16,20},{18,... | collective-permute-start | bytes 1769480 | tf_op jit(solution)/shard_map/ppermute | solution.py:447
  287.2 23.8 %collective-permute-start.27 = (bf16[2,64,2304]{2,1,0:T(8,128)(2,1)}, bf16[2,64,2304]{2,1,0:T(8,128)(2,1)}, u32[]{:S(2)}, u32[]{:S(2)}) collective-permute-start(bf16[2,64,2304]{2,1,0:T(8,128)(2,1)} %fusion.15.refs_15_), channel_id=1, source_target_pairs={{0,8},{2,10},{4,12},{6,14},{8,0},{10,2},{12,4},{14,6},{16,24},{18,... | collective-permute-start | bytes 1769480 | tf_op jit(solution)/shard_map/ppermute | solution.py:447
  313.3 15.1 %collective-permute-start.31 = (f32[18,128]{1,0:T(8,128)S(1)}, f32[18,128]{1,0:T(8,128)S(1)}, u32[]{:S(2)}, u32[]{:S(2)}) collective-permute-start(f32[18,128]{1,0:T(8,128)S(1)} %maximum_bitcast_fusion.refs_6_), channel_id=1, source_target_pairs={{0,2},{2,0},{4,6},{6,4},{8,10},{10,8},{12,14},{14,12},{16,18},{18,... | collective-permute-start | bytes 27656 | tf_op jit(solution)/shard_map/ppermute | solution.py:447
  317.0 16.3 %collective-permute-start.30 = (bf16[64,2304]{1,0:T(8,128)(2,1)S(1)}, bf16[64,2304]{1,0:T(8,128)(2,1)S(1)}, u32[]{:S(2)}, u32[]{:S(2)}) collective-permute-start(bf16[64,2304]{1,0:T(8,128)(2,1)S(1)} %fusion.22.refs_3_.refs_4_), channel_id=1, source_target_pairs={{0,16},{2,18},{4,20},{6,22},{8,24},{10,26},{12,28},{14,30},{16,0},... | collective-permute-start | bytes 884744 | tf_op jit(solution)/shard_map/ppermute | solution.py:447
  328.3 23.7 %collective-permute-start.35 = (bf16[512,1536]{1,0:T(8,128)(2,1)}, bf16[512,1536]{1,0:T(8,128)(2,1)}, u32[]{:S(2)}, u32[]{:S(2)}) collective-permute-start(bf16[512,1536]{1,0:T(8,128)(2,1)} %get-tuple-element.189), channel_id=1, source_target_pairs={{0,2},{2,0},{4,6},{6,4},{8,10},{10,8},{12,14},{14,12},{16,18},{18,... | collective-permute-start | bytes 4718600 | tf_op jit(solution)/shard_map/ppermute | solution.py:447
  343.0 8.9 %collective-permute-start.36 = (bf16[512,1536]{1,0:T(8,128)(2,1)}, bf16[512,1536]{1,0:T(8,128)(2,1)S(1)}, u32[]{:S(2)}, u32[]{:S(2)}) collective-permute-start(bf16[512,1536]{1,0:T(8,128)(2,1)} %get-tuple-element.190), channel_id=1, source_target_pairs={{0,2},{2,0},{4,6},{6,4},{8,10},{10,8},{12,14},{14,12},{16,18},{18,... | collective-permute-start | bytes 4718600 | tf_op jit(solution)/shard_map/ppermute | solution.py:447
  343.1 3.7 collective-permute-start.33
  348.1 3.8 collective-permute-start.37
  355.2 23.0 %collective-permute-start.38 = (bf16[2,2,64,1536]{3,2,1,0:T(8,128)(2,1)S(1)}, bf16[2,2,64,1536]{3,2,1,0:T(8,128)(2,1)S(1)}, u32[]{:S(2)}, u32[]{:S(2)}) collective-permute-start(bf16[2,2,64,1536]{3,2,1,0:T(8,128)(2,1)S(1)} %bitcast.207), channel_id=1, source_target_pairs={{0,4},{2,6},{4,0},{6,2},{8,12},{10,14},{12,8},{14,10},{16,20},{18,... | collective-permute-start | bytes 2359304 | tf_op jit(solution)/shard_map/ppermute | solution.py:447
  356.4 24.0 %collective-permute-start.39 = (bf16[2,2,64,1536]{3,2,1,0:T(8,128)(2,1)S(1)}, bf16[2,2,64,1536]{3,2,1,0:T(8,128)(2,1)S(1)}, u32[]{:S(2)}, u32[]{:S(2)}) collective-permute-start(bf16[2,2,64,1536]{3,2,1,0:T(8,128)(2,1)S(1)} %fusion.16), channel_id=1, source_target_pairs={{0,8},{2,10},{4,12},{6,14},{8,0},{10,2},{12,4},{14,6},{16,24},{18,... | collective-permute-start | bytes 2359304 | tf_op jit(solution)/shard_map/ppermute | solution.py:447
  356.5 21.5 %collective-permute-start.40 = (bf16[64,2304]{1,0:T(8,128)(2,1)S(1)}, bf16[64,2304]{1,0:T(8,128)(2,1)S(1)}, u32[]{:S(2)}, u32[]{:S(2)}) collective-permute-start(bf16[64,2304]{1,0:T(8,128)(2,1)S(1)} %copy-done.68), channel_id=1, source_target_pairs={{0,16},{2,18},{4,20},{6,22},{8,24},{10,26},{12,28},{14,30},{16,0},... | collective-permute-start | bytes 884744 | tf_op jit(solution)/shard_map/ppermute | solution.py:447
  358.1 36.8 %collective-permute-start.34 = (bf16[512,1024]{1,0:T(8,128)(2,1)}, bf16[512,1024]{1,0:T(8,128)(2,1)S(1)}, u32[]{:S(2)}, u32[]{:S(2)}) collective-permute-start(bf16[512,1024]{1,0:T(8,128)(2,1)} %get-tuple-element.176), channel_id=1, source_target_pairs={{0,1},{1,0},{2,3},{3,2},{4,5},{5,4},{6,7},{7,6},{8,9},{9,8},{10,11... | collective-permute-start | bytes 3145736 | tf_op jit(solution)/shard_map/ppermute | solution.py:447
  359.7 18.5 %collective-permute-start.41 = (f32[18,128]{1,0:T(8,128)S(1)}, f32[18,128]{1,0:T(8,128)S(1)}, u32[]{:S(2)}, u32[]{:S(2)}) collective-permute-start(f32[18,128]{1,0:T(8,128)S(1)} %add.299), channel_id=1, source_target_pairs={{0,16},{2,18},{4,20},{6,22},{8,24},{10,26},{12,28},{14,30},{16,0},... | collective-permute-start | bytes 27656 | tf_op jit(solution)/shard_map/ppermute | solution.py:447
  384.9 10.3 %collective-permute-start.43 = (bf16[2,64,1536]{2,1,0:T(8,128)(2,1)}, bf16[2,64,1536]{2,1,0:T(8,128)(2,1)}, u32[]{:S(2)}, u32[]{:S(2)}) collective-permute-start(bf16[2,64,1536]{2,1,0:T(8,128)(2,1)} %fusion.17.refs_2_), channel_id=1, source_target_pairs={{0,4},{2,6},{4,0},{6,2},{8,12},{10,14},{12,8},{14,10},{16,20},{18,... | collective-permute-start | bytes 1179656 | tf_op jit(solution)/shard_map/ppermute | solution.py:447
  387.8 10.0 %collective-permute-start.42 = (bf16[2,64,1536]{2,1,0:T(8,128)(2,1)}, bf16[2,64,1536]{2,1,0:T(8,128)(2,1)}, u32[]{:S(2)}, u32[]{:S(2)}) collective-permute-start(bf16[2,64,1536]{2,1,0:T(8,128)(2,1)} %fusion.18.refs_1_), channel_id=1, source_target_pairs={{0,8},{2,10},{4,12},{6,14},{8,0},{10,2},{12,4},{14,6},{16,24},{18,... | collective-permute-start | bytes 1179656 | tf_op jit(solution)/shard_map/ppermute | solution.py:447
  399.9 10.6 %collective-permute-start.46 = (f32[18,128]{1,0:T(8,128)}, f32[18,128]{1,0:T(8,128)S(1)}, u32[]{:S(2)}, u32[]{:S(2)}) collective-permute-start(f32[18,128]{1,0:T(8,128)} %get-tuple-element.204), channel_id=1, source_target_pairs={{0,1},{1,0},{2,3},{3,2},{4,5},{5,4},{6,7},{7,6},{8,9},{9,8},{10,11... | collective-permute-start | bytes 27656 | tf_op jit(solution)/shard_map/ppermute | solution.py:447
  403.0 13.3 %collective-permute-start.45 = (bf16[64,1536]{1,0:T(8,128)(2,1)S(1)}, bf16[64,1536]{1,0:T(8,128)(2,1)S(1)}, u32[]{:S(2)}, u32[]{:S(2)}) collective-permute-start(bf16[64,1536]{1,0:T(8,128)(2,1)S(1)} %fusion.23), channel_id=1, source_target_pairs={{0,16},{2,18},{4,20},{6,22},{8,24},{10,26},{12,28},{14,30},{16,0},... | collective-permute-start | bytes 589832 | tf_op jit(solution)/shard_map/ppermute | solution.py:447
  403.9 16.4 %collective-permute-start.44 = (bf16[64,1536]{1,0:T(8,128)(2,1)S(1)}, bf16[64,1536]{1,0:T(8,128)(2,1)S(1)}, u32[]{:S(2)}, u32[]{:S(2)}) collective-permute-start(bf16[64,1536]{1,0:T(8,128)(2,1)S(1)} %fusion.25), channel_id=1, source_target_pairs={{0,16},{2,18},{4,20},{6,22},{8,24},{10,26},{12,28},{14,30},{16,0},... | collective-permute-start | bytes 589832 | tf_op jit(solution)/shard_map/ppermute | solution.py:447
  (103 other events, 743.1 us)

commit v5 on v4

--- a/solution.py
+++ b/solution.py
@@ -726,12 +726,13 @@
     hops += [("tensor", tensor_size, 1 << bit) for bit in range(tensor_size.bit_length() - 1)]
     attn_sums, after = [], [*after, sums]
     for index, cut in enumerate(attn_cuts):
-        sums_got = exchange(sums, *hops.pop(0))
+        sums_got = exchange(sums, *hops.pop(0)) if index == 0 else None
         keep, send, token = weight_grads(*normed_t, *attended_t, *dproj, head_out, heads, *cut, after, index > 0)
         attn_sums.append(BlockSum(dp_size, keep, send, orders[index]))
-        token, sums_got, ffn_rest = arrive([] if index else mlp_sums[:1], token, sums_got, ffn_rest)
-        sums = sums + sums_got
-        after = [token, sums]
+        if index == 0:
+            token, sums_got, ffn_rest = arrive(mlp_sums[:1], token, sums_got, ffn_rest)
+            sums = sums + sums_got
+        after = [token]
     ffn_got = jnp.concatenate([ffn_first, ffn_rest], axis=0) if by_pair else ffn_rest
 
     sums_got = exchange(sums, *hops.pop(0))
@@ -739,13 +740,15 @@
     sums = sums + sums_got
     sent = [block_sum.halve() for block_sum in attn_sums]
     sums_got = exchange(sums, *hops.pop(0))
-    (sums_got,) = arrive([*attn_sums, *mlp_sums[1:]], sums_got)
+    (sums_got,) = arrive(attn_sums, sums_got)
     sums = sums + sums_got
     sent = [block_sum.halve() for block_sum in attn_sums]
     dx_got, *_ = sync(dx_got, *sent)
     grad_normed = add_sum(dx_parts, dx_got)
     grad_inputs = (grad_middle + norm_back(unit_in, scale_in, grad_normed * gain_attn)).astype(BF16)
-    (sums,) = arrive(attn_sums, sums)
+    sums_got = exchange(sums, *hops.pop(0))
+    (sums_got,) = arrive([*attn_sums, *mlp_sums[1:]], sums_got)
+    sums = sums + sums_got
     while any(block_sum.flips for block_sum in attn_sums):
         for block_sum in attn_sums:
             block_sum.halve()

time: 430 us -> 432 us (level)
    unnamed x218 -> x220, local copies, waits for them, and re-layouts: 22.1 us -> 24.1 us
    pallas_call x35 -> x34, Pallas kernels: 163 us -> 163 us  [kernel_call(): pl.pallas_call(run, grid=grid, in_specs=[spec for _, spec in inputs] + [p...]
  transfers between devices with their start and end apart: 47 -> 47, of which waited for: 23 -> 19; matrix products, arithmetic and copies ran while one was open for 17% -> 17% of each run, Pallas kernels for 34% -> 34%
where the time goes in v5:
time: 432 us; the launch traced here: 427 us
  Pallas kernels  163 us (38%)
  waiting for transfers between devices  100 us (23%)
  other arithmetic  72.7 us (17%)
  starting transfers between devices  50.7 us (12%)
  local copies, waits for them, and re-layouts  38.4 us (9%)
    pallas_call x34, Pallas kernels, kernel_call(): pl.pallas_call(run, grid=grid, in_specs=[spec for _, spec in inputs] + [p...  163 us
    ppermute x47, waiting for transfers between devices, exchange(): lax.ppermute(array, axis, [(index, index ^ flip) for index in range(size)])  100 us
    ppermute x47, starting transfers between devices, exchange(): lax.ppermute(array, axis, [(index, index ^ flip) for index in range(size)])  50.7 us
    unnamed x220, local copies, waits for them, and re-layouts  24.1 us
    convert_element_type x12, other arithmetic, halve(): sent = self.part(flip).astype(BF16)  21.5 us
    concatenate x12, other arithmetic, join(): self.held = jnp.concatenate([self.held, self.got], axis=0)  15.7 us
  transfers between devices with their start and end apart: 47, of which 19 were waited for; matrix products, arithmetic and copies ran while one was open for 17% of the time, Pallas kernels for 34%

profile of v5, /device:TPU:0, one launch (start us, length us, event | category | flops | bytes accessed | tf_op | source)
XLA Modules:
  0.0 427.1 jit_solution(2506860977968813195)
XLA Ops:
  4.8 4.1 collective-permute-start.1
  14.4 2.6 turn.7.refs_4_
  18.3 2.6 turn.8.refs_5_
  20.9 2.2 collective-permute-done.1.refs_1_
  23.0 3.4 collective-permute-done.refs_0_
  33.1 6.6 %collective-permute-done.4.refs_1_ = bf16[128,1536]{1,0:T(8,128)(2,1)S(1)} collective-permute-done((bf16[128,1536]{1,0:T(8,128)(2,1)S(1)}, bf16[128,1536]{1,0:T(8,128)(2,1)S(1)}, u32[]{:S(2)}, u32[]{:S(2)}) %collective-permute-start.4) | collective-permute-done | bytes 393248 | tf_op jit(solution)/shard_map/ppermute | solution.py:447
  46.4 3.4 collective-permute-start.8
  49.9 19.7 %collective-permute-done.8.refs_3_ = bf16[64,2304]{1,0:T(8,128)(2,1)S(1)} collective-permute-done((bf16[64,2304]{1,0:T(8,128)(2,1)S(1)}, bf16[64,2304]{1,0:T(8,128)(2,1)S(1)}, u32[]{:S(2)}, u32[]{:S(2)}) %collective-permute-start.8) | collective-permute-done | bytes 294944 | tf_op jit(solution)/shard_map/ppermute | solution.py:447
  69.6 4.1 collective-permute-done.7.refs_2_
  83.6 3.8 collective-permute-start.10
  88.6 16.7 %attend.2 = (bf16[512,1024]{1,0:T(8,128)(2,1)}, f32[32,512]{1,0:T(8,128)}, bf16[1024,3584]{1,0:T(8,128)(2,1)}, bf16[1024,1024]{1,0:T(8,128)(2,1)}) custom-call(bf16[512,1024]{1,0:T(8,128)(2,1)} %get-tuple-element.113.refs_0_.refs_1_, f32[512,128]{1,0:T(8,128)} %constant.32.clone.refs_1_.refs_4_, f32[512,128]{1,0:T(8,128)} %constant.33.clone.refs_2_.refs_5_, ...), custom_call_target="tpu_custom_call" | custom-call | flops 274877906944 | bytes 503390208 | tf_op jit(solution)/shard_map/attend/pallas_call | solution.py:46
  106.4 2.2 pad_maximum_fusion.4.refs_13_
  108.6 2.2 pad_maximum_fusion.5.refs_14_
  111.9 16.5 %attend.3 = (bf16[512,1024]{1,0:T(8,128)(2,1)}, f32[32,512]{1,0:T(8,128)}, bf16[1024,3584]{1,0:T(8,128)(2,1)}, bf16[1024,1024]{1,0:T(8,128)(2,1)}) custom-call(bf16[512,1024]{1,0:T(8,128)(2,1)} %fusion.5.refs_1_.refs_0_, f32[512,128]{1,0:T(8,128)} %constant.32.clone.refs_1_.refs_4_, ...), custom_call_target="tpu_custom_call", output_to_operand_aliasing={{2}: (11, {}), {3}: (12, {})} | custom-call | flops 274877906944 | bytes 503390208 | tf_op jit(solution)/shard_map/attend/pallas_call | solution.py:46
  130.2 8.1 %collective-permute-done.16.refs_1_ = bf16[256,2304]{1,0:T(8,128)(2,1)} collective-permute-done((bf16[256,2304]{1,0:T(8,128)(2,1)}, bf16[256,2304]{1,0:T(8,128)(2,1)}, u32[]{:S(2)}, u32[]{:S(2)}) %collective-permute-start.16) | collective-permute-done | bytes 1179680 | tf_op jit(solution)/shard_map/ppermute | solution.py:447
  141.4 2.4 pad_maximum_fusion.1.refs_7_
  149.2 2.7 multiply_convert_fusion.refs_0_.refs_9_.refs_1_
  154.5 17.7 %mlp.2 = (bf16[512,1024]{1,0:T(8,128)(2,1)}, bf16[512,1024]{1,0:T(8,128)(2,1)}, f32[1,1024]{1,0:T(1,128)}, bf16[1024,3072]{1,0:T(8,128)(2,1)}, bf16[1024,1536]{1,0:T(8,128)(2,1)}) custom-call(bf16[512,1024]{1,0:T(8,128)(2,1)} %multiply_convert_fusion.refs_0_.refs_9_.refs_1_, bf16[512,1024]{1,0:T(8,128)(2,1)} %refs_1_.5, f32[1,1024]{1,0:T(1,128)} %bitcast.222, ...), custom_call_target="tpu_custom_call" | custom-call | flops 618475290624 | bytes 738467840 | tf_op jit(solution)/shard_map/mlp/pallas_call | solution.py:46
  172.2 2.6 turn.9.refs_3_.refs_2_
  174.8 2.6 turn.10.refs_3_
  177.4 18.3 %mlp.3 = (bf16[512,1024]{1,0:T(8,128)(2,1)}, bf16[512,1024]{1,0:T(8,128)(2,1)}, f32[1,1024]{1,0:T(1,128)}, bf16[1024,3072]{1,0:T(8,128)(2,1)}, bf16[1024,1536]{1,0:T(8,128)(2,1)}) custom-call(bf16[512,1024]{1,0:T(8,128)(2,1)} %get-tuple-element.136.refs_0_.refs_2_, ...), custom_call_target="tpu_custom_call", output_to_operand_aliasing={{3}: (9, {}), {4}: (10, {})} | custom-call | flops 618475290624 | bytes 738467840 | tf_op jit(solution)/shard_map/mlp/pallas_call | solution.py:46
  196.7 3.5 turn.11.refs_0_
  200.2 9.3 %weight_grads.4 = (bf16[512,2304]{1,0:T(8,128)(2,1)}, bf16[512,2304]{1,0:T(8,128)(2,1)}, f32[8,128]{1,0:T(8,128)}) custom-call(bf16[1024,1024]{1,0:T(8,128)(2,1)} %turn.11.refs_0_, bf16[1024,1024]{1,0:T(8,128)(2,1)} %get-tuple-element.141.refs_1_, bf16[1024,3072]{1,0:T(8,128)(2,1)} %get-tuple-element.142.refs_2_, ...), custom_call_target="tpu_custom_call" | custom-call | bytes 1 | tf_op jit(solution)/shard_map/weight_grads/pallas_call | solution.py:46
  209.5 11.1 %collective-permute-done.22.refs_1_ = bf16[512,1024]{1,0:T(8,128)(2,1)S(1)} collective-permute-done((bf16[512,1024]{1,0:T(8,128)(2,1)}, bf16[512,1024]{1,0:T(8,128)(2,1)S(1)}, u32[]{:S(2)}, u32[]{:S(2)}) %collective-permute-start.22) | collective-permute-done | bytes 1048608 | tf_op jit(solution)/shard_map/ppermute | solution.py:447
  221.6 2.6 multiply_reduce_fusion.1
  224.2 4.0 fusion.33
  228.2 9.2 %weight_grads.5 = (bf16[512,2304]{1,0:T(8,128)(2,1)}, bf16[512,2304]{1,0:T(8,128)(2,1)}, f32[8,128]{1,0:T(8,128)}) custom-call(bf16[1024,1024]{1,0:T(8,128)(2,1)} %turn.11.refs_0_, bf16[1024,1024]{1,0:T(8,128)(2,1)} %get-tuple-element.141.refs_1_, bf16[1024,3072]{1,0:T(8,128)(2,1)} %get-tuple-element.142.refs_2_, ...), custom_call_target="tpu_custom_call" | custom-call | flops 309237645312 | bytes 872415232 | tf_op jit(solution)/shard_map/weight_grads/pallas_call | solution.py:46
  238.9 2.7 turn.12.refs_3_
  243.6 2.7 add_convert_fusion.1
  250.6 20.8 %attend_back.2 = (bf16[512,1024]{1,0:T(8,128)(2,1)}, f32[8,128]{1,0:T(8,128)}, bf16[1024,2048]{1,0:T(8,128)(2,1)}) custom-call(bf16[512,1024]{1,0:T(8,128)(2,1)} %get-tuple-element.199.refs_4_.refs_1_.refs_0_, bf16[1024,3584]{1,0:T(8,128)(2,1)} %get-tuple-element.153.refs_1_, bf16[1024,1024]{1,0:T(8,128)(2,1)} %get-tuple-element.154.refs_2_.refs_3_, ...), custom_call_target="tpu_custom_call" | custom-call | flops 377957122048 | bytes 1111564288 | tf_op jit(solution)/shard_map/attend_back/pallas_call | solution.py:46
  271.4 3.3 collective-permute-done.24.refs_0_
  274.7 2.3 collective-permute-done.25.refs_1_
  277.0 2.2 fusion.35
  281.3 2.4 fusion.14.refs_16_
  284.7 2.5 fusion.15.refs_15_
  289.0 20.8 %attend_back.3 = (bf16[512,1024]{1,0:T(8,128)(2,1)}, f32[8,128]{1,0:T(8,128)}, bf16[1024,2048]{1,0:T(8,128)(2,1)}) custom-call(bf16[512,1024]{1,0:T(8,128)(2,1)} %get-tuple-element.162.refs_0_.refs_1_, bf16[1024,3584]{1,0:T(8,128)(2,1)} %get-tuple-element.153.refs_1_, ...), custom_call_target="tpu_custom_call", output_to_operand_aliasing={{2}: (14, {})} | custom-call | flops 377957122048 | bytes 1111564288 | tf_op jit(solution)/shard_map/attend_back/pallas_call | solution.py:46
  314.9 2.2 fusion.21.refs_4_.refs_5_
  318.4 2.6 turn.13.refs_1_
  321.0 7.3 %weight_grads.6 = (bf16[512,1536]{1,0:T(8,128)(2,1)}, bf16[512,1536]{1,0:T(8,128)(2,1)}, f32[8,128]{1,0:T(8,128)}) custom-call(bf16[1024,1024]{1,0:T(8,128)(2,1)} %get-tuple-element.169.refs_0_, bf16[1024,1024]{1,0:T(8,128)(2,1)} %turn.13.refs_1_, bf16[1024,2048]{1,0:T(8,128)(2,1)} %get-tuple-element.171.refs_2_, ...), custom_call_target="tpu_custom_call" | custom-call | bytes 1 | tf_op jit(solution)/shard_map/weight_grads/pallas_call | solution.py:46
  328.6 4.9 %collective-permute-done.30.refs_0_ = bf16[64,2304]{1,0:T(8,128)(2,1)S(1)} collective-permute-done((bf16[64,2304]{1,0:T(8,128)(2,1)S(1)}, bf16[64,2304]{1,0:T(8,128)(2,1)S(1)}, u32[]{:S(2)}, u32[]{:S(2)}) %collective-permute-start.30) | collective-permute-done | bytes 294944 | tf_op jit(solution)/shard_map/ppermute | solution.py:447
  334.2 7.6 %weight_grads.7 = (bf16[512,1536]{1,0:T(8,128)(2,1)}, bf16[512,1536]{1,0:T(8,128)(2,1)}, f32[8,128]{1,0:T(8,128)}) custom-call(bf16[1024,1024]{1,0:T(8,128)(2,1)} %get-tuple-element.169.refs_0_, bf16[1024,1024]{1,0:T(8,128)(2,1)} %turn.13.refs_1_, bf16[1024,2048]{1,0:T(8,128)(2,1)} %get-tuple-element.171.refs_2_, ...), custom_call_target="tpu_custom_call" | custom-call | flops 206158430208 | bytes 671088640 | tf_op jit(solution)/shard_map/weight_grads/pallas_call | solution.py:46
  342.9 2.7 collective-permute-done.36.refs_2_
  354.8 21.6 %collective-permute-done.39.refs_2_ = f32[18,128]{1,0:T(8,128)S(1)} collective-permute-done((f32[18,128]{1,0:T(8,128)S(1)}, f32[18,128]{1,0:T(8,128)S(1)}, u32[]{:S(2)}, u32[]{:S(2)}) %collective-permute-start.39) | collective-permute-done | bytes 9248 | tf_op jit(solution)/shard_map/ppermute | solution.py:447
  386.0 3.4 collective-permute-done.41.refs_1_
  389.3 2.2 collective-permute-done.40.refs_0_
  393.8 2.3 fusion.19
  407.9 2.7 reshape.314
  410.6 5.6 %fusion.10 = (bf16[512,1024]{1,0:T(8,128)(2,1)}, bf16[512,1024]{1,0:T(8,128)(2,1)}) fusion(f32[512,1024]{1,0:T(8,128)} %get-tuple-element.200, bf16[512,1024]{1,0:T(8,128)(2,1)S(1)} %copy-done.4, bf16[512,1024]{1,0:T(8,128)(2,1)S(1)} %copy-done.9, bf16[512,1024]{1,0:T(8,128)(2,1)} %get-tuple-element.192, f32[512]{0:T(512)S(1)} %broadcast_multiply_fusion, ...), kind=kLoop, calls=%fused_computation.19 | loop fusion | flops 12058624 | bytes 11542528 | tf_op jit(solution)/shard_map/convert_element_type | solution.py:748
  (377 shorter events, 116.4 us)
Async XLA Ops:
  4.8 18.3 %collective-permute-start.1 = (bf16[64,1536]{1,0:T(8,128)(2,1)S(1)}, bf16[64,1536]{1,0:T(8,128)(2,1)S(1)}, u32[]{:S(2)}, u32[]{:S(2)}) collective-permute-start(bf16[64,1536]{1,0:T(8,128)(2,1)S(1)} %get-tuple-element.216), channel_id=1, source_target_pairs={{0,16},{2,18},{4,20},{6,22},{8,24},{10,26},{12,28},{14,30},{16,0},... | collective-permute-start | bytes 589832 | tf_op jit(solution)/shard_map/ppermute | solution.py:447
  8.9 17.5 %collective-permute-start = (bf16[64,1536]{1,0:T(8,128)(2,1)S(1)}, bf16[64,1536]{1,0:T(8,128)(2,1)S(1)}, u32[]{:S(2)}, u32[]{:S(2)}) collective-permute-start(bf16[64,1536]{1,0:T(8,128)(2,1)S(1)} %get-tuple-element.217), channel_id=1, source_target_pairs={{0,16},{2,18},{4,20},{6,22},{8,24},{10,26},{12,28},{14,30},{16,0},... | collective-permute-start | bytes 589832 | tf_op jit(solution)/shard_map/ppermute | solution.py:447
  10.0 16.4 %collective-permute-start.2 = (bf16[256,1024]{1,0:T(8,128)(2,1)}, bf16[256,1024]{1,0:T(8,128)(2,1)S(1)}, u32[]{:S(2)}, u32[]{:S(2)}) collective-permute-start(bf16[256,1024]{1,0:T(8,128)(2,1)} %get-tuple-element.209), channel_id=1, source_target_pairs={{0,1},{1,0},{2,3},{3,2},{4,5},{5,4},{6,7},{7,6},{8,9},{9,8},{10,11... | collective-permute-start | bytes 1572872 | tf_op jit(solution)/shard_map/ppermute | solution.py:447
  29.3 10.4 %collective-permute-start.4 = (bf16[128,1536]{1,0:T(8,128)(2,1)S(1)}, bf16[128,1536]{1,0:T(8,128)(2,1)S(1)}, u32[]{:S(2)}, u32[]{:S(2)}) collective-permute-start(bf16[128,1536]{1,0:T(8,128)(2,1)S(1)} %pad_maximum_fusion.15), channel_id=1, source_target_pairs={{0,4},{2,6},{4,0},{6,2},{8,12},{10,14},{12,8},{14,10},{16,20},{18,... | collective-permute-start | bytes 1179656 | tf_op jit(solution)/shard_map/ppermute | solution.py:447
  30.9 9.7 %collective-permute-start.3 = (bf16[128,1536]{1,0:T(8,128)(2,1)S(1)}, bf16[128,1536]{1,0:T(8,128)(2,1)S(1)}, u32[]{:S(2)}, u32[]{:S(2)}) collective-permute-start(bf16[128,1536]{1,0:T(8,128)(2,1)S(1)} %pad_maximum_fusion.14), channel_id=1, source_target_pairs={{0,8},{2,10},{4,12},{6,14},{8,0},{10,2},{12,4},{14,6},{16,24},{18,... | collective-permute-start | bytes 1179656 | tf_op jit(solution)/shard_map/ppermute | solution.py:447
  31.6 42.1 %collective-permute-start.9 = (bf16[512,1024]{1,0:T(8,128)(2,1)S(1)}, bf16[512,1024]{1,0:T(8,128)(2,1)S(1)}, u32[]{:S(2)}, u32[]{:S(2)}) collective-permute-start(bf16[512,1024]{1,0:T(8,128)(2,1)S(1)} %copy-done.38), channel_id=1, source_target_pairs={{0,1},{1,0},{2,3},{3,2},{4,5},{5,4},{6,7},{7,6},{8,9},{9,8},{10,11... | collective-permute-start | bytes 3145736 | tf_op jit(solution)/shard_map/ppermute | solution.py:447
  43.5 31.0 %collective-permute-start.6 = (bf16[256,1536]{1,0:T(8,128)(2,1)S(1)}, bf16[256,1536]{1,0:T(8,128)(2,1)S(1)}, u32[]{:S(2)}, u32[]{:S(2)}) collective-permute-start(bf16[256,1536]{1,0:T(8,128)(2,1)S(1)} %pad_maximum_fusion.9), channel_id=1, source_target_pairs={{0,8},{2,10},{4,12},{6,14},{8,0},{10,2},{12,4},{14,6},{16,24},{18,... | collective-permute-start | bytes 2359304 | tf_op jit(solution)/shard_map/ppermute | solution.py:447
  45.3 29.2 %collective-permute-start.5 = (bf16[256,1536]{1,0:T(8,128)(2,1)S(1)}, bf16[256,1536]{1,0:T(8,128)(2,1)S(1)}, u32[]{:S(2)}, u32[]{:S(2)}) collective-permute-start(bf16[256,1536]{1,0:T(8,128)(2,1)S(1)} %pad_maximum_fusion.8), channel_id=1, source_target_pairs={{0,4},{2,6},{4,0},{6,2},{8,12},{10,14},{12,8},{14,10},{16,20},{18,... | collective-permute-start | bytes 2359304 | tf_op jit(solution)/shard_map/ppermute | solution.py:447
  46.4 42.3 %copy-start.32 = (bf16[64,2304]{1,0:T(8,128)(2,1)}, bf16[64,2304]{1,0:T(8,128)(2,1)S(1)}, u32[]{:S(2)}) copy-start(bf16[64,2304]{1,0:T(8,128)(2,1)S(1)} %get-tuple-element.214) | copy-start | bytes 884740
  46.4 23.2 %collective-permute-start.8 = (bf16[64,2304]{1,0:T(8,128)(2,1)S(1)}, bf16[64,2304]{1,0:T(8,128)(2,1)S(1)}, u32[]{:S(2)}, u32[]{:S(2)}) collective-permute-start(bf16[64,2304]{1,0:T(8,128)(2,1)S(1)} %get-tuple-element.214), channel_id=1, source_target_pairs={{0,16},{2,18},{4,20},{6,22},{8,24},{10,26},{12,28},{14,30},{16,0},... | collective-permute-start | bytes 884744 | tf_op jit(solution)/shard_map/ppermute | solution.py:447
  49.8 23.9 %collective-permute-start.7 = (bf16[64,2304]{1,0:T(8,128)(2,1)S(1)}, bf16[64,2304]{1,0:T(8,128)(2,1)S(1)}, u32[]{:S(2)}, u32[]{:S(2)}) collective-permute-start(bf16[64,2304]{1,0:T(8,128)(2,1)S(1)} %get-tuple-element.215), channel_id=1, source_target_pairs={{0,16},{2,18},{4,20},{6,22},{8,24},{10,26},{12,28},{14,30},{16,0},... | collective-permute-start | bytes 884744 | tf_op jit(solution)/shard_map/ppermute | solution.py:447
  77.9 9.6 %collective-permute-start.13 = (bf16[512,1536]{1,0:T(8,128)(2,1)S(1)}, bf16[512,1536]{1,0:T(8,128)(2,1)S(1)}, u32[]{:S(2)}, u32[]{:S(2)}) collective-permute-start(bf16[512,1536]{1,0:T(8,128)(2,1)S(1)} %pad_maximum_fusion.3.refs_9_.refs_12_), channel_id=1, source_target_pairs={{0,2},{2,0},{4,6},{6,4},{8,10},{10,8},{12,14},{14,12},{16,18},{18,... | collective-permute-start | bytes 4718600 | tf_op jit(solution)/shard_map/ppermute | solution.py:447
  78.0 9.5 %collective-permute-start.12 = (bf16[512,1536]{1,0:T(8,128)(2,1)S(1)}, bf16[512,1536]{1,0:T(8,128)(2,1)}, u32[]{:S(2)}, u32[]{:S(2)}) collective-permute-start(bf16[512,1536]{1,0:T(8,128)(2,1)S(1)} %pad_maximum_fusion.2.refs_6_.refs_9_), channel_id=1, source_target_pairs={{0,2},{2,0},{4,6},{6,4},{8,10},{10,8},{12,14},{14,12},{16,18},{18,... | collective-permute-start | bytes 4718600 | tf_op jit(solution)/shard_map/ppermute | solution.py:447
  78.5 26.9 %collective-permute-start.14 = (bf16[256,1024]{1,0:T(8,128)(2,1)}, bf16[256,1024]{1,0:T(8,128)(2,1)}, u32[]{:S(2)}, u32[]{:S(2)}) collective-permute-start(bf16[256,1024]{1,0:T(8,128)(2,1)} %get-tuple-element.208), channel_id=1, source_target_pairs={{0,1},{1,0},{2,3},{3,2},{4,5},{5,4},{6,7},{7,6},{8,9},{9,8},{10,11... | collective-permute-start | bytes 1572872 | tf_op jit(solution)/shard_map/ppermute | solution.py:447
  81.4 24.0 %collective-permute-start.11 = (bf16[128,2304]{1,0:T(8,128)(2,1)}, bf16[128,2304]{1,0:T(8,128)(2,1)}, u32[]{:S(2)}, u32[]{:S(2)}) collective-permute-start(bf16[128,2304]{1,0:T(8,128)(2,1)} %pad_maximum_fusion.12.refs_12_), channel_id=1, source_target_pairs={{0,4},{2,6},{4,0},{6,2},{8,12},{10,14},{12,8},{14,10},{16,20},{18,... | collective-permute-start | bytes 1769480 | tf_op jit(solution)/shard_map/ppermute | solution.py:447
  83.6 21.8 %collective-permute-start.10 = (bf16[128,2304]{1,0:T(8,128)(2,1)}, bf16[128,2304]{1,0:T(8,128)(2,1)}, u32[]{:S(2)}, u32[]{:S(2)}) collective-permute-start(bf16[128,2304]{1,0:T(8,128)(2,1)} %pad_maximum_fusion.11.refs_11_), channel_id=1, source_target_pairs={{0,8},{2,10},{4,12},{6,14},{8,0},{10,2},{12,4},{14,6},{16,24},{18,... | collective-permute-start | bytes 1769480 | tf_op jit(solution)/shard_map/ppermute | solution.py:447
  105.5 24.7 %collective-permute-start.17 = (bf16[512,1024]{1,0:T(8,128)(2,1)}, bf16[512,1024]{1,0:T(8,128)(2,1)}, u32[]{:S(2)}, u32[]{:S(2)}) collective-permute-start(bf16[512,1024]{1,0:T(8,128)(2,1)} %get-tuple-element.124), channel_id=1, source_target_pairs={{0,1},{1,0},{2,3},{3,2},{4,5},{5,4},{6,7},{7,6},{8,9},{9,8},{10,11... | collective-permute-start | bytes 3145736 | tf_op jit(solution)/shard_map/ppermute | solution.py:447
  110.8 27.4 %collective-permute-start.16 = (bf16[256,2304]{1,0:T(8,128)(2,1)}, bf16[256,2304]{1,0:T(8,128)(2,1)}, u32[]{:S(2)}, u32[]{:S(2)}) collective-permute-start(bf16[256,2304]{1,0:T(8,128)(2,1)} %pad_maximum_fusion.5.refs_14_), channel_id=1, source_target_pairs={{0,8},{2,10},{4,12},{6,14},{8,0},{10,2},{12,4},{14,6},{16,24},{18,... | collective-permute-start | bytes 3538952 | tf_op jit(solution)/shard_map/ppermute | solution.py:447
  110.9 27.7 %collective-permute-start.15 = (bf16[256,2304]{1,0:T(8,128)(2,1)}, bf16[256,2304]{1,0:T(8,128)(2,1)}, u32[]{:S(2)}, u32[]{:S(2)}) collective-permute-start(bf16[256,2304]{1,0:T(8,128)(2,1)} %pad_maximum_fusion.4.refs_13_), channel_id=1, source_target_pairs={{0,4},{2,6},{4,0},{6,2},{8,12},{10,14},{12,8},{14,10},{16,20},{18,... | collective-permute-start | bytes 3538952 | tf_op jit(solution)/shard_map/ppermute | solution.py:447
  143.8 9.3 %collective-permute-start.19 = (bf16[512,2304]{1,0:T(8,128)(2,1)S(1)}, bf16[512,2304]{1,0:T(8,128)(2,1)S(1)}, u32[]{:S(2)}, u32[]{:S(2)}) collective-permute-start(bf16[512,2304]{1,0:T(8,128)(2,1)S(1)} %pad_maximum_fusion.1.refs_7_), channel_id=1, source_target_pairs={{0,2},{2,0},{4,6},{6,4},{8,10},{10,8},{12,14},{14,12},{16,18},{18,... | collective-permute-start | bytes 7077896 | tf_op jit(solution)/shard_map/ppermute | solution.py:447
  143.9 9.2 %collective-permute-start.18 = (bf16[512,2304]{1,0:T(8,128)(2,1)S(1)}, bf16[512,2304]{1,0:T(8,128)(2,1)}, u32[]{:S(2)}, u32[]{:S(2)}) collective-permute-start(bf16[512,2304]{1,0:T(8,128)(2,1)S(1)} %pad_maximum_fusion.refs_4_), channel_id=1, source_target_pairs={{0,2},{2,0},{4,6},{6,4},{8,10},{10,8},{12,14},{14,12},{16,18},{18,... | collective-permute-start | bytes 7077896 | tf_op jit(solution)/shard_map/ppermute | solution.py:447
  151.9 25.5 %collective-permute-start.20 = (bf16[512,1024]{1,0:T(8,128)(2,1)}, bf16[512,1024]{1,0:T(8,128)(2,1)}, u32[]{:S(2)}, u32[]{:S(2)}) collective-permute-start(bf16[512,1024]{1,0:T(8,128)(2,1)} %multiply_convert_fusion.refs_0_.refs_9_.refs_1_), channel_id=1, source_target_pairs={{0,1},{1,0},{2,3},{3,2},{4,5},{5,4},{6,7},{7,6},{8,9},{9,8},{10,11... | collective-permute-start | bytes 3145736 | tf_op jit(solution)/shard_map/ppermute | solution.py:447
  195.7 24.9 %collective-permute-start.22 = (bf16[512,1024]{1,0:T(8,128)(2,1)}, bf16[512,1024]{1,0:T(8,128)(2,1)S(1)}, u32[]{:S(2)}, u32[]{:S(2)}) collective-permute-start(bf16[512,1024]{1,0:T(8,128)(2,1)} %get-tuple-element.140.refs_3_.refs_4_), channel_id=1, source_target_pairs={{0,1},{1,0},{2,3},{3,2},{4,5},{5,4},{6,7},{7,6},{8,9},{9,8},{10,11... | collective-permute-start | bytes 3145736 | tf_op jit(solution)/shard_map/ppermute | solution.py:447
  209.5 32.1 %collective-permute-start.21 = (bf16[512,2304]{1,0:T(8,128)(2,1)}, bf16[512,2304]{1,0:T(8,128)(2,1)}, u32[]{:S(2)}, u32[]{:S(2)}) collective-permute-start(bf16[512,2304]{1,0:T(8,128)(2,1)} %get-tuple-element.145), channel_id=1, source_target_pairs={{0,2},{2,0},{4,6},{6,4},{8,10},{10,8},{12,14},{14,12},{16,18},{18,... | collective-permute-start | bytes 7077896 | tf_op jit(solution)/shard_map/ppermute | solution.py:447
  237.4 4.7 %collective-permute-start.23 = (bf16[512,2304]{1,0:T(8,128)(2,1)}, bf16[512,2304]{1,0:T(8,128)(2,1)S(1)}, u32[]{:S(2)}, u32[]{:S(2)}) collective-permute-start(bf16[512,2304]{1,0:T(8,128)(2,1)} %get-tuple-element.148), channel_id=1, source_target_pairs={{0,2},{2,0},{4,6},{6,4},{8,10},{10,8},{12,14},{14,12},{16,18},{18,... | collective-permute-start | bytes 7077896 | tf_op jit(solution)/shard_map/ppermute | solution.py:447
  238.0 33.4 %collective-permute-start.26 = (bf16[512,1024]{1,0:T(8,128)(2,1)}, bf16[512,1024]{1,0:T(8,128)(2,1)}, u32[]{:S(2)}, u32[]{:S(2)}) collective-permute-start(bf16[512,1024]{1,0:T(8,128)(2,1)} %get-tuple-element.199.refs_4_.refs_1_.refs_0_), channel_id=1, source_target_pairs={{0,1},{1,0},{2,3},{3,2},{4,5},{5,4},{6,7},{7,6},{8,9},{9,8},{10,11... | collective-permute-start | bytes 3145736 | tf_op jit(solution)/shard_map/ppermute | solution.py:447
  246.3 28.4 %collective-permute-start.24 = (bf16[2,2,64,2304]{3,2,1,0:T(8,128)(2,1)}, bf16[2,2,64,2304]{3,2,1,0:T(8,128)(2,1)}, u32[]{:S(2)}, u32[]{:S(2)}) collective-permute-start(bf16[2,2,64,2304]{3,2,1,0:T(8,128)(2,1)} %bitcast.8.refs_16_), channel_id=1, source_target_pairs={{0,4},{2,6},{4,0},{6,2},{8,12},{10,14},{12,8},{14,10},{16,20},{18,... | collective-permute-start | bytes 3538952 | tf_op jit(solution)/shard_map/ppermute | solution.py:447
  248.6 28.4 %collective-permute-start.25 = (bf16[2,2,64,2304]{3,2,1,0:T(8,128)(2,1)}, bf16[2,2,64,2304]{3,2,1,0:T(8,128)(2,1)}, u32[]{:S(2)}, u32[]{:S(2)}) collective-permute-start(bf16[2,2,64,2304]{3,2,1,0:T(8,128)(2,1)} %fusion.13.refs_17_), channel_id=1, source_target_pairs={{0,8},{2,10},{4,12},{6,14},{8,0},{10,2},{12,4},{14,6},{16,24},{18,... | collective-permute-start | bytes 3538952 | tf_op jit(solution)/shard_map/ppermute | solution.py:447
  279.2 49.3 %collective-permute-start.32 = (bf16[256,1024]{1,0:T(8,128)(2,1)}, bf16[256,1024]{1,0:T(8,128)(2,1)}, u32[]{:S(2)}, u32[]{:S(2)}) collective-permute-start(bf16[256,1024]{1,0:T(8,128)(2,1)} %get-tuple-element.206), channel_id=1, source_target_pairs={{0,1},{1,0},{2,3},{3,2},{4,5},{5,4},{6,7},{7,6},{8,9},{9,8},{10,11... | collective-permute-start | bytes 1572872 | tf_op jit(solution)/shard_map/ppermute | solution.py:447
  280.9 30.1 %collective-permute-start.29 = (bf16[256,1024]{1,0:T(8,128)(2,1)}, bf16[256,1024]{1,0:T(8,128)(2,1)}, u32[]{:S(2)}, u32[]{:S(2)}) collective-permute-start(bf16[256,1024]{1,0:T(8,128)(2,1)} %get-tuple-element.207), channel_id=1, source_target_pairs={{0,1},{1,0},{2,3},{3,2},{4,5},{5,4},{6,7},{7,6},{8,9},{9,8},{10,11... | collective-permute-start | bytes 1572872 | tf_op jit(solution)/shard_map/ppermute | solution.py:447
  283.7 27.3 %collective-permute-start.28 = (bf16[2,64,2304]{2,1,0:T(8,128)(2,1)}, bf16[2,64,2304]{2,1,0:T(8,128)(2,1)}, u32[]{:S(2)}, u32[]{:S(2)}) collective-permute-start(bf16[2,64,2304]{2,1,0:T(8,128)(2,1)} %fusion.14.refs_16_), channel_id=1, source_target_pairs={{0,4},{2,6},{4,0},{6,2},{8,12},{10,14},{12,8},{14,10},{16,20},{18,... | collective-permute-start | bytes 1769480 | tf_op jit(solution)/shard_map/ppermute | solution.py:447
  287.2 23.8 %collective-permute-start.27 = (bf16[2,64,2304]{2,1,0:T(8,128)(2,1)}, bf16[2,64,2304]{2,1,0:T(8,128)(2,1)}, u32[]{:S(2)}, u32[]{:S(2)}) collective-permute-start(bf16[2,64,2304]{2,1,0:T(8,128)(2,1)} %fusion.15.refs_15_), channel_id=1, source_target_pairs={{0,8},{2,10},{4,12},{6,14},{8,0},{10,2},{12,4},{14,6},{16,24},{18,... | collective-permute-start | bytes 1769480 | tf_op jit(solution)/shard_map/ppermute | solution.py:447
  313.4 15.2 %collective-permute-start.31 = (f32[18,128]{1,0:T(8,128)S(1)}, f32[18,128]{1,0:T(8,128)S(1)}, u32[]{:S(2)}, u32[]{:S(2)}) collective-permute-start(f32[18,128]{1,0:T(8,128)S(1)} %maximum_bitcast_fusion.refs_6_), channel_id=1, source_target_pairs={{0,2},{2,0},{4,6},{6,4},{8,10},{10,8},{12,14},{14,12},{16,18},{18,... | collective-permute-start | bytes 27656 | tf_op jit(solution)/shard_map/ppermute | solution.py:447
  317.1 16.4 %collective-permute-start.30 = (bf16[64,2304]{1,0:T(8,128)(2,1)S(1)}, bf16[64,2304]{1,0:T(8,128)(2,1)S(1)}, u32[]{:S(2)}, u32[]{:S(2)}) collective-permute-start(bf16[64,2304]{1,0:T(8,128)(2,1)S(1)} %fusion.22.refs_3_.refs_4_), channel_id=1, source_target_pairs={{0,16},{2,18},{4,20},{6,22},{8,24},{10,26},{12,28},{14,30},{16,0},... | collective-permute-start | bytes 884744 | tf_op jit(solution)/shard_map/ppermute | solution.py:447
  328.3 17.3 %collective-permute-start.34 = (bf16[512,1536]{1,0:T(8,128)(2,1)}, bf16[512,1536]{1,0:T(8,128)(2,1)}, u32[]{:S(2)}, u32[]{:S(2)}) collective-permute-start(bf16[512,1536]{1,0:T(8,128)(2,1)} %get-tuple-element.182), channel_id=1, source_target_pairs={{0,2},{2,0},{4,6},{6,4},{8,10},{10,8},{12,14},{14,12},{16,18},{18,... | collective-permute-start | bytes 4718600 | tf_op jit(solution)/shard_map/ppermute | solution.py:447
  341.8 3.9 collective-permute-start.35
  341.9 3.8 collective-permute-start.36
  348.9 27.5 %collective-permute-start.37 = (bf16[2,2,64,1536]{3,2,1,0:T(8,128)(2,1)S(1)}, bf16[2,2,64,1536]{3,2,1,0:T(8,128)(2,1)S(1)}, u32[]{:S(2)}, u32[]{:S(2)}) collective-permute-start(bf16[2,2,64,1536]{3,2,1,0:T(8,128)(2,1)S(1)} %bitcast.207), channel_id=1, source_target_pairs={{0,4},{2,6},{4,0},{6,2},{8,12},{10,14},{12,8},{14,10},{16,20},{18,... | collective-permute-start | bytes 2359304 | tf_op jit(solution)/shard_map/ppermute | solution.py:447
  351.3 25.1 %collective-permute-start.38 = (bf16[2,2,64,1536]{3,2,1,0:T(8,128)(2,1)S(1)}, bf16[2,2,64,1536]{3,2,1,0:T(8,128)(2,1)S(1)}, u32[]{:S(2)}, u32[]{:S(2)}) collective-permute-start(bf16[2,2,64,1536]{3,2,1,0:T(8,128)(2,1)S(1)} %fusion.16), channel_id=1, source_target_pairs={{0,8},{2,10},{4,12},{6,14},{8,0},{10,2},{12,4},{14,6},{16,24},{18,... | collective-permute-start | bytes 2359304 | tf_op jit(solution)/shard_map/ppermute | solution.py:447
  351.4 25.0 %collective-permute-start.39 = (f32[18,128]{1,0:T(8,128)S(1)}, f32[18,128]{1,0:T(8,128)S(1)}, u32[]{:S(2)}, u32[]{:S(2)}) collective-permute-start(f32[18,128]{1,0:T(8,128)S(1)} %fusion.41), channel_id=1, source_target_pairs={{0,8},{2,10},{4,12},{6,14},{8,0},{10,2},{12,4},{14,6},{16,24},{18,... | collective-permute-start | bytes 27656 | tf_op jit(solution)/shard_map/ppermute | solution.py:447
  353.4 32.5 %collective-permute-start.42 = (bf16[64,2304]{1,0:T(8,128)(2,1)}, bf16[64,2304]{1,0:T(8,128)(2,1)}, u32[]{:S(2)}, u32[]{:S(2)}) collective-permute-start(bf16[64,2304]{1,0:T(8,128)(2,1)} %fusion.21.refs_4_.refs_5_), channel_id=1, source_target_pairs={{0,16},{2,18},{4,20},{6,22},{8,24},{10,26},{12,28},{14,30},{16,0},... | collective-permute-start | bytes 884744 | tf_op jit(solution)/shard_map/ppermute | solution.py:447
  353.5 42.6 %collective-permute-start.33 = (bf16[512,1024]{1,0:T(8,128)(2,1)S(1)}, bf16[512,1024]{1,0:T(8,128)(2,1)S(1)}, u32[]{:S(2)}, u32[]{:S(2)}) collective-permute-start(bf16[512,1024]{1,0:T(8,128)(2,1)S(1)} %copy-done.39), channel_id=1, source_target_pairs={{0,1},{1,0},{2,3},{3,2},{4,5},{5,4},{6,7},{7,6},{8,9},{9,8},{10,11... | collective-permute-start | bytes 3145736 | tf_op jit(solution)/shard_map/ppermute | solution.py:447
  378.9 7.1 %collective-permute-start.43 = (f32[18,128]{1,0:T(8,128)S(1)}, f32[18,128]{1,0:T(8,128)S(1)}, u32[]{:S(2)}, u32[]{:S(2)}) collective-permute-start(f32[18,128]{1,0:T(8,128)S(1)} %add.308), channel_id=1, source_target_pairs={{0,16},{2,18},{4,20},{6,22},{8,24},{10,26},{12,28},{14,30},{16,0},... | collective-permute-start | bytes 27656 | tf_op jit(solution)/shard_map/ppermute | solution.py:447
  380.1 9.2 %collective-permute-start.41 = (bf16[2,64,1536]{2,1,0:T(8,128)(2,1)S(1)}, bf16[2,64,1536]{2,1,0:T(8,128)(2,1)S(1)}, u32[]{:S(2)}, u32[]{:S(2)}) collective-permute-start(bf16[2,64,1536]{2,1,0:T(8,128)(2,1)S(1)} %fusion.17.refs_2_), channel_id=1, source_target_pairs={{0,4},{2,6},{4,0},{6,2},{8,12},{10,14},{12,8},{14,10},{16,20},{18,... | collective-permute-start | bytes 1179656 | tf_op jit(solution)/shard_map/ppermute | solution.py:447
  382.5 9.0 %collective-permute-start.40 = (bf16[2,64,1536]{2,1,0:T(8,128)(2,1)S(1)}, bf16[2,64,1536]{2,1,0:T(8,128)(2,1)S(1)}, u32[]{:S(2)}, u32[]{:S(2)}) collective-permute-start(bf16[2,64,1536]{2,1,0:T(8,128)(2,1)S(1)} %fusion.18.refs_1_), channel_id=1, source_target_pairs={{0,8},{2,10},{4,12},{6,14},{8,0},{10,2},{12,4},{14,6},{16,24},{18,... | collective-permute-start | bytes 1179656 | tf_op jit(solution)/shard_map/ppermute | solution.py:447
  399.1 19.9 %collective-permute-start.46 = (f32[18,128]{1,0:T(8,128)}, f32[18,128]{1,0:T(8,128)}, u32[]{:S(2)}, u32[]{:S(2)}) collective-permute-start(f32[18,128]{1,0:T(8,128)} %add.334), channel_id=1, source_target_pairs={{0,1},{1,0},{2,3},{3,2},{4,5},{5,4},{6,7},{7,6},{8,9},{9,8},{10,11... | collective-permute-start | bytes 27656 | tf_op jit(solution)/shard_map/ppermute | solution.py:447
  403.9 16.9 %collective-permute-start.45 = (bf16[64,1536]{1,0:T(8,128)(2,1)}, bf16[64,1536]{1,0:T(8,128)(2,1)}, u32[]{:S(2)}, u32[]{:S(2)}) collective-permute-start(bf16[64,1536]{1,0:T(8,128)(2,1)} %fusion.23), channel_id=1, source_target_pairs={{0,16},{2,18},{4,20},{6,22},{8,24},{10,26},{12,28},{14,30},{16,0},... | collective-permute-start | bytes 589832 | tf_op jit(solution)/shard_map/ppermute | solution.py:447
  405.8 16.3 %collective-permute-start.44 = (bf16[64,1536]{1,0:T(8,128)(2,1)}, bf16[64,1536]{1,0:T(8,128)(2,1)}, u32[]{:S(2)}, u32[]{:S(2)}) collective-permute-start(bf16[64,1536]{1,0:T(8,128)(2,1)} %fusion.25), channel_id=1, source_target_pairs={{0,16},{2,18},{4,20},{6,22},{8,24},{10,26},{12,28},{14,30},{16,0},... | collective-permute-start | bytes 589832 | tf_op jit(solution)/shard_map/ppermute | solution.py:447
  (104 other events, 685.3 us)

commit v6 on v5

--- a/solution.py
+++ b/solution.py
@@ -423,17 +423,28 @@
 
 
 def pack(parts, pieces):
-    rows = parts[0].shape[0]
-    split = [part.reshape(rows, pieces, part.shape[1] // pieces) for part in parts]
-    return jnp.concatenate(split, axis=2).reshape(rows, -1)
+    return jnp.concatenate(
+        [
+            part[:, index * part.shape[1] // pieces : (index + 1) * part.shape[1] // pieces]
+            for index in range(pieces)
+            for part in parts
+        ],
+        axis=1,
+    )
 
 
 def unpack(packed, pieces, widths):
-    rows = packed.shape[0]
-    split = packed.reshape(rows, pieces, -1).astype(F32)
+    unit = packed.shape[1] // pieces
     ends = np.cumsum([width // pieces for width in widths])
     return [
-        split[:, :, end - width // pieces : end].reshape(rows, width) for end, width in zip(ends, widths)
+        jnp.concatenate(
+            [
+                packed[:, index * unit + end - width // pieces : index * unit + end]
+                for index in range(pieces)
+            ],
+            axis=1,
+        )
+        for end, width in zip(ends, widths)
     ]
 
 

time: 432 us -> 433 us (level)
  waiting for transfers between devices: 100 us -> 108 us
  other arithmetic: 72.7 us -> 67.8 us
    ppermute x47, waiting for transfers between devices: 100 us -> 108 us  [exchange(): lax.ppermute(array, axis, [(index, index ^ flip) for index in range(size)])]
    reshape x9 -> x0, local copies, waits for them, and re-layouts: 7.56 us -> none  [the longest x7 4.46 us: pack(): part.reshape(rows, pieces, part.shape[1] // pieces)]
    unnamed x220 -> x258, local copies, waits for them, and re-layouts: 24.1 us -> 28.3 us
  transfers between devices with their start and end apart: 47 -> 47, of which waited for: 19 -> 21; matrix products, arithmetic and copies ran while one was open for 17% -> 15% of each run, Pallas kernels for 34% -> 34%
where the time goes in v6:
time: 433 us; the launch traced here: 428 us
  Pallas kernels  163 us (38%)
  waiting for transfers between devices  108 us (25%)
  other arithmetic  67.8 us (16%)
  starting transfers between devices  49.6 us (11%)
  local copies, waits for them, and re-layouts  37.4 us (9%)
    pallas_call x34, Pallas kernels, kernel_call(): pl.pallas_call(run, grid=grid, in_specs=[spec for _, spec in inputs] + [p...  163 us
    ppermute x47, waiting for transfers between devices, exchange(): lax.ppermute(array, axis, [(index, index ^ flip) for index in range(size)])  108 us
    ppermute x47, starting transfers between devices, exchange(): lax.ppermute(array, axis, [(index, index ^ flip) for index in range(size)])  49.6 us
    unnamed x258, local copies, waits for them, and re-layouts  28.3 us
    convert_element_type x12, other arithmetic, halve(): sent = self.part(flip).astype(BF16)  19.2 us
    concatenate x12, other arithmetic, join(): self.held = jnp.concatenate([self.held, self.got], axis=0)  15.6 us
  transfers between devices with their start and end apart: 47, of which 21 were waited for; matrix products, arithmetic and copies ran while one was open for 15% of the time, Pallas kernels for 34%

profile of v6, /device:TPU:0, one launch (start us, length us, event | category | flops | bytes accessed | tf_op | source)
XLA Modules:
  0.0 427.8 jit_solution(4824535339151843140)
XLA Ops:
  6.9 4.0 collective-permute-start.1
  17.2 2.6 turn.7.refs_4_
  19.9 2.6 turn.8.refs_5_
  22.5 2.7 collective-permute-done.1.refs_1_
  25.1 3.4 collective-permute-done.refs_0_
  35.8 6.6 %collective-permute-done.4.refs_1_ = bf16[128,1536]{1,0:T(8,128)(2,1)S(1)} collective-permute-done((bf16[128,1536]{1,0:T(8,128)(2,1)S(1)}, bf16[128,1536]{1,0:T(8,128)(2,1)S(1)}, u32[]{:S(2)}, u32[]{:S(2)}) %collective-permute-start.4) | collective-permute-done | bytes 393248 | tf_op jit(solution)/shard_map/ppermute | solution.py:458
  49.0 3.4 collective-permute-start.8
  52.6 19.7 %collective-permute-done.8.refs_3_ = bf16[64,2304]{1,0:T(8,128)(2,1)S(1)} collective-permute-done((bf16[64,2304]{1,0:T(8,128)(2,1)S(1)}, bf16[64,2304]{1,0:T(8,128)(2,1)S(1)}, u32[]{:S(2)}, u32[]{:S(2)}) %collective-permute-start.8) | collective-permute-done | bytes 294944 | tf_op jit(solution)/shard_map/ppermute | solution.py:458
  72.3 4.1 collective-permute-done.7.refs_2_
  86.2 3.8 collective-permute-start.10
  92.4 16.6 %attend.2 = (bf16[512,1024]{1,0:T(8,128)(2,1)}, f32[32,512]{1,0:T(8,128)}, bf16[1024,3584]{1,0:T(8,128)(2,1)}, bf16[1024,1024]{1,0:T(8,128)(2,1)}) custom-call(bf16[512,1024]{1,0:T(8,128)(2,1)} %get-tuple-element.113.refs_0_.refs_1_, f32[512,128]{1,0:T(8,128)} %constant.32.clone.refs_1_.refs_4_, f32[512,128]{1,0:T(8,128)} %constant.33.clone.refs_2_.refs_5_, ...), custom_call_target="tpu_custom_call" | custom-call | flops 274877906944 | bytes 503390208 | tf_op jit(solution)/shard_map/attend/pallas_call | solution.py:46
  110.1 2.2 pad_maximum_fusion.4.refs_13_
  115.4 16.4 %attend.3 = (bf16[512,1024]{1,0:T(8,128)(2,1)}, f32[32,512]{1,0:T(8,128)}, bf16[1024,3584]{1,0:T(8,128)(2,1)}, bf16[1024,1024]{1,0:T(8,128)(2,1)}) custom-call(bf16[512,1024]{1,0:T(8,128)(2,1)} %fusion.5.refs_1_.refs_0_, f32[512,128]{1,0:T(8,128)} %constant.32.clone.refs_1_.refs_4_, ...), custom_call_target="tpu_custom_call", output_to_operand_aliasing={{2}: (11, {}), {3}: (12, {})} | custom-call | flops 274877906944 | bytes 503390208 | tf_op jit(solution)/shard_map/attend/pallas_call | solution.py:46
  133.8 8.0 %collective-permute-done.16.refs_1_ = bf16[256,2304]{1,0:T(8,128)(2,1)} collective-permute-done((bf16[256,2304]{1,0:T(8,128)(2,1)}, bf16[256,2304]{1,0:T(8,128)(2,1)}, u32[]{:S(2)}, u32[]{:S(2)}) %collective-permute-start.16) | collective-permute-done | bytes 1179680 | tf_op jit(solution)/shard_map/ppermute | solution.py:458
  144.7 2.4 pad_maximum_fusion.1.refs_7_
  152.5 2.7 multiply_convert_fusion.refs_0_.refs_9_.refs_1_
  157.8 17.8 %mlp.2 = (bf16[512,1024]{1,0:T(8,128)(2,1)}, bf16[512,1024]{1,0:T(8,128)(2,1)}, f32[1,1024]{1,0:T(1,128)}, bf16[1024,3072]{1,0:T(8,128)(2,1)}, bf16[1024,1536]{1,0:T(8,128)(2,1)}) custom-call(bf16[512,1024]{1,0:T(8,128)(2,1)} %multiply_convert_fusion.refs_0_.refs_9_.refs_1_, bf16[512,1024]{1,0:T(8,128)(2,1)} %refs_1_.5, f32[1,1024]{1,0:T(1,128)} %bitcast.187, ...), custom_call_target="tpu_custom_call" | custom-call | flops 618475290624 | bytes 738467840 | tf_op jit(solution)/shard_map/mlp/pallas_call | solution.py:46
  175.6 2.6 turn.9.refs_3_.refs_2_
  178.2 2.6 turn.10.refs_3_
  180.7 18.0 %mlp.3 = (bf16[512,1024]{1,0:T(8,128)(2,1)}, bf16[512,1024]{1,0:T(8,128)(2,1)}, f32[1,1024]{1,0:T(1,128)}, bf16[1024,3072]{1,0:T(8,128)(2,1)}, bf16[1024,1536]{1,0:T(8,128)(2,1)}) custom-call(bf16[512,1024]{1,0:T(8,128)(2,1)} %get-tuple-element.136.refs_0_.refs_2_, ...), custom_call_target="tpu_custom_call", output_to_operand_aliasing={{3}: (9, {}), {4}: (10, {})} | custom-call | flops 618475290624 | bytes 738467840 | tf_op jit(solution)/shard_map/mlp/pallas_call | solution.py:46
  199.7 3.5 turn.11.refs_0_
  203.2 9.2 %weight_grads.4 = (bf16[512,2304]{1,0:T(8,128)(2,1)}, bf16[512,2304]{1,0:T(8,128)(2,1)}, f32[8,128]{1,0:T(8,128)}) custom-call(bf16[1024,1024]{1,0:T(8,128)(2,1)} %turn.11.refs_0_, bf16[1024,1024]{1,0:T(8,128)(2,1)} %get-tuple-element.141.refs_1_, bf16[1024,3072]{1,0:T(8,128)(2,1)} %get-tuple-element.142.refs_2_, ...), custom_call_target="tpu_custom_call" | custom-call | bytes 1 | tf_op jit(solution)/shard_map/weight_grads/pallas_call | solution.py:46
  212.5 11.2 %collective-permute-done.22.refs_1_ = bf16[512,1024]{1,0:T(8,128)(2,1)S(1)} collective-permute-done((bf16[512,1024]{1,0:T(8,128)(2,1)}, bf16[512,1024]{1,0:T(8,128)(2,1)S(1)}, u32[]{:S(2)}, u32[]{:S(2)}) %collective-permute-start.22) | collective-permute-done | bytes 1048608 | tf_op jit(solution)/shard_map/ppermute | solution.py:458
  224.7 2.6 multiply_reduce_fusion.1
  227.3 4.0 fusion.33
  231.3 9.2 %weight_grads.5 = (bf16[512,2304]{1,0:T(8,128)(2,1)}, bf16[512,2304]{1,0:T(8,128)(2,1)}, f32[8,128]{1,0:T(8,128)}) custom-call(bf16[1024,1024]{1,0:T(8,128)(2,1)} %turn.11.refs_0_, bf16[1024,1024]{1,0:T(8,128)(2,1)} %get-tuple-element.141.refs_1_, bf16[1024,3072]{1,0:T(8,128)(2,1)} %get-tuple-element.142.refs_2_, ...), custom_call_target="tpu_custom_call" | custom-call | flops 309237645312 | bytes 872415232 | tf_op jit(solution)/shard_map/weight_grads/pallas_call | solution.py:46
  242.0 2.6 turn.12.refs_3_
  246.6 2.7 add_convert_fusion.1
  251.7 2.2 collective-permute-start.25
  253.9 21.0 %attend_back.2 = (bf16[512,1024]{1,0:T(8,128)(2,1)}, f32[8,128]{1,0:T(8,128)}, bf16[1024,2048]{1,0:T(8,128)(2,1)}) custom-call(bf16[512,1024]{1,0:T(8,128)(2,1)} %get-tuple-element.199.refs_4_.refs_1_.refs_0_, bf16[1024,3584]{1,0:T(8,128)(2,1)} %get-tuple-element.153.refs_1_, bf16[1024,1024]{1,0:T(8,128)(2,1)} %get-tuple-element.154.refs_2_.refs_3_, ...), custom_call_target="tpu_custom_call" | custom-call | flops 377957122048 | bytes 1111564288 | tf_op jit(solution)/shard_map/attend_back/pallas_call | solution.py:46
  275.0 2.7 collective-permute-done.24.refs_0_
  277.7 2.7 collective-permute-done.25.refs_1_
  280.3 2.3 fusion.34
  284.6 2.5 fusion.14.refs_16_
  288.1 2.5 fusion.15.refs_15_
  292.3 20.8 %attend_back.3 = (bf16[512,1024]{1,0:T(8,128)(2,1)}, f32[8,128]{1,0:T(8,128)}, bf16[1024,2048]{1,0:T(8,128)(2,1)}) custom-call(bf16[512,1024]{1,0:T(8,128)(2,1)} %get-tuple-element.162.refs_0_.refs_1_, bf16[1024,3584]{1,0:T(8,128)(2,1)} %get-tuple-element.153.refs_1_, ...), custom_call_target="tpu_custom_call", output_to_operand_aliasing={{2}: (14, {})} | custom-call | flops 377957122048 | bytes 1111564288 | tf_op jit(solution)/shard_map/attend_back/pallas_call | solution.py:46
  318.2 2.2 fusion.21.refs_4_.refs_5_
  321.7 2.6 turn.13.refs_1_
  324.3 7.3 %weight_grads.6 = (bf16[512,1536]{1,0:T(8,128)(2,1)}, bf16[512,1536]{1,0:T(8,128)(2,1)}, f32[8,128]{1,0:T(8,128)}) custom-call(bf16[1024,1024]{1,0:T(8,128)(2,1)} %get-tuple-element.169.refs_0_, bf16[1024,1024]{1,0:T(8,128)(2,1)} %turn.13.refs_1_, bf16[1024,2048]{1,0:T(8,128)(2,1)} %get-tuple-element.171.refs_2_, ...), custom_call_target="tpu_custom_call" | custom-call | bytes 1 | tf_op jit(solution)/shard_map/weight_grads/pallas_call | solution.py:46
  331.8 4.9 %collective-permute-done.30.refs_0_ = bf16[64,2304]{1,0:T(8,128)(2,1)S(1)} collective-permute-done((bf16[64,2304]{1,0:T(8,128)(2,1)S(1)}, bf16[64,2304]{1,0:T(8,128)(2,1)S(1)}, u32[]{:S(2)}, u32[]{:S(2)}) %collective-permute-start.30) | collective-permute-done | bytes 294944 | tf_op jit(solution)/shard_map/ppermute | solution.py:458
  337.5 7.7 %weight_grads.7 = (bf16[512,1536]{1,0:T(8,128)(2,1)}, bf16[512,1536]{1,0:T(8,128)(2,1)}, f32[8,128]{1,0:T(8,128)}) custom-call(bf16[1024,1024]{1,0:T(8,128)(2,1)} %get-tuple-element.169.refs_0_, bf16[1024,1024]{1,0:T(8,128)(2,1)} %turn.13.refs_1_, bf16[1024,2048]{1,0:T(8,128)(2,1)} %get-tuple-element.171.refs_2_, ...), custom_call_target="tpu_custom_call" | custom-call | flops 206158430208 | bytes 671088640 | tf_op jit(solution)/shard_map/weight_grads/pallas_call | solution.py:46
  346.8 2.3 collective-permute-done.36.refs_2_
  357.8 20.3 %collective-permute-done.39.refs_2_ = f32[18,128]{1,0:T(8,128)S(1)} collective-permute-done((f32[18,128]{1,0:T(8,128)S(1)}, f32[18,128]{1,0:T(8,128)S(1)}, u32[]{:S(2)}, u32[]{:S(2)}) %collective-permute-start.39) | collective-permute-done | bytes 9248 | tf_op jit(solution)/shard_map/ppermute | solution.py:458
  387.3 5.5 %collective-permute-done.43.refs_3_ = f32[18,128]{1,0:T(8,128)S(1)} collective-permute-done((f32[18,128]{1,0:T(8,128)S(1)}, f32[18,128]{1,0:T(8,128)S(1)}, u32[]{:S(2)}, u32[]{:S(2)}) %collective-permute-start.43) | collective-permute-done | bytes 9248 | tf_op jit(solution)/shard_map/ppermute | solution.py:458
  392.9 2.2 collective-permute-done.40.refs_0_
  409.1 4.6 %fusion.10 = (bf16[512,1024]{1,0:T(8,128)(2,1)}, bf16[512,1024]{1,0:T(8,128)(2,1)}) fusion(f32[512,1024]{1,0:T(8,128)S(1)} %copy-done.20, bf16[512,1024]{1,0:T(8,128)(2,1)S(1)} %copy-done.4, bf16[512,1024]{1,0:T(8,128)(2,1)S(1)} %copy-done.9, bf16[512,1024]{1,0:T(8,128)(2,1)S(1)} %copy-done.12, f32[512]{0:T(512)S(1)} %broadcast_multiply_fusion, ...), kind=kLoop, calls=%fused_computation.19 | loop fusion | flops 12058624 | bytes 11542528 | tf_op jit(solution)/shard_map/convert_element_type | solution.py:759
  415.5 4.0 collective-permute-done.45
  420.6 3.0 collective-permute-done.44
  (409 shorter events, 115.3 us)
Async XLA Ops:
  6.9 18.2 %collective-permute-start.1 = (bf16[64,1536]{1,0:T(8,128)(2,1)S(1)}, bf16[64,1536]{1,0:T(8,128)(2,1)S(1)}, u32[]{:S(2)}, u32[]{:S(2)}) collective-permute-start(bf16[64,1536]{1,0:T(8,128)(2,1)S(1)} %get-tuple-element.243), channel_id=1, source_target_pairs={{0,16},{2,18},{4,20},{6,22},{8,24},{10,26},{12,28},{14,30},{16,0},... | collective-permute-start | bytes 589832 | tf_op jit(solution)/shard_map/ppermute | solution.py:458
  11.0 17.5 %collective-permute-start = (bf16[64,1536]{1,0:T(8,128)(2,1)S(1)}, bf16[64,1536]{1,0:T(8,128)(2,1)S(1)}, u32[]{:S(2)}, u32[]{:S(2)}) collective-permute-start(bf16[64,1536]{1,0:T(8,128)(2,1)S(1)} %get-tuple-element.244), channel_id=1, source_target_pairs={{0,16},{2,18},{4,20},{6,22},{8,24},{10,26},{12,28},{14,30},{16,0},... | collective-permute-start | bytes 589832 | tf_op jit(solution)/shard_map/ppermute | solution.py:458
  13.1 15.4 %collective-permute-start.2 = (bf16[256,1024]{1,0:T(8,128)(2,1)S(1)}, bf16[256,1024]{1,0:T(8,128)(2,1)S(1)}, u32[]{:S(2)}, u32[]{:S(2)}) collective-permute-start(bf16[256,1024]{1,0:T(8,128)(2,1)S(1)} %get-tuple-element.206), channel_id=1, source_target_pairs={{0,1},{1,0},{2,3},{3,2},{4,5},{5,4},{6,7},{7,6},{8,9},{9,8},{10,11... | collective-permute-start | bytes 1572872 | tf_op jit(solution)/shard_map/ppermute | solution.py:458
  32.0 10.4 %collective-permute-start.4 = (bf16[128,1536]{1,0:T(8,128)(2,1)S(1)}, bf16[128,1536]{1,0:T(8,128)(2,1)S(1)}, u32[]{:S(2)}, u32[]{:S(2)}) collective-permute-start(bf16[128,1536]{1,0:T(8,128)(2,1)S(1)} %pad_maximum_fusion.11), channel_id=1, source_target_pairs={{0,4},{2,6},{4,0},{6,2},{8,12},{10,14},{12,8},{14,10},{16,20},{18,... | collective-permute-start | bytes 1179656 | tf_op jit(solution)/shard_map/ppermute | solution.py:458
  33.6 9.7 %collective-permute-start.3 = (bf16[128,1536]{1,0:T(8,128)(2,1)S(1)}, bf16[128,1536]{1,0:T(8,128)(2,1)S(1)}, u32[]{:S(2)}, u32[]{:S(2)}) collective-permute-start(bf16[128,1536]{1,0:T(8,128)(2,1)S(1)} %pad_maximum_fusion.10), channel_id=1, source_target_pairs={{0,8},{2,10},{4,12},{6,14},{8,0},{10,2},{12,4},{14,6},{16,24},{18,... | collective-permute-start | bytes 1179656 | tf_op jit(solution)/shard_map/ppermute | solution.py:458
  34.3 42.1 %collective-permute-start.9 = (bf16[512,1024]{1,0:T(8,128)(2,1)S(1)}, bf16[512,1024]{1,0:T(8,128)(2,1)S(1)}, u32[]{:S(2)}, u32[]{:S(2)}) collective-permute-start(bf16[512,1024]{1,0:T(8,128)(2,1)S(1)} %copy-done.37), channel_id=1, source_target_pairs={{0,1},{1,0},{2,3},{3,2},{4,5},{5,4},{6,7},{7,6},{8,9},{9,8},{10,11... | collective-permute-start | bytes 3145736 | tf_op jit(solution)/shard_map/ppermute | solution.py:458
  46.2 31.0 %collective-permute-start.6 = (bf16[256,1536]{1,0:T(8,128)(2,1)S(1)}, bf16[256,1536]{1,0:T(8,128)(2,1)S(1)}, u32[]{:S(2)}, u32[]{:S(2)}) collective-permute-start(bf16[256,1536]{1,0:T(8,128)(2,1)S(1)} %pad_maximum_fusion.7), channel_id=1, source_target_pairs={{0,8},{2,10},{4,12},{6,14},{8,0},{10,2},{12,4},{14,6},{16,24},{18,... | collective-permute-start | bytes 2359304 | tf_op jit(solution)/shard_map/ppermute | solution.py:458
  48.0 29.2 %collective-permute-start.5 = (bf16[256,1536]{1,0:T(8,128)(2,1)S(1)}, bf16[256,1536]{1,0:T(8,128)(2,1)S(1)}, u32[]{:S(2)}, u32[]{:S(2)}) collective-permute-start(bf16[256,1536]{1,0:T(8,128)(2,1)S(1)} %pad_maximum_fusion.6), channel_id=1, source_target_pairs={{0,4},{2,6},{4,0},{6,2},{8,12},{10,14},{12,8},{14,10},{16,20},{18,... | collective-permute-start | bytes 2359304 | tf_op jit(solution)/shard_map/ppermute | solution.py:458
  49.0 43.4 %copy-start.31 = (bf16[64,2304]{1,0:T(8,128)(2,1)}, bf16[64,2304]{1,0:T(8,128)(2,1)S(1)}, u32[]{:S(2)}) copy-start(bf16[64,2304]{1,0:T(8,128)(2,1)S(1)} %get-tuple-element.225) | copy-start | bytes 884740
  49.0 23.2 %collective-permute-start.8 = (bf16[64,2304]{1,0:T(8,128)(2,1)S(1)}, bf16[64,2304]{1,0:T(8,128)(2,1)S(1)}, u32[]{:S(2)}, u32[]{:S(2)}) collective-permute-start(bf16[64,2304]{1,0:T(8,128)(2,1)S(1)} %get-tuple-element.225), channel_id=1, source_target_pairs={{0,16},{2,18},{4,20},{6,22},{8,24},{10,26},{12,28},{14,30},{16,0},... | collective-permute-start | bytes 884744 | tf_op jit(solution)/shard_map/ppermute | solution.py:458
  52.5 23.9 %collective-permute-start.7 = (bf16[64,2304]{1,0:T(8,128)(2,1)S(1)}, bf16[64,2304]{1,0:T(8,128)(2,1)S(1)}, u32[]{:S(2)}, u32[]{:S(2)}) collective-permute-start(bf16[64,2304]{1,0:T(8,128)(2,1)S(1)} %get-tuple-element.226), channel_id=1, source_target_pairs={{0,16},{2,18},{4,20},{6,22},{8,24},{10,26},{12,28},{14,30},{16,0},... | collective-permute-start | bytes 884744 | tf_op jit(solution)/shard_map/ppermute | solution.py:458
  80.6 9.5 %collective-permute-start.13 = (bf16[512,1536]{1,0:T(8,128)(2,1)S(1)}, bf16[512,1536]{1,0:T(8,128)(2,1)S(1)}, u32[]{:S(2)}, u32[]{:S(2)}) collective-permute-start(bf16[512,1536]{1,0:T(8,128)(2,1)S(1)} %pad_maximum_fusion.3.refs_9_.refs_12_), channel_id=1, source_target_pairs={{0,2},{2,0},{4,6},{6,4},{8,10},{10,8},{12,14},{14,12},{16,18},{18,... | collective-permute-start | bytes 4718600 | tf_op jit(solution)/shard_map/ppermute | solution.py:458
  80.6 9.4 %collective-permute-start.12 = (bf16[512,1536]{1,0:T(8,128)(2,1)S(1)}, bf16[512,1536]{1,0:T(8,128)(2,1)S(1)}, u32[]{:S(2)}, u32[]{:S(2)}) collective-permute-start(bf16[512,1536]{1,0:T(8,128)(2,1)S(1)} %pad_maximum_fusion.2.refs_6_.refs_9_), channel_id=1, source_target_pairs={{0,2},{2,0},{4,6},{6,4},{8,10},{10,8},{12,14},{14,12},{16,18},{18,... | collective-permute-start | bytes 4718600 | tf_op jit(solution)/shard_map/ppermute | solution.py:458
  81.1 27.9 %collective-permute-start.14 = (bf16[256,1024]{1,0:T(8,128)(2,1)}, bf16[256,1024]{1,0:T(8,128)(2,1)}, u32[]{:S(2)}, u32[]{:S(2)}) collective-permute-start(bf16[256,1024]{1,0:T(8,128)(2,1)} %get-tuple-element.205), channel_id=1, source_target_pairs={{0,1},{1,0},{2,3},{3,2},{4,5},{5,4},{6,7},{7,6},{8,9},{9,8},{10,11... | collective-permute-start | bytes 1572872 | tf_op jit(solution)/shard_map/ppermute | solution.py:458
  84.0 25.0 %collective-permute-start.11 = (bf16[128,2304]{1,0:T(8,128)(2,1)}, bf16[128,2304]{1,0:T(8,128)(2,1)}, u32[]{:S(2)}, u32[]{:S(2)}) collective-permute-start(bf16[128,2304]{1,0:T(8,128)(2,1)} %pad_maximum_fusion.9.refs_12_), channel_id=1, source_target_pairs={{0,4},{2,6},{4,0},{6,2},{8,12},{10,14},{12,8},{14,10},{16,20},{18,... | collective-permute-start | bytes 1769480 | tf_op jit(solution)/shard_map/ppermute | solution.py:458
  86.2 22.8 %collective-permute-start.10 = (bf16[128,2304]{1,0:T(8,128)(2,1)}, bf16[128,2304]{1,0:T(8,128)(2,1)}, u32[]{:S(2)}, u32[]{:S(2)}) collective-permute-start(bf16[128,2304]{1,0:T(8,128)(2,1)} %pad_maximum_fusion.8.refs_11_), channel_id=1, source_target_pairs={{0,8},{2,10},{4,12},{6,14},{8,0},{10,2},{12,4},{14,6},{16,24},{18,... | collective-permute-start | bytes 1769480 | tf_op jit(solution)/shard_map/ppermute | solution.py:458
  109.1 24.7 %collective-permute-start.17 = (bf16[512,1024]{1,0:T(8,128)(2,1)}, bf16[512,1024]{1,0:T(8,128)(2,1)}, u32[]{:S(2)}, u32[]{:S(2)}) collective-permute-start(bf16[512,1024]{1,0:T(8,128)(2,1)} %get-tuple-element.124), channel_id=1, source_target_pairs={{0,1},{1,0},{2,3},{3,2},{4,5},{5,4},{6,7},{7,6},{8,9},{9,8},{10,11... | collective-permute-start | bytes 3145736 | tf_op jit(solution)/shard_map/ppermute | solution.py:458
  114.4 27.4 %collective-permute-start.16 = (bf16[256,2304]{1,0:T(8,128)(2,1)}, bf16[256,2304]{1,0:T(8,128)(2,1)}, u32[]{:S(2)}, u32[]{:S(2)}) collective-permute-start(bf16[256,2304]{1,0:T(8,128)(2,1)} %pad_maximum_fusion.5.refs_14_), channel_id=1, source_target_pairs={{0,8},{2,10},{4,12},{6,14},{8,0},{10,2},{12,4},{14,6},{16,24},{18,... | collective-permute-start | bytes 3538952 | tf_op jit(solution)/shard_map/ppermute | solution.py:458
  114.4 27.6 %collective-permute-start.15 = (bf16[256,2304]{1,0:T(8,128)(2,1)}, bf16[256,2304]{1,0:T(8,128)(2,1)}, u32[]{:S(2)}, u32[]{:S(2)}) collective-permute-start(bf16[256,2304]{1,0:T(8,128)(2,1)} %pad_maximum_fusion.4.refs_13_), channel_id=1, source_target_pairs={{0,4},{2,6},{4,0},{6,2},{8,12},{10,14},{12,8},{14,10},{16,20},{18,... | collective-permute-start | bytes 3538952 | tf_op jit(solution)/shard_map/ppermute | solution.py:458
  147.2 9.3 %collective-permute-start.19 = (bf16[512,2304]{1,0:T(8,128)(2,1)S(1)}, bf16[512,2304]{1,0:T(8,128)(2,1)S(1)}, u32[]{:S(2)}, u32[]{:S(2)}) collective-permute-start(bf16[512,2304]{1,0:T(8,128)(2,1)S(1)} %pad_maximum_fusion.1.refs_7_), channel_id=1, source_target_pairs={{0,2},{2,0},{4,6},{6,4},{8,10},{10,8},{12,14},{14,12},{16,18},{18,... | collective-permute-start | bytes 7077896 | tf_op jit(solution)/shard_map/ppermute | solution.py:458
  147.3 9.2 %collective-permute-start.18 = (bf16[512,2304]{1,0:T(8,128)(2,1)S(1)}, bf16[512,2304]{1,0:T(8,128)(2,1)}, u32[]{:S(2)}, u32[]{:S(2)}) collective-permute-start(bf16[512,2304]{1,0:T(8,128)(2,1)S(1)} %pad_maximum_fusion.refs_4_), channel_id=1, source_target_pairs={{0,2},{2,0},{4,6},{6,4},{8,10},{10,8},{12,14},{14,12},{16,18},{18,... | collective-permute-start | bytes 7077896 | tf_op jit(solution)/shard_map/ppermute | solution.py:458
  155.3 25.5 %collective-permute-start.20 = (bf16[512,1024]{1,0:T(8,128)(2,1)}, bf16[512,1024]{1,0:T(8,128)(2,1)}, u32[]{:S(2)}, u32[]{:S(2)}) collective-permute-start(bf16[512,1024]{1,0:T(8,128)(2,1)} %multiply_convert_fusion.refs_0_.refs_9_.refs_1_), channel_id=1, source_target_pairs={{0,1},{1,0},{2,3},{3,2},{4,5},{5,4},{6,7},{7,6},{8,9},{9,8},{10,11... | collective-permute-start | bytes 3145736 | tf_op jit(solution)/shard_map/ppermute | solution.py:458
  198.7 24.9 %collective-permute-start.22 = (bf16[512,1024]{1,0:T(8,128)(2,1)}, bf16[512,1024]{1,0:T(8,128)(2,1)S(1)}, u32[]{:S(2)}, u32[]{:S(2)}) collective-permute-start(bf16[512,1024]{1,0:T(8,128)(2,1)} %get-tuple-element.140.refs_3_.refs_4_), channel_id=1, source_target_pairs={{0,1},{1,0},{2,3},{3,2},{4,5},{5,4},{6,7},{7,6},{8,9},{9,8},{10,11... | collective-permute-start | bytes 3145736 | tf_op jit(solution)/shard_map/ppermute | solution.py:458
  212.5 32.1 %collective-permute-start.21 = (bf16[512,2304]{1,0:T(8,128)(2,1)}, bf16[512,2304]{1,0:T(8,128)(2,1)}, u32[]{:S(2)}, u32[]{:S(2)}) collective-permute-start(bf16[512,2304]{1,0:T(8,128)(2,1)} %get-tuple-element.145), channel_id=1, source_target_pairs={{0,2},{2,0},{4,6},{6,4},{8,10},{10,8},{12,14},{14,12},{16,18},{18,... | collective-permute-start | bytes 7077896 | tf_op jit(solution)/shard_map/ppermute | solution.py:458
  240.5 4.7 %collective-permute-start.23 = (bf16[512,2304]{1,0:T(8,128)(2,1)}, bf16[512,2304]{1,0:T(8,128)(2,1)S(1)}, u32[]{:S(2)}, u32[]{:S(2)}) collective-permute-start(bf16[512,2304]{1,0:T(8,128)(2,1)} %get-tuple-element.148), channel_id=1, source_target_pairs={{0,2},{2,0},{4,6},{6,4},{8,10},{10,8},{12,14},{14,12},{16,18},{18,... | collective-permute-start | bytes 7077896 | tf_op jit(solution)/shard_map/ppermute | solution.py:458
  241.1 33.9 %collective-permute-start.26 = (bf16[512,1024]{1,0:T(8,128)(2,1)}, bf16[512,1024]{1,0:T(8,128)(2,1)}, u32[]{:S(2)}, u32[]{:S(2)}) collective-permute-start(bf16[512,1024]{1,0:T(8,128)(2,1)} %get-tuple-element.199.refs_4_.refs_1_.refs_0_), channel_id=1, source_target_pairs={{0,1},{1,0},{2,3},{3,2},{4,5},{5,4},{6,7},{7,6},{8,9},{9,8},{10,11... | collective-permute-start | bytes 3145736 | tf_op jit(solution)/shard_map/ppermute | solution.py:458
  249.3 28.3 %collective-permute-start.24 = (bf16[2,2,64,2304]{3,2,1,0:T(8,128)(2,1)}, bf16[2,2,64,2304]{3,2,1,0:T(8,128)(2,1)}, u32[]{:S(2)}, u32[]{:S(2)}) collective-permute-start(bf16[2,2,64,2304]{3,2,1,0:T(8,128)(2,1)} %bitcast.8.refs_16_), channel_id=1, source_target_pairs={{0,4},{2,6},{4,0},{6,2},{8,12},{10,14},{12,8},{14,10},{16,20},{18,... | collective-permute-start | bytes 3538952 | tf_op jit(solution)/shard_map/ppermute | solution.py:458
  251.7 28.6 %collective-permute-start.25 = (bf16[2,2,64,2304]{3,2,1,0:T(8,128)(2,1)}, bf16[2,2,64,2304]{3,2,1,0:T(8,128)(2,1)}, u32[]{:S(2)}, u32[]{:S(2)}) collective-permute-start(bf16[2,2,64,2304]{3,2,1,0:T(8,128)(2,1)} %fusion.13.refs_17_), channel_id=1, source_target_pairs={{0,8},{2,10},{4,12},{6,14},{8,0},{10,2},{12,4},{14,6},{16,24},{18,... | collective-permute-start | bytes 3538952 | tf_op jit(solution)/shard_map/ppermute | solution.py:458
  282.6 49.2 %collective-permute-start.32 = (bf16[256,1024]{1,0:T(8,128)(2,1)}, bf16[256,1024]{1,0:T(8,128)(2,1)}, u32[]{:S(2)}, u32[]{:S(2)}) collective-permute-start(bf16[256,1024]{1,0:T(8,128)(2,1)} %get-tuple-element.203), channel_id=1, source_target_pairs={{0,1},{1,0},{2,3},{3,2},{4,5},{5,4},{6,7},{7,6},{8,9},{9,8},{10,11... | collective-permute-start | bytes 1572872 | tf_op jit(solution)/shard_map/ppermute | solution.py:458
  284.0 30.4 %collective-permute-start.29 = (bf16[256,1024]{1,0:T(8,128)(2,1)}, bf16[256,1024]{1,0:T(8,128)(2,1)}, u32[]{:S(2)}, u32[]{:S(2)}) collective-permute-start(bf16[256,1024]{1,0:T(8,128)(2,1)} %get-tuple-element.204), channel_id=1, source_target_pairs={{0,1},{1,0},{2,3},{3,2},{4,5},{5,4},{6,7},{7,6},{8,9},{9,8},{10,11... | collective-permute-start | bytes 1572872 | tf_op jit(solution)/shard_map/ppermute | solution.py:458
  287.1 27.3 %collective-permute-start.28 = (bf16[2,64,2304]{2,1,0:T(8,128)(2,1)}, bf16[2,64,2304]{2,1,0:T(8,128)(2,1)}, u32[]{:S(2)}, u32[]{:S(2)}) collective-permute-start(bf16[2,64,2304]{2,1,0:T(8,128)(2,1)} %fusion.14.refs_16_), channel_id=1, source_target_pairs={{0,4},{2,6},{4,0},{6,2},{8,12},{10,14},{12,8},{14,10},{16,20},{18,... | collective-permute-start | bytes 1769480 | tf_op jit(solution)/shard_map/ppermute | solution.py:458
  290.6 23.8 %collective-permute-start.27 = (bf16[2,64,2304]{2,1,0:T(8,128)(2,1)}, bf16[2,64,2304]{2,1,0:T(8,128)(2,1)}, u32[]{:S(2)}, u32[]{:S(2)}) collective-permute-start(bf16[2,64,2304]{2,1,0:T(8,128)(2,1)} %fusion.15.refs_15_), channel_id=1, source_target_pairs={{0,8},{2,10},{4,12},{6,14},{8,0},{10,2},{12,4},{14,6},{16,24},{18,... | collective-permute-start | bytes 1769480 | tf_op jit(solution)/shard_map/ppermute | solution.py:458
  316.8 15.1 %collective-permute-start.31 = (f32[18,128]{1,0:T(8,128)S(1)}, f32[18,128]{1,0:T(8,128)S(1)}, u32[]{:S(2)}, u32[]{:S(2)}) collective-permute-start(f32[18,128]{1,0:T(8,128)S(1)} %maximum_bitcast_fusion.1.refs_6_), channel_id=1, source_target_pairs={{0,2},{2,0},{4,6},{6,4},{8,10},{10,8},{12,14},{14,12},{16,18},{18,... | collective-permute-start | bytes 27656 | tf_op jit(solution)/shard_map/ppermute | solution.py:458
  320.4 16.3 %collective-permute-start.30 = (bf16[64,2304]{1,0:T(8,128)(2,1)S(1)}, bf16[64,2304]{1,0:T(8,128)(2,1)S(1)}, u32[]{:S(2)}, u32[]{:S(2)}) collective-permute-start(bf16[64,2304]{1,0:T(8,128)(2,1)S(1)} %fusion.22.refs_3_.refs_4_), channel_id=1, source_target_pairs={{0,16},{2,18},{4,20},{6,22},{8,24},{10,26},{12,28},{14,30},{16,0},... | collective-permute-start | bytes 884744 | tf_op jit(solution)/shard_map/ppermute | solution.py:458
  331.6 17.5 %collective-permute-start.34 = (bf16[512,1536]{1,0:T(8,128)(2,1)}, bf16[512,1536]{1,0:T(8,128)(2,1)}, u32[]{:S(2)}, u32[]{:S(2)}) collective-permute-start(bf16[512,1536]{1,0:T(8,128)(2,1)} %get-tuple-element.182), channel_id=1, source_target_pairs={{0,2},{2,0},{4,6},{6,4},{8,10},{10,8},{12,14},{14,12},{16,18},{18,... | collective-permute-start | bytes 4718600 | tf_op jit(solution)/shard_map/ppermute | solution.py:458
  345.2 3.9 collective-permute-start.35
  345.3 3.8 collective-permute-start.36
  346.4 41.0 %collective-permute-start.42 = (bf16[64,2304]{1,0:T(8,128)(2,1)S(1)}, bf16[64,2304]{1,0:T(8,128)(2,1)}, u32[]{:S(2)}, u32[]{:S(2)}) collective-permute-start(bf16[64,2304]{1,0:T(8,128)(2,1)S(1)} %copy-done.75), channel_id=1, source_target_pairs={{0,16},{2,18},{4,20},{6,22},{8,24},{10,26},{12,28},{14,30},{16,0},... | collective-permute-start | bytes 884744 | tf_op jit(solution)/shard_map/ppermute | solution.py:458
  346.4 52.5 %collective-permute-start.33 = (bf16[512,1024]{1,0:T(8,128)(2,1)S(1)}, bf16[512,1024]{1,0:T(8,128)(2,1)S(1)}, u32[]{:S(2)}, u32[]{:S(2)}) collective-permute-start(bf16[512,1024]{1,0:T(8,128)(2,1)S(1)} %copy-done.38), channel_id=1, source_target_pairs={{0,1},{1,0},{2,3},{3,2},{4,5},{5,4},{6,7},{7,6},{8,9},{9,8},{10,11... | collective-permute-start | bytes 3145736 | tf_op jit(solution)/shard_map/ppermute | solution.py:458
  352.3 25.8 %collective-permute-start.37 = (bf16[2,2,64,1536]{3,2,1,0:T(8,128)(2,1)S(1)}, bf16[2,2,64,1536]{3,2,1,0:T(8,128)(2,1)S(1)}, u32[]{:S(2)}, u32[]{:S(2)}) collective-permute-start(bf16[2,2,64,1536]{3,2,1,0:T(8,128)(2,1)S(1)} %bitcast.175), channel_id=1, source_target_pairs={{0,4},{2,6},{4,0},{6,2},{8,12},{10,14},{12,8},{14,10},{16,20},{18,... | collective-permute-start | bytes 2359304 | tf_op jit(solution)/shard_map/ppermute | solution.py:458
  353.6 24.6 %collective-permute-start.38 = (bf16[2,2,64,1536]{3,2,1,0:T(8,128)(2,1)S(1)}, bf16[2,2,64,1536]{3,2,1,0:T(8,128)(2,1)S(1)}, u32[]{:S(2)}, u32[]{:S(2)}) collective-permute-start(bf16[2,2,64,1536]{3,2,1,0:T(8,128)(2,1)S(1)} %fusion.16), channel_id=1, source_target_pairs={{0,8},{2,10},{4,12},{6,14},{8,0},{10,2},{12,4},{14,6},{16,24},{18,... | collective-permute-start | bytes 2359304 | tf_op jit(solution)/shard_map/ppermute | solution.py:458
  355.1 23.0 %collective-permute-start.39 = (f32[18,128]{1,0:T(8,128)S(1)}, f32[18,128]{1,0:T(8,128)S(1)}, u32[]{:S(2)}, u32[]{:S(2)}) collective-permute-start(f32[18,128]{1,0:T(8,128)S(1)} %fusion.41), channel_id=1, source_target_pairs={{0,8},{2,10},{4,12},{6,14},{8,0},{10,2},{12,4},{14,6},{16,24},{18,... | collective-permute-start | bytes 27656 | tf_op jit(solution)/shard_map/ppermute | solution.py:458
  381.2 11.7 %collective-permute-start.41 = (bf16[2,64,1536]{2,1,0:T(8,128)(2,1)S(1)}, bf16[2,64,1536]{2,1,0:T(8,128)(2,1)S(1)}, u32[]{:S(2)}, u32[]{:S(2)}) collective-permute-start(bf16[2,64,1536]{2,1,0:T(8,128)(2,1)S(1)} %fusion.17.refs_2_), channel_id=1, source_target_pairs={{0,4},{2,6},{4,0},{6,2},{8,12},{10,14},{12,8},{14,10},{16,20},{18,... | collective-permute-start | bytes 1179656 | tf_op jit(solution)/shard_map/ppermute | solution.py:458
  384.0 11.1 %collective-permute-start.40 = (bf16[2,64,1536]{2,1,0:T(8,128)(2,1)S(1)}, bf16[2,64,1536]{2,1,0:T(8,128)(2,1)S(1)}, u32[]{:S(2)}, u32[]{:S(2)}) collective-permute-start(bf16[2,64,1536]{2,1,0:T(8,128)(2,1)S(1)} %fusion.18.refs_1_), channel_id=1, source_target_pairs={{0,8},{2,10},{4,12},{6,14},{8,0},{10,2},{12,4},{14,6},{16,24},{18,... | collective-permute-start | bytes 1179656 | tf_op jit(solution)/shard_map/ppermute | solution.py:458
  384.7 8.1 %collective-permute-start.43 = (f32[18,128]{1,0:T(8,128)S(1)}, f32[18,128]{1,0:T(8,128)S(1)}, u32[]{:S(2)}, u32[]{:S(2)}) collective-permute-start(f32[18,128]{1,0:T(8,128)S(1)} %add.308), channel_id=1, source_target_pairs={{0,16},{2,18},{4,20},{6,22},{8,24},{10,26},{12,28},{14,30},{16,0},... | collective-permute-start | bytes 27656 | tf_op jit(solution)/shard_map/ppermute | solution.py:458
  402.0 12.4 %collective-permute-start.46 = (f32[18,128]{1,0:T(8,128)S(1)}, f32[18,128]{1,0:T(8,128)S(1)}, u32[]{:S(2)}, u32[]{:S(2)}) collective-permute-start(f32[18,128]{1,0:T(8,128)S(1)} %copy-done.100), channel_id=1, source_target_pairs={{0,1},{1,0},{2,3},{3,2},{4,5},{5,4},{6,7},{7,6},{8,9},{9,8},{10,11... | collective-permute-start | bytes 27656 | tf_op jit(solution)/shard_map/ppermute | solution.py:458
  404.8 14.7 %collective-permute-start.45 = (bf16[64,1536]{1,0:T(8,128)(2,1)S(1)}, bf16[64,1536]{1,0:T(8,128)(2,1)S(1)}, u32[]{:S(2)}, u32[]{:S(2)}) collective-permute-start(bf16[64,1536]{1,0:T(8,128)(2,1)S(1)} %fusion.23), channel_id=1, source_target_pairs={{0,16},{2,18},{4,20},{6,22},{8,24},{10,26},{12,28},{14,30},{16,0},... | collective-permute-start | bytes 589832 | tf_op jit(solution)/shard_map/ppermute | solution.py:458
  406.7 16.9 %collective-permute-start.44 = (bf16[64,1536]{1,0:T(8,128)(2,1)S(1)}, bf16[64,1536]{1,0:T(8,128)(2,1)S(1)}, u32[]{:S(2)}, u32[]{:S(2)}) collective-permute-start(bf16[64,1536]{1,0:T(8,128)(2,1)S(1)} %fusion.25), channel_id=1, source_target_pairs={{0,16},{2,18},{4,20},{6,22},{8,24},{10,26},{12,28},{14,30},{16,0},... | collective-permute-start | bytes 589832 | tf_op jit(solution)/shard_map/ppermute | solution.py:458
  (113 other events, 774.7 us)
